TPU v7x, 1024 devices: a whole 8x8x8 slice. The times are simulated.
1024 devices in a mesh: ep: 32 (over z_hi, y), edp: 32 (over z_lo, x, core).
Axes of the slice: x: 8, y: 8, z: 8 (z_hi: 4, z_lo: 2; z = z_hi * 2 + z_lo), core: 2. Of those that a mesh axis runs over, the one named last changes fastest.
Arguments:
- routes: int32 [49152, 8], P(('ep', 'edp')), may hold values from 0 to 31, all different within a row; in each aligned block of 48 rows (0 to 47, 48 to 95, ...) at most 16 rows name the same one
- gate_pre: bfloat16 [32, 32, 32, 16, 768], P('ep', 'edp'), may hold values from -8 to 8
- up_pre: bfloat16 [32, 32, 32, 16, 768], P('ep', 'edp'), may hold values from -6 to 6
- hidden_grad: bfloat16 [32, 32, 32, 16, 768], P('ep', 'edp'), may hold values from -6 to 6
- w_gate: bfloat16 [32, 2048, 768], P('ep'), may hold values from -0.15625 to 0.15625
- w_up: bfloat16 [32, 2048, 768], P('ep'), may hold values from -0.15625 to 0.15625
- bucket_terms: float32 [32, 32, 128, 1536], P('ep', 'edp'), may hold values from -6 to 6
Outputs:
- token_grad: bfloat16 [49152, 2048], P(('ep', 'edp'))
- reduced: float32 [32, 128, 1536], P('ep', 'edp')
Inputs may be any that keep to these rules, and one draw needn't show every extreme that they name: `routes`: each row names 8 different experts; the 48 rows of one device name no expert more than 16 times, a bound that some block reaches.
All inputs are finite; a program needn't handle non-finite values.
Results may differ from a plain program's by a relative error of at most 0.0057.
Values may be sent and summed in bfloat16 or wider, within the bound.
No kernel may reach another device: no remote copies, remote signals or barrier semaphores. Data moves between devices by JAX's collectives and lax.ppermute only.
A program may use at most 32 MiB of HBM per device.

v0:
```python
import jax
import jax.numpy as jnp
from jax import lax
from jax.sharding import PartitionSpec as P


def reduce_bucket(bucket_terms):
    summed = lax.psum_scatter(bucket_terms[0, 0], "edp", scatter_dimension=0, tiled=True)
    return summed[None]


def shards(routes, gate_pre, up_pre, hidden_grad, w_gate, w_up, bucket_terms):
    experts = lax.axis_size("ep")
    capacity = gate_pre.shape[3]
    width = w_gate.shape[1]
    gate_f = gate_pre[0, 0].astype(jnp.float32)
    up_f = up_pre[0, 0].astype(jnp.float32)
    grad_f = hidden_grad[0, 0].astype(jnp.float32)
    sigmoid_gate = 1.0 / (1.0 + jnp.exp(-gate_f))
    grad_gate = (grad_f * up_f * sigmoid_gate * (1.0 + gate_f * (1.0 - sigmoid_gate))).astype(
        jnp.bfloat16
    )
    grad_up = (grad_f * gate_f * sigmoid_gate).astype(jnp.bfloat16)
    dims = (((2,), (1,)), ((), ()))
    first = lax.dot_general(grad_gate, w_gate[0], dims, preferred_element_type=jnp.float32)
    second = lax.dot_general(grad_up, w_up[0], dims, preferred_element_type=jnp.float32)
    slot_grad = (first + second).astype(jnp.bfloat16)
    returned = lax.all_to_all(slot_grad, "ep", split_axis=0, concat_axis=0, tiled=True)
    flat_rows = returned.reshape(experts * capacity, width)
    matches = (
        (routes[:, :, None] == jnp.arange(experts, dtype=jnp.int32)[None, None, :])
        .astype(jnp.int32)
        .sum(axis=1)
    )
    earlier = jnp.cumsum(matches, axis=0) - matches
    position = jnp.take_along_axis(earlier, routes, axis=1)
    row_index = routes * capacity + position
    token_sum = flat_rows[row_index].astype(jnp.float32).sum(axis=1)
    token_grad = token_sum.astype(jnp.bfloat16)
    reduced = reduce_bucket(bucket_terms)
    return (token_grad, reduced)


def solution(mesh):
    placed = (
        P(("ep", "edp"), None),
        P("ep", "edp", None, None, None),
        P("ep", "edp", None, None, None),
        P("ep", "edp", None, None, None),
        P("ep", None, None),
        P("ep", None, None),
        P("ep", "edp", None, None),
    )
    return jax.shard_map(
        shards,
        mesh=mesh,
        in_specs=placed,
        out_specs=(P(("ep", "edp"), None), P("ep", "edp", None)),
        check_vma=False,
    )
```

profile of v0, /device:TPU:1, one launch (start us, length us, event | category | flops | bytes accessed | tf_op | source)
XLA Modules:
  0.0 307.9 jit_solution(4513688528030878695)
XLA Ops:
  7.2 0.0 copy-start
  7.2 0.0 copy-start.3
  7.2 0.0 copy-start.4
  7.2 0.0 copy-start.2
  7.2 0.0 copy-start.5
  7.2 1.8 copy-done
  9.1 3.9 %fusion = f32[32,16,2048]{2,1,0:T(8,128)S(1)} fusion(bf16[1,2048,768]{2,1,0:T(8,128)(2,1)S(1)} %copy-done, bf16[1,1,32,16,768]{4,3,2,1,0:T(8,128)(2,1)} %param.8, bf16[1,1,32,16,768]{4,3,2,1,0:T(8,128)(2,1)} %param.10), kind=kOutput, calls=%fused_computation.3 | convolution fusion | flops 1613758464 | bytes 8912896 | tf_op jit(solution)/shard_map/dot_general | solution.py:26
  13.0 0.0 copy-done.3
  13.0 0.0 copy-done.4
  13.0 0.0 copy-done.2
  13.0 0.0 copy-done.5
  13.0 3.5 %add_convert_fusion = bf16[32,16,2048]{2,1,0:T(8,128)(2,1)} fusion(f32[32,16,2048]{2,1,0:T(8,128)S(1)} %fusion, bf16[1,2048,768]{2,1,0:T(8,128)(2,1)S(1)} %copy-done.2, bf16[1,1,32,16,768]{4,3,2,1,0:T(8,128)(2,1)S(1)} %copy-done.4, bf16[1,1,32,16,768]{4,3,2,1,0:T(8,128)(2,1)S(1)} %copy-done.3, bf16[1,1,32,16,768]{4,3,2,1,0:T(8,128)(2,1)S(1)} %copy-done.5), kind=kOutput, calls=%fused_computation.2 | convolution fusion | flops 1617821696 | bytes 11796480 | tf_op jit(solution)/shard_map/dot_general | solution.py:25
  16.5 0.0 copy-start.1
  16.5 22.7 %all-to-all-start = ((bf16[32,16,2048]{2,1,0:T(8,128)(2,1)}), bf16[32,16,2048]{2,1,0:T(8,128)(2,1)}, u32[]{:S(2)}, u32[]{:S(2)}) async-start(bf16[32,16,2048]{2,1,0:T(8,128)(2,1)} %add_convert_fusion), calls=%async_computation | async-start | bytes 4194304 | tf_op jit(solution)/shard_map/all_to_all | solution.py:28
  39.2 0.0 all-reduce.3.cloned.1.call-start
  39.3 0.7 all-reduce.3.cloned.1.call-update
  40.0 0.0 copy-done.1
  40.0 0.1 copy.35
  40.1 0.1 reduce_window_sum.11
  40.2 0.1 copy.37
  40.3 0.1 reshape.29
  40.4 2.9 gather_fusion.1
  43.2 0.1 reshape.32
  43.3 0.1 copy.38
  43.4 0.1 copy.39
  43.5 0.1 reshape.23
  43.6 1.3 dynamic-slice
  45.5 244.0 %all-reduce.3.cloned.1.call-done = f32[128,1536]{1,0:T(8,128)} async-done(((f32[128,1536]{1,0:T(8,128)}), f32[128,1536]{1,0:T(8,128)}) %all-reduce.3.cloned.1.call-update) | async-done | bytes 786448
  289.6 1.4 dynamic-slice_bitcast_fusion
  291.0 0.0 all-to-all-done
  291.0 6.9 %gather_fusion = bf16[384,2048]{1,0:T(8,128)(2,1)} fusion(bf16[512,2048]{1,0:T(8,128)(2,1)} %bitcast.6, s32[1024]{0:T(1024)S(1)} %pad_clamp_fusion), kind=kCustom, calls=%fused_computation | custom fusion | bytes 3147264 | tf_op jit(solution)/shard_map/gather | solution.py:38
  297.9 3.2 %bitcast_reduce_fusion = bf16[48,2048]{1,0:T(8,128)(2,1)} fusion(bf16[384,2048]{1,0:T(8,128)(2,1)} %gather_fusion), kind=kLoop, calls=%fused_computation.20 | loop fusion | flops 688128 | bytes 1769472 | tf_op jit(solution)/shard_map/reduce_sum | solution.py:38
  (5 shorter events, 0.1 us)
Async XLA Ops:
  7.2 1.9 copy-start
  7.2 5.8 %copy-start.3 = (bf16[1,1,32,16,768]{4,3,2,1,0:T(8,128)(2,1)S(1)}, bf16[1,1,32,16,768]{4,3,2,1,0:T(8,128)(2,1)}, u32[]{:S(2)}) copy-start(bf16[1,1,32,16,768]{4,3,2,1,0:T(8,128)(2,1)} %param.8) | copy-start | bytes 2359300
  7.2 5.8 %copy-start.4 = (bf16[1,1,32,16,768]{4,3,2,1,0:T(8,128)(2,1)S(1)}, bf16[1,1,32,16,768]{4,3,2,1,0:T(8,128)(2,1)}, u32[]{:S(2)}) copy-start(bf16[1,1,32,16,768]{4,3,2,1,0:T(8,128)(2,1)} %param.10) | copy-start | bytes 2359300
  7.2 5.8 %copy-start.2 = (bf16[1,2048,768]{2,1,0:T(8,128)(2,1)S(1)}, bf16[1,2048,768]{2,1,0:T(8,128)(2,1)}, u32[]{:S(2)}) copy-start(bf16[1,2048,768]{2,1,0:T(8,128)(2,1)} %param.11) | copy-start | bytes 9437188
  7.2 5.8 %copy-start.5 = (bf16[1,1,32,16,768]{4,3,2,1,0:T(8,128)(2,1)S(1)}, bf16[1,1,32,16,768]{4,3,2,1,0:T(8,128)(2,1)}, u32[]{:S(2)}) copy-start(bf16[1,1,32,16,768]{4,3,2,1,0:T(8,128)(2,1)} %param.9) | copy-start | bytes 2359300
  16.5 23.4 %copy-start.1 = (s32[48,8]{0,1:T(8,128)S(1)}, s32[48,8]{0,1:T(8,128)}, u32[]{:S(2)}) copy-start(s32[48,8]{0,1:T(8,128)} %param.7) | copy-start | bytes 4612
  16.5 274.4 %all-to-all-start = ((bf16[32,16,2048]{2,1,0:T(8,128)(2,1)}), bf16[32,16,2048]{2,1,0:T(8,128)(2,1)}, u32[]{:S(2)}, u32[]{:S(2)}) async-start(bf16[32,16,2048]{2,1,0:T(8,128)(2,1)} %add_convert_fusion), calls=%async_computation | async-start | bytes 4194304 | tf_op jit(solution)/shard_map/all_to_all | solution.py:28
  39.2 250.3 %all-reduce.3.cloned.1.call-start = ((), (), s32[]{:S(2)}) async-start(), calls=%async_computation.1 | async-start | bytes 1572864
Sparse Core Ops, SparseCore 0:
  43.5 245.9 all-reduce.2
where the time goes:
time: 308 us
  waiting for transfers between devices  245 us (80%)
  starting transfers between devices  22.7 us (7%)
  local copies, waits for them, and re-layouts  14.9 us (5%)
  between operations  14.8 us (5%)
  matrix products  7.42 us (2%)
  other arithmetic  3.29 us (1%)
    unnamed x2, waiting for transfers between devices  245 us
    all_to_all x1, starting transfers between devices, shards(): lax.all_to_all(slot_grad, 'ep', split_axis=0, concat_axis=0, tiled=True)  22.7 us
    gather x1, local copies, waits for them, and re-layouts, shards(): token_sum = flat_rows[row_index].astype(jnp.float32).sum(axis=1)  6.91 us
  transfers between devices with their start and end apart: 2, of which 1 were waited for; matrix products, arithmetic and copies ran while one was open for 2% of the time, Pallas kernels for 0%

commit v1 on v0

v1 whole, which is shorter than its diff:
```python
import jax
import jax.numpy as jnp
from jax import lax
from jax.sharding import PartitionSpec as P


def reduce_bucket(bucket):
    rows, width = bucket.shape
    members = lax.axis_size("edp")
    own = lax.axis_index("edp")
    part = bucket.reshape(members, rows * width // (members * 128), 128)
    stride = 1
    while stride < members:
        pairs = part.reshape(part.shape[0] // 2, 2, *part.shape[1:])
        bit = (own // stride) % 2
        kept = lax.dynamic_index_in_dim(pairs, bit, axis=1, keepdims=False)
        given = lax.dynamic_index_in_dim(pairs, 1 - bit, axis=1, keepdims=False)
        swap = [(i, i ^ stride) for i in range(members)]
        part = kept + lax.ppermute(given, "edp", swap)
        stride *= 2
    return part.reshape(1, rows // members, width)


def choice(routes, experts, capacity):
    matches = (routes[:, :, None] == jnp.arange(experts, dtype=jnp.int32)).any(axis=1)
    count = matches.astype(jnp.int32)
    earlier = jnp.cumsum(count, axis=0) - count
    slot = jnp.where(matches, earlier, -1)
    chosen = slot[:, :, None] == jnp.arange(capacity, dtype=jnp.int32)
    return chosen.astype(jnp.bfloat16).reshape(routes.shape[0], experts * capacity)


def shards(routes, gate_pre, up_pre, hidden_grad, w_gate, w_up, bucket_terms):
    experts = lax.axis_size("ep")
    capacity = gate_pre.shape[3]
    width, hidden = w_gate.shape[1:]
    gate_f = gate_pre.reshape(experts * capacity, hidden).astype(jnp.float32)
    up_f = up_pre.reshape(experts * capacity, hidden).astype(jnp.float32)
    grad_f = hidden_grad.reshape(experts * capacity, hidden).astype(jnp.float32)
    sigmoid_gate = 1.0 / (1.0 + jnp.exp(-gate_f))
    grad_gate = (grad_f * up_f * sigmoid_gate * (1.0 + gate_f * (1.0 - sigmoid_gate))).astype(
        jnp.bfloat16
    )
    grad_up = (grad_f * gate_f * sigmoid_gate).astype(jnp.bfloat16)
    dims = (((1,), (1,)), ((), ()))
    first = lax.dot_general(grad_gate, w_gate[0], dims, preferred_element_type=jnp.float32)
    second = lax.dot_general(grad_up, w_up[0], dims, preferred_element_type=jnp.float32)
    slot_grad = (first + second).astype(jnp.bfloat16)
    returned = lax.all_to_all(
        slot_grad.reshape(experts, capacity, width), "ep", split_axis=0, concat_axis=0, tiled=True
    )
    flat_rows = returned.reshape(experts * capacity, width)
    chosen = choice(routes, experts, capacity)
    token_grad = jnp.dot(chosen, flat_rows, preferred_element_type=jnp.float32).astype(jnp.bfloat16)
    reduced = reduce_bucket(bucket_terms[0, 0])
    return (token_grad, reduced)


def solution(mesh):
    placed = (
        P(("ep", "edp"), None),
        P("ep", "edp", None, None, None),
        P("ep", "edp", None, None, None),
        P("ep", "edp", None, None, None),
        P("ep", None, None),
        P("ep", None, None),
        P("ep", "edp", None, None),
    )
    return jax.shard_map(
        shards,
        mesh=mesh,
        in_specs=placed,
        out_specs=(P(("ep", "edp"), None), P("ep", "edp", None)),
        check_vma=False,
    )
```

time: 308 us -> 107 us (0.35)
  the two profiles are of different devices: /device:TPU:1 before, /device:TPU:190 now
where the time goes in v1:
time: 107 us
  waiting for transfers between devices  48.9 us (46%)
  starting transfers between devices  37.1 us (35%)
  matrix products  8.53 us (8%)
  other arithmetic  5.72 us (5%)
  local copies, waits for them, and re-layouts  5.38 us (5%)
    all_to_all x1, waiting for transfers between devices, shards(): lax.all_to_all(slot_grad.reshape(experts, capacity, width), 'ep', split_a...  28 us
    ppermute x5, waiting for transfers between devices, reduce_bucket(): part = kept + lax.ppermute(given, 'edp', swap)  20.9 us
    all_to_all x1, starting transfers between devices, shards(): lax.all_to_all(slot_grad.reshape(experts, capacity, width), 'ep', split_a...  20.7 us
    ppermute x5, starting transfers between devices, reduce_bucket(): part = kept + lax.ppermute(given, 'edp', swap)  16.4 us
    dot_general x1, matrix products, shards(): jnp.dot(chosen, flat_rows, preferred_element_type=jnp.float32)  3.57 us
    dot_general x1, matrix products, shards(): lax.dot_general(grad_gate, w_gate[0], dims, preferred_element_type=jnp.fl...  3.14 us
    add x5, other arithmetic, reduce_bucket(): part = kept + lax.ppermute(given, 'edp', swap)  3.03 us
    convert_element_type x1, other arithmetic, shards(): (grad_f * up_f * sigmoid_gate * (1.0 + gate_f * (1.0 - sigmoid_gate))).as...  2.57 us
  transfers between devices with their start and end apart: 6, of which 6 were waited for; matrix products, arithmetic and copies ran while one was open for 7% of the time, Pallas kernels for 0%

profile of v1, /device:TPU:190, one launch (start us, length us, event | category | flops | bytes accessed | tf_op | source)
XLA Modules:
  0.0 106.5 jit_solution(15105519293164851321)
XLA Ops:
  0.6 0.0 copy-start
  0.6 2.6 %fusion.10 = (bf16[1,1,32,16,768]{4,3,2,1,0:T(8,128)(2,1)S(1)}, bf16[1,1,32,16,768]{4,3,2,1,0:T(8,128)(2,1)S(1)}) fusion(bf16[1,1,32,16,768]{4,3,2,1,0:T(8,128)(2,1)} %param.10, bf16[1,1,32,16,768]{4,3,2,1,0:T(8,128)(2,1)} %param.8, bf16[1,1,32,16,768]{4,3,2,1,0:T(8,128)(2,1)} %param.9), kind=kLoop, calls=%fused_computation.14 | loop fusion | flops 6291456 | bytes 3932160 | tf_op jit(solution)/shard_map/convert_element_type | solution.py:41
  3.2 0.0 copy-done
  3.2 1.8 %fusion = f32[512,2048]{1,0:T(8,128)S(1)} fusion(bf16[512,768]{1,0:T(8,128)(2,1)S(1)} %bitcast.48, bf16[1,2048,768]{2,1,0:T(8,128)(2,1)S(1)} %copy-done), kind=kOutput, calls=%fused_computation.1 | convolution fusion | flops 1610612736 | bytes 8126464 | tf_op jit(solution)/shard_map/dot_general | solution.py:47
  5.1 0.1 copy-done.3
  5.1 3.1 %add_convert_fusion = bf16[512,2048]{1,0:T(8,128)(2,1)} fusion(f32[512,2048]{1,0:T(8,128)S(1)} %fusion, bf16[512,768]{1,0:T(8,128)(2,1)S(1)} %bitcast.47, bf16[1,2048,768]{2,1,0:T(8,128)(2,1)S(1)} %copy-done.3), kind=kOutput, calls=%fused_computation | convolution fusion | flops 1612709888 | bytes 10223616 | tf_op jit(solution)/shard_map/dot_general | solution.py:46
  8.3 20.7 %all-to-all-start = ((bf16[32,16,2048]{2,1,0:T(8,128)(2,1)}), bf16[32,16,2048]{2,1,0:T(8,128)(2,1)}, u32[]{:S(2)}, u32[]{:S(2)}) async-start(bf16[32,16,2048]{2,1,0:T(8,128)(2,1)} %bitcast.42), calls=%async_computation | async-start | bytes 4194304 | tf_op jit(solution)/shard_map/all_to_all | solution.py:49
  29.0 2.1 %reshape_reshape_squeeze.3 = f32[16,2,48,128]{3,2,1,0:T(8,128)} reshape(f32[1,1,128,1536]{3,2,1,0:T(8,128)} %param.13) | data formatting | bytes 1572864 | tf_op jit(solution)/shard_map/reshape;reshape;squeeze | solution.py:14
  31.0 1.0 dynamic-slice_bitcast_fusion
  32.1 1.9 %collective-permute-start = (f32[16,48,128]{2,1,0:T(8,128)S(1)}, f32[16,48,128]{2,1,0:T(8,128)}, u32[]{:S(2)}, u32[]{:S(2)}) collective-permute-start(f32[16,48,128]{2,1,0:T(8,128)S(1)} %dynamic-slice_bitcast_fusion), channel_id=1, source_target_pairs={{0,1},{1,0},{2,3},{3,2},{4,5},{5,4},{6,7},{7,6},{8,9},{9,8},{10,11... | collective-permute-start | bytes 1179656 | tf_op jit(solution)/shard_map/ppermute | solution.py:19
  34.0 1.8 %collective-permute-done = f32[16,48,128]{2,1,0:T(8,128)} collective-permute-done((f32[16,48,128]{2,1,0:T(8,128)S(1)}, f32[16,48,128]{2,1,0:T(8,128)}, u32[]{:S(2)}, u32[]{:S(2)}) %collective-permute-start) | collective-permute-done | bytes 393248 | tf_op jit(solution)/shard_map/ppermute | solution.py:19
  35.8 1.2 %bitcast_add_fusion = f32[16,48,128]{2,1,0:T(8,128)S(1)} fusion(f32[16,48,128]{2,1,0:T(8,128)} %collective-permute-done, f32[16,2,48,128]{3,2,1,0:T(8,128)} %reshape_reshape_squeeze.3, s32[]{:T(128)S(6)} %select_n.82), kind=kLoop, calls=%fused_computation.21 | loop fusion | flops 98304 | bytes 1179652 | tf_op jit(solution)/shard_map/add | solution.py:19
  37.0 0.7 dynamic-slice_bitcast_fusion.1
  37.7 3.3 %collective-permute-start.1 = (f32[8,48,128]{2,1,0:T(8,128)}, f32[8,48,128]{2,1,0:T(8,128)}, u32[]{:S(2)}, u32[]{:S(2)}) collective-permute-start(f32[8,48,128]{2,1,0:T(8,128)} %dynamic-slice_bitcast_fusion.1), channel_id=1, source_target_pairs={{0,2},{1,3},{2,0},{3,1},{4,6},{5,7},{6,4},{7,5},{8,10},{9,11},{10,... | collective-permute-start | bytes 589832 | tf_op jit(solution)/shard_map/ppermute | solution.py:19
  41.1 5.8 %collective-permute-done.1 = f32[8,48,128]{2,1,0:T(8,128)} collective-permute-done((f32[8,48,128]{2,1,0:T(8,128)}, f32[8,48,128]{2,1,0:T(8,128)}, u32[]{:S(2)}, u32[]{:S(2)}) %collective-permute-start.1) | collective-permute-done | bytes 196640 | tf_op jit(solution)/shard_map/ppermute | solution.py:19
  46.8 1.0 bitcast_add_fusion.1
  47.8 0.0 copy-start.1
  47.8 0.7 copy-done.1
  48.5 4.2 %collective-permute-start.2 = (f32[4,48,128]{2,1,0:T(8,128)S(1)}, f32[4,48,128]{2,1,0:T(8,128)S(1)}, u32[]{:S(2)}, u32[]{:S(2)}) collective-permute-start(f32[4,48,128]{2,1,0:T(8,128)S(1)} %dynamic-slice_bitcast_fusion.2), channel_id=1, source_target_pairs={{0,4},{1,5},{2,6},{3,7},{4,0},{5,1},{6,2},{7,3},{8,12},{9,13},{10,... | collective-permute-start | bytes 294920 | tf_op jit(solution)/shard_map/ppermute | solution.py:19
  52.7 4.6 %collective-permute-done.2 = f32[4,48,128]{2,1,0:T(8,128)S(1)} collective-permute-done((f32[4,48,128]{2,1,0:T(8,128)S(1)}, f32[4,48,128]{2,1,0:T(8,128)S(1)}, u32[]{:S(2)}, u32[]{:S(2)}) %collective-permute-start.2) | collective-permute-done | bytes 98336 | tf_op jit(solution)/shard_map/ppermute | solution.py:19
  57.4 0.9 bitcast_add_fusion.2
  58.3 5.0 %collective-permute-start.3 = (f32[2,48,128]{2,1,0:T(8,128)S(1)}, f32[2,48,128]{2,1,0:T(8,128)S(1)}, u32[]{:S(2)}, u32[]{:S(2)}) collective-permute-start(f32[2,48,128]{2,1,0:T(8,128)S(1)} %dynamic-slice_bitcast_fusion.3), channel_id=1, source_target_pairs={{0,8},{1,9},{2,10},{3,11},{4,12},{5,13},{6,14},{7,15},{8,0},{9,1},... | collective-permute-start | bytes 147464 | tf_op jit(solution)/shard_map/ppermute | solution.py:19
  63.3 0.0 copy-done.2
  63.4 0.1 copy.29
  63.5 0.1 reduce_window_sum.11
  63.6 4.9 %collective-permute-done.3 = f32[2,48,128]{2,1,0:T(8,128)S(1)} collective-permute-done((f32[2,48,128]{2,1,0:T(8,128)S(1)}, f32[2,48,128]{2,1,0:T(8,128)S(1)}, u32[]{:S(2)}, u32[]{:S(2)}) %collective-permute-start.3) | collective-permute-done | bytes 49184 | tf_op jit(solution)/shard_map/ppermute | solution.py:19
  68.5 1.9 %collective-permute-start.4 = (f32[1,48,128]{2,1,0:T(8,128)S(1)}, f32[1,48,128]{2,1,0:T(8,128)S(1)}, u32[]{:S(2)}, u32[]{:S(2)}) collective-permute-start(f32[1,48,128]{2,1,0:T(8,128)S(1)} %constant_dynamic-slice_fusion), channel_id=1, source_target_pairs={{0,16},{1,17},{2,18},{3,19},{4,20},{5,21},{6,22},{7,23},{8,24},{9,... | collective-permute-start | bytes 73736 | tf_op jit(solution)/shard_map/ppermute | solution.py:19
  70.4 0.1 copy.30
  70.5 3.9 %collective-permute-done.4 = f32[1,48,128]{2,1,0:T(8,128)S(1)} collective-permute-done((f32[1,48,128]{2,1,0:T(8,128)S(1)}, f32[1,48,128]{2,1,0:T(8,128)S(1)}, u32[]{:S(2)}, u32[]{:S(2)}) %collective-permute-start.4) | collective-permute-done | bytes 24608 | tf_op jit(solution)/shard_map/ppermute | solution.py:19
  74.4 0.6 reshape.49
  75.0 28.0 %all-to-all-done = bf16[32,16,2048]{2,1,0:T(8,128)(2,1)} async-done(((bf16[32,16,2048]{2,1,0:T(8,128)(2,1)}), bf16[32,16,2048]{2,1,0:T(8,128)(2,1)}, u32[]{:S(2)}, u32[]{:S(2)}) %all-to-all-start) | async-done | bytes 2097184 | tf_op jit(solution)/shard_map/all_to_all | solution.py:49
  103.0 3.6 %fusion.6 = bf16[48,2048]{1,0:T(8,128)(2,1)} fusion(bf16[32,16,2048]{2,1,0:T(8,128)(2,1)} %all-to-all-done, s32[48,32]{0,1:T(8,128)S(1)} %copy.30), kind=kOutput, calls=%fused_computation.9 | convolution fusion | flops 100786176 | bytes 2299904 | tf_op jit(solution)/shard_map/dot_general | solution.py:54
  (10 shorter events, 0.1 us)
Async XLA Ops:
  0.6 2.6 %copy-start = (bf16[1,2048,768]{2,1,0:T(8,128)(2,1)S(1)}, bf16[1,2048,768]{2,1,0:T(8,128)(2,1)}, u32[]{:S(2)}) copy-start(bf16[1,2048,768]{2,1,0:T(8,128)(2,1)} %param.12) | copy-start | bytes 9437188
  3.2 1.9 %copy-start.3 = (bf16[1,2048,768]{2,1,0:T(8,128)(2,1)S(1)}, bf16[1,2048,768]{2,1,0:T(8,128)(2,1)}, u32[]{:S(2)}) copy-start(bf16[1,2048,768]{2,1,0:T(8,128)(2,1)} %param.11) | copy-start | bytes 9437188
  8.3 94.7 %all-to-all-start = ((bf16[32,16,2048]{2,1,0:T(8,128)(2,1)}), bf16[32,16,2048]{2,1,0:T(8,128)(2,1)}, u32[]{:S(2)}, u32[]{:S(2)}) async-start(bf16[32,16,2048]{2,1,0:T(8,128)(2,1)} %bitcast.42), calls=%async_computation | async-start | bytes 4194304 | tf_op jit(solution)/shard_map/all_to_all | solution.py:49
  31.0 32.3 %copy-start.2 = (s32[48,8]{0,1:T(8,128)S(1)}, s32[48,8]{0,1:T(8,128)}, u32[]{:S(2)}) copy-start(s32[48,8]{0,1:T(8,128)} %param.7) | copy-start | bytes 4612
  32.1 3.7 %collective-permute-start = (f32[16,48,128]{2,1,0:T(8,128)S(1)}, f32[16,48,128]{2,1,0:T(8,128)}, u32[]{:S(2)}, u32[]{:S(2)}) collective-permute-start(f32[16,48,128]{2,1,0:T(8,128)S(1)} %dynamic-slice_bitcast_fusion), channel_id=1, source_target_pairs={{0,1},{1,0},{2,3},{3,2},{4,5},{5,4},{6,7},{7,6},{8,9},{9,8},{10,11... | collective-permute-start | bytes 1179656 | tf_op jit(solution)/shard_map/ppermute | solution.py:19
  37.7 9.1 %collective-permute-start.1 = (f32[8,48,128]{2,1,0:T(8,128)}, f32[8,48,128]{2,1,0:T(8,128)}, u32[]{:S(2)}, u32[]{:S(2)}) collective-permute-start(f32[8,48,128]{2,1,0:T(8,128)} %dynamic-slice_bitcast_fusion.1), channel_id=1, source_target_pairs={{0,2},{1,3},{2,0},{3,1},{4,6},{5,7},{6,4},{7,5},{8,10},{9,11},{10,... | collective-permute-start | bytes 589832 | tf_op jit(solution)/shard_map/ppermute | solution.py:19
  47.8 0.7 copy-start.1
  48.5 8.9 %collective-permute-start.2 = (f32[4,48,128]{2,1,0:T(8,128)S(1)}, f32[4,48,128]{2,1,0:T(8,128)S(1)}, u32[]{:S(2)}, u32[]{:S(2)}) collective-permute-start(f32[4,48,128]{2,1,0:T(8,128)S(1)} %dynamic-slice_bitcast_fusion.2), channel_id=1, source_target_pairs={{0,4},{1,5},{2,6},{3,7},{4,0},{5,1},{6,2},{7,3},{8,12},{9,13},{10,... | collective-permute-start | bytes 294920 | tf_op jit(solution)/shard_map/ppermute | solution.py:19
  58.3 10.1 %collective-permute-start.3 = (f32[2,48,128]{2,1,0:T(8,128)S(1)}, f32[2,48,128]{2,1,0:T(8,128)S(1)}, u32[]{:S(2)}, u32[]{:S(2)}) collective-permute-start(f32[2,48,128]{2,1,0:T(8,128)S(1)} %dynamic-slice_bitcast_fusion.3), channel_id=1, source_target_pairs={{0,8},{1,9},{2,10},{3,11},{4,12},{5,13},{6,14},{7,15},{8,0},{9,1},... | collective-permute-start | bytes 147464 | tf_op jit(solution)/shard_map/ppermute | solution.py:19
  68.5 5.9 %collective-permute-start.4 = (f32[1,48,128]{2,1,0:T(8,128)S(1)}, f32[1,48,128]{2,1,0:T(8,128)S(1)}, u32[]{:S(2)}, u32[]{:S(2)}) collective-permute-start(f32[1,48,128]{2,1,0:T(8,128)S(1)} %constant_dynamic-slice_fusion), channel_id=1, source_target_pairs={{0,16},{1,17},{2,18},{3,19},{4,20},{5,21},{6,22},{7,23},{8,24},{9,... | collective-permute-start | bytes 73736 | tf_op jit(solution)/shard_map/ppermute | solution.py:19

commit v2 on v1

v2 whole, which is shorter than its diff:
```python
import jax
import jax.numpy as jnp
from jax import lax
from jax.experimental import pallas as pl
from jax.experimental.pallas import tpu as pltpu
from jax.sharding import PartitionSpec as P

BOTH = ("ep", "edp")
LINE = 8
REST = 4
TILE = 256


def reduce_bucket(bucket):
    rows, width = bucket.shape
    members = lax.axis_size("edp")
    own = lax.axis_index("edp")
    part = bucket.reshape(members, rows * width // (members * 128), 128)
    stride = 1
    while stride < members:
        pairs = part.reshape(part.shape[0] // 2, 2, *part.shape[1:])
        bit = (own // stride) % 2
        kept = lax.dynamic_index_in_dim(pairs, bit, axis=1, keepdims=False)
        given = lax.dynamic_index_in_dim(pairs, 1 - bit, axis=1, keepdims=False)
        swap = [(i, i ^ stride) for i in range(members)]
        part = kept + lax.ppermute(given, "edp", swap)
        stride *= 2
    return part.reshape(1, rows // members, width)


def place(core, member, rest):
    across = rest * LINE + member
    along = (member // 2) * LINE + rest * 2 + member % 2
    return across + core * (along - across)


def first_groups(members):
    return [
        [place(j % 2, g, r) * members + j for g in range(LINE)]
        for j in range(members)
        for r in range(REST)
    ]


def second_groups(members):
    return [
        [place(j % 2, g, r) * members + j for r in range(REST)]
        for j in range(members)
        for g in range(LINE)
    ]


def row_kernel(core_ref, gate_ref, up_ref, grad_ref, w_gate_ref, w_up_ref, out_ref, packed):
    hidden = gate_ref.shape[2]
    rows = gate_ref.shape[1]
    core = core_ref[0]

    @pl.when(pl.program_id(0) == 0)
    def _():
        def block(p, carry):
            s = place(core, p // REST, p % REST)
            gate = gate_ref[s].astype(jnp.float32)
            up = up_ref[s].astype(jnp.float32)
            grad = grad_ref[s].astype(jnp.float32)
            sig = 0.5 + 0.5 * jnp.tanh(0.5 * gate)
            scaled = grad * sig
            to = pl.ds(pl.multiple_of(p * rows, rows), rows)
            packed[to, :hidden] = (scaled * up * (1.0 + gate * (1.0 - sig))).astype(jnp.bfloat16)
            packed[to, hidden:] = (scaled * gate).astype(jnp.bfloat16)
            return carry

        lax.fori_loop(0, gate_ref.shape[0], block, 0, unroll=4)

    dims = (((1,), (1,)), ((), ()))
    total = lax.dot_general(
        packed[:, :hidden], w_gate_ref[...], dims, preferred_element_type=jnp.float32
    ) + lax.dot_general(
        packed[:, hidden:], w_up_ref[...], dims, preferred_element_type=jnp.float32
    )
    out_ref[...] = total.astype(jnp.bfloat16)


def send_rows(core, gate, up, grad, w_gate, w_up):
    sources, capacity, hidden = gate.shape
    width = w_gate.shape[0]
    whole = pl.BlockSpec((sources, capacity, hidden), lambda n, core: (0, 0, 0), pipeline_mode=pl.Buffered(1))
    weight = pl.BlockSpec((TILE, hidden), lambda n, core: (n, 0))
    return pl.pallas_call(
        row_kernel,
        grid_spec=pltpu.PrefetchScalarGridSpec(
            num_scalar_prefetch=1,
            grid=(width // TILE,),
            in_specs=[whole, whole, whole, weight, weight],
            out_specs=pl.BlockSpec((sources * capacity, TILE), lambda n, core: (0, n)),
            scratch_shapes=[pltpu.VMEM((sources * capacity, 2 * hidden), jnp.bfloat16)],
        ),
        out_shape=jax.ShapeDtypeStruct((sources * capacity, width), jnp.bfloat16),
        compiler_params=pltpu.CompilerParams(vmem_limit_bytes=60 * 1024 * 1024),
        cost_estimate=pl.CostEstimate(
            flops=4 * sources * capacity * hidden * width,
            bytes_accessed=6 * sources * capacity * hidden + 4 * hidden * width + 2 * sources * capacity * width,
            transcendentals=sources * capacity * hidden,
        ),
    )(core.reshape(1), gate, up, grad, w_gate, w_up)


def gathered_routes(routes, core, rest, experts, members):
    stack = routes[None]
    size = 1
    while size < REST:
        swap = [
            (place(j % 2, g, r) * members + j, place(j % 2, g, r ^ size) * members + j)
            for j in range(members)
            for g in range(LINE)
            for r in range(REST)
        ]
        other = lax.ppermute(stack, BOTH, swap)
        low = (rest // size) % 2 == 0
        stack = jnp.concatenate(
            [jnp.where(low, stack, other), jnp.where(low, other, stack)], axis=0
        )
        size *= 2
    return stack


def choice(routes, core, rest, capacity):
    tokens = routes.shape[1]
    named = place(core, jnp.arange(LINE, dtype=jnp.int32), rest)
    matches = (routes[:, :, :, None] == named).any(axis=2)
    count = matches.astype(jnp.int32)
    earlier = jnp.cumsum(count, axis=1) - count
    slot = jnp.where(matches, earlier, -1).reshape(REST * tokens, LINE).astype(jnp.bfloat16)
    column = jnp.arange(LINE * REST * capacity, dtype=jnp.int32)
    spread = (column[None, :] // (REST * capacity) == jnp.arange(LINE, dtype=jnp.int32)[:, None]).astype(jnp.bfloat16)
    slots = jnp.dot(slot, spread, preferred_element_type=jnp.float32)
    owner = jnp.arange(REST * tokens, dtype=jnp.int32)[:, None] // tokens
    same = owner == (column // capacity % REST)[None, :]
    chosen = same & (slots == (column % capacity).astype(jnp.float32)[None, :])
    return chosen.astype(jnp.bfloat16)


def shards(routes, gate_pre, up_pre, hidden_grad, w_gate, w_up, bucket_terms):
    members = lax.axis_size("edp")
    experts, capacity, hidden = gate_pre.shape[2:]
    tokens = routes.shape[0]
    width = w_gate.shape[1]
    core = lax.axis_index("edp") % 2
    own = lax.axis_index("ep")
    rest = jnp.where(core == 0, own // LINE, own % LINE // 2)
    rows = send_rows(core, gate_pre[0, 0], up_pre[0, 0], hidden_grad[0, 0], w_gate[0], w_up[0])
    arrived = lax.all_to_all(
        rows.reshape(LINE, REST * capacity, width),
        BOTH,
        split_axis=0,
        concat_axis=0,
        axis_index_groups=first_groups(members),
        tiled=True,
    )
    chosen = choice(gathered_routes(routes, core, rest, experts, members), core, rest, capacity)
    chosen = lax.optimization_barrier(chosen)
    partial = jnp.dot(
        chosen, arrived.reshape(experts * capacity, width), preferred_element_type=jnp.float32
    ).astype(jnp.bfloat16)
    last = lax.all_to_all(
        partial.reshape(REST, tokens, width),
        BOTH,
        split_axis=0,
        concat_axis=0,
        axis_index_groups=second_groups(members),
        tiled=True,
    )
    parts = [last[r].astype(jnp.float32) for r in range(REST)]
    token_grad = sum(parts[1:], parts[0]).astype(jnp.bfloat16)
    reduced = reduce_bucket(bucket_terms[0, 0])
    return (token_grad, reduced)


def solution(mesh):
    placed = (
        P(("ep", "edp"), None),
        P("ep", "edp", None, None, None),
        P("ep", "edp", None, None, None),
        P("ep", "edp", None, None, None),
        P("ep", None, None),
        P("ep", None, None),
        P("ep", "edp", None, None),
    )
    return jax.shard_map(
        shards,
        mesh=mesh,
        in_specs=placed,
        out_specs=(P(("ep", "edp"), None), P("ep", "edp", None)),
        check_vma=False,
    )
```

time: 107 us -> 112 us (1.047)
  the two profiles are of different devices: /device:TPU:190 before, /device:TPU:1 now
where the time goes in v2:
time: 112 us
  waiting for transfers between devices  47.2 us (42%)
  starting transfers between devices  46.9 us (42%)
  Pallas kernels  10.6 us (9%)
  local copies, waits for them, and re-layouts  2.89 us (3%)
  matrix products  1.73 us (2%)
  other arithmetic  1.17 us (1%)
    ppermute x2, waiting for transfers between devices, gathered_routes(): other = lax.ppermute(stack, BOTH, swap)  27.5 us
    ppermute x5, waiting for transfers between devices, reduce_bucket(): part = kept + lax.ppermute(given, 'edp', swap)  19.8 us
    all_to_all x1, starting transfers between devices, shards(): lax.all_to_all(rows.reshape(LINE, REST * capacity, width), BOTH, split_ax...  17.6 us
    ppermute x2, starting transfers between devices, gathered_routes(): other = lax.ppermute(stack, BOTH, swap)  11.2 us
    pallas_call x1, Pallas kernels, send_rows(): pl.pallas_call(row_kernel, grid_spec=pltpu.PrefetchScalarGridSpec(num_sca...  10.6 us
    ppermute x5, starting transfers between devices, reduce_bucket(): part = kept + lax.ppermute(given, 'edp', swap)  9.59 us
    all_to_all x1, starting transfers between devices, shards(): lax.all_to_all(partial.reshape(REST, tokens, width), BOTH, split_axis=0,...  8.6 us
  transfers between devices with their start and end apart: 9, of which 6 were waited for; matrix products, arithmetic and copies ran while one was open for 3% of the time, Pallas kernels for 0%

profile of v2, /device:TPU:1, one launch (start us, length us, event | category | flops | bytes accessed | tf_op | source)
XLA Modules:
  0.0 111.6 jit_solution(15135449785512016214)
XLA Ops:
  0.6 10.6 %shard_map.86 = bf16[512,2048]{1,0:T(8,128)(2,1)} custom-call(s32[1]{0:T(128)} %bitcast.2.core_ref, bf16[32,16,768]{2,1,0:T(8,128)(2,1)} %bitcast.56, bf16[32,16,768]{2,1,0:T(8,128)(2,1)} %bitcast.57, bf16[32,16,768]{2,1,0:T(8,128)(2,1)} %bitcast.58, bf16[2048,768]{1,0:T(8,128)(2,1)} %bitcast.54, bf16[2048,768]{1,0:T(8,128)(2,1)} %bitcast.55), custom_call_target="tpu_custom_call" | custom-call | flops 3221225472 | bytes 10747904 | tf_op jit(solution)/shard_map/pallas_call | solution.py:88
  11.2 17.6 %all-to-all-start = ((bf16[8,64,2048]{2,1,0:T(8,128)(2,1)}), bf16[8,64,2048]{2,1,0:T(8,128)(2,1)S(1)}, u32[]{:S(2)}, u32[]{:S(2)}) async-start(bf16[8,64,2048]{2,1,0:T(8,128)(2,1)} %bitcast.45), calls=%async_computation | async-start | bytes 4194304 | tf_op jit(solution)/shard_map/all_to_all | solution.py:151
  28.8 0.0 copy-done
  28.8 4.4 %collective-permute-start = (s32[1,48,8]{1,2,0:T(8,128)S(1)}, s32[1,48,8]{1,2,0:T(8,128)S(1)}, u32[]{:S(2)}, u32[]{:S(2)}) collective-permute-start(s32[1,48,8]{1,2,0:T(8,128)S(1)} %bitcast.53), channel_id=1, source_target_pairs={{0,256},{256,0},{512,768},{768,512},{32,288},{288,32},{544,800},{8... | collective-permute-start | bytes 4616 | tf_op jit(solution)/shard_map/ppermute | solution.py:117
  33.2 1.2 %reshape_reshape_squeeze.3 = f32[16,2,48,128]{3,2,1,0:T(8,128)S(1)} reshape(f32[1,1,128,1536]{3,2,1,0:T(8,128)} %param.13) | data formatting | bytes 1572864 | tf_op jit(solution)/shard_map/reshape;reshape;squeeze | solution.py:21
  34.4 0.8 dynamic-slice_bitcast_fusion
  35.2 1.9 %collective-permute-start.2 = (f32[16,48,128]{2,1,0:T(8,128)}, f32[16,48,128]{2,1,0:T(8,128)S(1)}, u32[]{:S(2)}, u32[]{:S(2)}) collective-permute-start(f32[16,48,128]{2,1,0:T(8,128)} %dynamic-slice_bitcast_fusion), channel_id=1, source_target_pairs={{0,1},{1,0},{2,3},{3,2},{4,5},{5,4},{6,7},{7,6},{8,9},{9,8},{10,11... | collective-permute-start | bytes 1179656 | tf_op jit(solution)/shard_map/ppermute | solution.py:26
  37.3 26.0 %collective-permute-done = s32[1,48,8]{1,2,0:T(8,128)S(1)} collective-permute-done((s32[1,48,8]{1,2,0:T(8,128)S(1)}, s32[1,48,8]{1,2,0:T(8,128)S(1)}, u32[]{:S(2)}, u32[]{:S(2)}) %collective-permute-start) | collective-permute-done | bytes 1568 | tf_op jit(solution)/shard_map/ppermute | solution.py:117
  63.3 6.7 %collective-permute-start.1 = (s32[2,48,8]{1,2,0:T(8,128)S(1)}, s32[2,48,8]{1,2,0:T(8,128)S(1)}, u32[]{:S(2)}, u32[]{:S(2)}) collective-permute-start(s32[2,48,8]{1,2,0:T(8,128)S(1)} %pad_add_fusion.1), channel_id=1, source_target_pairs={{0,512},{256,768},{512,0},{768,256},{32,544},{288,800},{544,32},{8... | collective-permute-start | bytes 9224 | tf_op jit(solution)/shard_map/ppermute | solution.py:117
  70.1 1.5 %collective-permute-done.1 = s32[2,48,8]{1,2,0:T(8,128)S(1)} collective-permute-done((s32[2,48,8]{1,2,0:T(8,128)S(1)}, s32[2,48,8]{1,2,0:T(8,128)S(1)}, u32[]{:S(2)}, u32[]{:S(2)}) %collective-permute-start.1) | collective-permute-done | bytes 3104 | tf_op jit(solution)/shard_map/ppermute | solution.py:117
  71.6 0.1 compare_reduce_fusion
  71.7 0.1 reduce_or.12
  71.8 0.1 copy.19
  71.9 0.1 reduce_window_sum.13
  72.0 0.1 copy.20
  72.1 0.0 collective-permute-done.2
  72.1 0.1 bitcast_add_fusion
  72.2 1.9 %collective-permute-start.3 = (f32[8,48,128]{2,1,0:T(8,128)S(1)}, f32[8,48,128]{2,1,0:T(8,128)S(1)}, u32[]{:S(2)}, u32[]{:S(2)}) collective-permute-start(f32[8,48,128]{2,1,0:T(8,128)S(1)} %dynamic-slice_bitcast_fusion.1), channel_id=1, source_target_pairs={{0,2},{1,3},{2,0},{3,1},{4,6},{5,7},{6,4},{7,5},{8,10},{9,11},{10,... | collective-permute-start | bytes 589832 | tf_op jit(solution)/shard_map/ppermute | solution.py:26
  74.1 0.3 fusion.1
  74.4 4.2 %collective-permute-done.3 = f32[8,48,128]{2,1,0:T(8,128)S(1)} collective-permute-done((f32[8,48,128]{2,1,0:T(8,128)S(1)}, f32[8,48,128]{2,1,0:T(8,128)S(1)}, u32[]{:S(2)}, u32[]{:S(2)}) %collective-permute-start.3) | collective-permute-done | bytes 196640 | tf_op jit(solution)/shard_map/ppermute | solution.py:26
  78.6 0.0 all-to-all-done
  78.6 1.5 %convolution_convert_fusion = bf16[192,2048]{1,0:T(8,128)(2,1)} fusion(bf16[192,512]{1,0:T(8,128)(2,1)S(1)} %fusion.1, bf16[512,2048]{1,0:T(8,128)(2,1)S(1)} %bitcast.44), kind=kOutput, calls=%fused_computation | convolution fusion | flops 403046400 | bytes 3080192 | tf_op jit(solution)/shard_map/dot_general | solution.py:161
  80.1 8.6 %all-to-all-start.1 = ((bf16[4,48,2048]{2,1,0:T(8,128)(2,1)}), bf16[4,48,2048]{2,1,0:T(8,128)(2,1)S(1)}, u32[]{:S(2)}, u32[]{:S(2)}) async-start(bf16[4,48,2048]{2,1,0:T(8,128)(2,1)} %bitcast.10), calls=%async_computation.1 | async-start | bytes 1572864 | tf_op jit(solution)/shard_map/all_to_all | solution.py:164
  88.7 1.9 %collective-permute-start.4 = (f32[4,48,128]{2,1,0:T(8,128)S(1)}, f32[4,48,128]{2,1,0:T(8,128)S(1)}, u32[]{:S(2)}, u32[]{:S(2)}) collective-permute-start(f32[4,48,128]{2,1,0:T(8,128)S(1)} %dynamic-slice_bitcast_fusion.2), channel_id=1, source_target_pairs={{0,4},{1,5},{2,6},{3,7},{4,0},{5,1},{6,2},{7,3},{8,12},{9,13},{10,... | collective-permute-start | bytes 294920 | tf_op jit(solution)/shard_map/ppermute | solution.py:26
  90.7 6.1 %collective-permute-done.4 = f32[4,48,128]{2,1,0:T(8,128)S(1)} collective-permute-done((f32[4,48,128]{2,1,0:T(8,128)S(1)}, f32[4,48,128]{2,1,0:T(8,128)S(1)}, u32[]{:S(2)}, u32[]{:S(2)}) %collective-permute-start.4) | collective-permute-done | bytes 98336 | tf_op jit(solution)/shard_map/ppermute | solution.py:26
  96.9 1.9 %collective-permute-start.5 = (f32[2,48,128]{2,1,0:T(8,128)S(1)}, f32[2,48,128]{2,1,0:T(8,128)S(1)}, u32[]{:S(2)}, u32[]{:S(2)}) collective-permute-start(f32[2,48,128]{2,1,0:T(8,128)S(1)} %dynamic-slice_bitcast_fusion.3), channel_id=1, source_target_pairs={{0,8},{1,9},{2,10},{3,11},{4,12},{5,13},{6,14},{7,15},{8,0},{9,1},... | collective-permute-start | bytes 147464 | tf_op jit(solution)/shard_map/ppermute | solution.py:26
  98.8 6.8 %collective-permute-done.5 = f32[2,48,128]{2,1,0:T(8,128)S(1)} collective-permute-done((f32[2,48,128]{2,1,0:T(8,128)S(1)}, f32[2,48,128]{2,1,0:T(8,128)S(1)}, u32[]{:S(2)}, u32[]{:S(2)}) %collective-permute-start.5) | collective-permute-done | bytes 49184 | tf_op jit(solution)/shard_map/ppermute | solution.py:26
  105.6 1.9 %collective-permute-start.6 = (f32[1,48,128]{2,1,0:T(8,128)S(1)}, f32[1,48,128]{2,1,0:T(8,128)S(1)}, u32[]{:S(2)}, u32[]{:S(2)}) collective-permute-start(f32[1,48,128]{2,1,0:T(8,128)S(1)} %constant_dynamic-slice_fusion), channel_id=1, source_target_pairs={{0,16},{1,17},{2,18},{3,19},{4,20},{5,21},{6,22},{7,23},{8,24},{9,... | collective-permute-start | bytes 73736 | tf_op jit(solution)/shard_map/ppermute | solution.py:26
  107.6 2.6 %collective-permute-done.6 = f32[1,48,128]{2,1,0:T(8,128)S(1)} collective-permute-done((f32[1,48,128]{2,1,0:T(8,128)S(1)}, f32[1,48,128]{2,1,0:T(8,128)S(1)}, u32[]{:S(2)}, u32[]{:S(2)}) %collective-permute-start.6) | collective-permute-done | bytes 24608 | tf_op jit(solution)/shard_map/ppermute | solution.py:26
  110.2 0.6 reshape.172
  110.8 0.0 all-to-all-done.1
  110.8 0.8 fusion.2
  (19 shorter events, 0.2 us)
Async XLA Ops:
  11.2 17.6 %copy-start = (s32[48,8]{0,1:T(8,128)S(1)}, s32[48,8]{0,1:T(8,128)}, u32[]{:S(2)}) copy-start(s32[48,8]{0,1:T(8,128)} %param.7) | copy-start | bytes 4612
  11.2 67.4 %all-to-all-start = ((bf16[8,64,2048]{2,1,0:T(8,128)(2,1)}), bf16[8,64,2048]{2,1,0:T(8,128)(2,1)S(1)}, u32[]{:S(2)}, u32[]{:S(2)}) async-start(bf16[8,64,2048]{2,1,0:T(8,128)(2,1)} %bitcast.45), calls=%async_computation | async-start | bytes 4194304 | tf_op jit(solution)/shard_map/all_to_all | solution.py:151
  28.8 34.5 %collective-permute-start = (s32[1,48,8]{1,2,0:T(8,128)S(1)}, s32[1,48,8]{1,2,0:T(8,128)S(1)}, u32[]{:S(2)}, u32[]{:S(2)}) collective-permute-start(s32[1,48,8]{1,2,0:T(8,128)S(1)} %bitcast.53), channel_id=1, source_target_pairs={{0,256},{256,0},{512,768},{768,512},{32,288},{288,32},{544,800},{8... | collective-permute-start | bytes 4616 | tf_op jit(solution)/shard_map/ppermute | solution.py:117
  35.2 36.9 %collective-permute-start.2 = (f32[16,48,128]{2,1,0:T(8,128)}, f32[16,48,128]{2,1,0:T(8,128)S(1)}, u32[]{:S(2)}, u32[]{:S(2)}) collective-permute-start(f32[16,48,128]{2,1,0:T(8,128)} %dynamic-slice_bitcast_fusion), channel_id=1, source_target_pairs={{0,1},{1,0},{2,3},{3,2},{4,5},{5,4},{6,7},{7,6},{8,9},{9,8},{10,11... | collective-permute-start | bytes 1179656 | tf_op jit(solution)/shard_map/ppermute | solution.py:26
  63.3 8.3 %collective-permute-start.1 = (s32[2,48,8]{1,2,0:T(8,128)S(1)}, s32[2,48,8]{1,2,0:T(8,128)S(1)}, u32[]{:S(2)}, u32[]{:S(2)}) collective-permute-start(s32[2,48,8]{1,2,0:T(8,128)S(1)} %pad_add_fusion.1), channel_id=1, source_target_pairs={{0,512},{256,768},{512,0},{768,256},{32,544},{288,800},{544,32},{8... | collective-permute-start | bytes 9224 | tf_op jit(solution)/shard_map/ppermute | solution.py:117
  72.2 6.4 %collective-permute-start.3 = (f32[8,48,128]{2,1,0:T(8,128)S(1)}, f32[8,48,128]{2,1,0:T(8,128)S(1)}, u32[]{:S(2)}, u32[]{:S(2)}) collective-permute-start(f32[8,48,128]{2,1,0:T(8,128)S(1)} %dynamic-slice_bitcast_fusion.1), channel_id=1, source_target_pairs={{0,2},{1,3},{2,0},{3,1},{4,6},{5,7},{6,4},{7,5},{8,10},{9,11},{10,... | collective-permute-start | bytes 589832 | tf_op jit(solution)/shard_map/ppermute | solution.py:26
  80.1 30.7 %all-to-all-start.1 = ((bf16[4,48,2048]{2,1,0:T(8,128)(2,1)}), bf16[4,48,2048]{2,1,0:T(8,128)(2,1)S(1)}, u32[]{:S(2)}, u32[]{:S(2)}) async-start(bf16[4,48,2048]{2,1,0:T(8,128)(2,1)} %bitcast.10), calls=%async_computation.1 | async-start | bytes 1572864 | tf_op jit(solution)/shard_map/all_to_all | solution.py:164
  88.7 8.1 %collective-permute-start.4 = (f32[4,48,128]{2,1,0:T(8,128)S(1)}, f32[4,48,128]{2,1,0:T(8,128)S(1)}, u32[]{:S(2)}, u32[]{:S(2)}) collective-permute-start(f32[4,48,128]{2,1,0:T(8,128)S(1)} %dynamic-slice_bitcast_fusion.2), channel_id=1, source_target_pairs={{0,4},{1,5},{2,6},{3,7},{4,0},{5,1},{6,2},{7,3},{8,12},{9,13},{10,... | collective-permute-start | bytes 294920 | tf_op jit(solution)/shard_map/ppermute | solution.py:26
  96.9 8.7 %collective-permute-start.5 = (f32[2,48,128]{2,1,0:T(8,128)S(1)}, f32[2,48,128]{2,1,0:T(8,128)S(1)}, u32[]{:S(2)}, u32[]{:S(2)}) collective-permute-start(f32[2,48,128]{2,1,0:T(8,128)S(1)} %dynamic-slice_bitcast_fusion.3), channel_id=1, source_target_pairs={{0,8},{1,9},{2,10},{3,11},{4,12},{5,13},{6,14},{7,15},{8,0},{9,1},... | collective-permute-start | bytes 147464 | tf_op jit(solution)/shard_map/ppermute | solution.py:26
  105.6 4.6 %collective-permute-start.6 = (f32[1,48,128]{2,1,0:T(8,128)S(1)}, f32[1,48,128]{2,1,0:T(8,128)S(1)}, u32[]{:S(2)}, u32[]{:S(2)}) collective-permute-start(f32[1,48,128]{2,1,0:T(8,128)S(1)} %constant_dynamic-slice_fusion), channel_id=1, source_target_pairs={{0,16},{1,17},{2,18},{3,19},{4,20},{5,21},{6,22},{7,23},{8,24},{9,... | collective-permute-start | bytes 73736 | tf_op jit(solution)/shard_map/ppermute | solution.py:26

commit v3 on v1

v3 whole, which is shorter than its diff:
```python
import jax
import jax.numpy as jnp
from jax import lax
from jax.experimental import pallas as pl
from jax.experimental.pallas import tpu as pltpu
from jax.sharding import PartitionSpec as P

BOTH = ("ep", "edp")
GROUP = 16
CHUNKS = 4
HALVES = 2


def reduce_bucket(bucket):
    rows, width = bucket.shape
    members = lax.axis_size("edp")
    own = lax.axis_index("edp")
    part = bucket.reshape(members, rows * width // (members * 128), 128)
    stride = 1
    while stride < members:
        pairs = part.reshape(part.shape[0] // 2, 2, *part.shape[1:])
        bit = (own // stride) % 2
        kept = lax.dynamic_index_in_dim(pairs, bit, axis=1, keepdims=False)
        given = lax.dynamic_index_in_dim(pairs, 1 - bit, axis=1, keepdims=False)
        swap = [(i, i ^ stride) for i in range(members)]
        part = kept + lax.ppermute(given, "edp", swap)
        stride *= 2
    return part.reshape(1, rows // members, width)


def place(core, member, rest):
    across = rest * GROUP + member
    along = (member // 4) * 8 + rest * 4 + member % 4
    return across + core * (along - across)


def groups(members):
    return [
        [place(j % 2, g, r) * members + j for g in range(GROUP)]
        for j in range(members)
        for r in range(2)
    ]


def partners(members):
    return [
        (place(j % 2, g, r) * members + j, place(j % 2, g, 1 - r) * members + j)
        for j in range(members)
        for g in range(GROUP)
        for r in range(2)
    ]


def row_kernel(
    core_ref, gate_hbm, up_hbm, grad_hbm, w_gate_hbm, w_up_hbm, out_hbm,
    gate, up, grad, weight, packed, rows, in_sem, weight_sem, out_sem,
):
    core = core_ref[0]
    sources, capacity, hidden = gate.shape
    width = weight.shape[0]
    some, tile = sources // CHUNKS, width // HALVES
    arriving, loading, leaving = [], [], []
    for q in range(CHUNKS):
        part = pl.ds(q * some, some)
        for i, (here, there) in enumerate(((gate_hbm, gate), (up_hbm, up), (grad_hbm, grad))):
            arriving.append(pltpu.make_async_copy(here.at[part], there.at[part], in_sem.at[q, i]))
            arriving[-1].start()
    for n in range(HALVES):
        part = pl.ds(n * tile, tile)
        for i, here in enumerate((w_gate_hbm, w_up_hbm)):
            there = weight.at[part, pl.ds(i * hidden, hidden)]
            loading.append(pltpu.make_async_copy(here.at[part], there, weight_sem.at[n, i]))
            loading[-1].start()
    for q in range(CHUNKS):
        for i in range(3):
            arriving[3 * q + i].wait()
        for s in range(q * some, (q + 1) * some):
            gate_f = gate[s].astype(jnp.float32)
            up_f = up[s].astype(jnp.float32)
            grad_f = grad[s].astype(jnp.float32)
            sig = 0.5 + 0.5 * jnp.tanh(0.5 * gate_f)
            scaled = grad_f * sig
            across = s % GROUP * 2 + s // GROUP
            along = (s // 8 * 4 + s % 4) * 2 + s // 4 % 2
            position = jnp.where(core == 0, across, along)
            to = pl.ds(pl.multiple_of(position * capacity, capacity), capacity)
            packed[to, :hidden] = (scaled * up_f * (1.0 + gate_f * (1.0 - sig))).astype(jnp.bfloat16)
            packed[to, hidden:] = (scaled * gate_f).astype(jnp.bfloat16)
    for n in range(HALVES):
        part = pl.ds(n * tile, tile)
        loading[2 * n].wait()
        loading[2 * n + 1].wait()
        total = lax.dot_general(
            packed[...],
            weight[n * tile : (n + 1) * tile, :],
            (((1,), (1,)), ((), ())),
            preferred_element_type=jnp.float32,
        )
        rows[:, n * tile : (n + 1) * tile] = total.astype(jnp.bfloat16)
        leaving.append(pltpu.make_async_copy(rows.at[:, part], out_hbm.at[:, part], out_sem.at[n]))
        leaving[-1].start()
    for copy in leaving:
        copy.wait()


def send_rows(core, gate, up, grad, w_gate, w_up):
    sources, capacity, hidden = gate.shape
    width = w_gate.shape[0]
    anywhere = pl.BlockSpec(memory_space=pl.ANY)
    held = pltpu.VMEM((sources, capacity, hidden), jnp.bfloat16)
    return pl.pallas_call(
        row_kernel,
        in_specs=[pl.BlockSpec(memory_space=pltpu.SMEM)] + [anywhere] * 5,
        out_specs=anywhere,
        scratch_shapes=[
            held,
            held,
            held,
            pltpu.VMEM((width, 2 * hidden), jnp.bfloat16),
            pltpu.VMEM((sources * capacity, 2 * hidden), jnp.bfloat16),
            pltpu.VMEM((sources * capacity, width), jnp.bfloat16),
            pltpu.SemaphoreType.DMA((CHUNKS, 3)),
            pltpu.SemaphoreType.DMA((HALVES, 2)),
            pltpu.SemaphoreType.DMA((HALVES,)),
        ],
        out_shape=jax.ShapeDtypeStruct((sources * capacity, width), jnp.bfloat16),
        compiler_params=pltpu.CompilerParams(vmem_limit_bytes=60 * 1024 * 1024),
        cost_estimate=pl.CostEstimate(
            flops=4 * sources * capacity * hidden * width,
            bytes_accessed=6 * sources * capacity * hidden + 4 * hidden * width + 2 * sources * capacity * width,
            transcendentals=sources * capacity * hidden,
        ),
    )(core.reshape(1), gate, up, grad, w_gate, w_up)


def choice(routes, core, rest, capacity):
    tokens = routes.shape[1]
    named = place(core, jnp.arange(GROUP, dtype=jnp.int32), rest)
    matches = (routes[:, :, :, None] == named).any(axis=2)
    count = matches.astype(jnp.int32)
    earlier = jnp.cumsum(count, axis=1) - count
    slot = jnp.where(matches, earlier, -1).reshape(2 * tokens, GROUP).astype(jnp.bfloat16)
    column = jnp.arange(GROUP * 2 * capacity, dtype=jnp.int32)
    spread = column[None, :] // (2 * capacity) == jnp.arange(GROUP, dtype=jnp.int32)[:, None]
    slots = jnp.dot(slot, spread.astype(jnp.bfloat16), preferred_element_type=jnp.float32)
    second = jnp.arange(2 * tokens, dtype=jnp.int32)[:, None] // tokens
    owner = jnp.where(second == 0, 1 - rest, rest)
    same = owner == (column // capacity % 2)[None, :]
    chosen = same & (slots == (column % capacity).astype(jnp.float32)[None, :])
    return chosen.astype(jnp.bfloat16)


def shards(routes, gate_pre, up_pre, hidden_grad, w_gate, w_up, bucket_terms):
    members = lax.axis_size("edp")
    experts, capacity = gate_pre.shape[2:4]
    tokens = routes.shape[0]
    width = w_gate.shape[1]
    core = lax.axis_index("edp") % 2
    own = lax.axis_index("ep")
    rest = jnp.where(core == 0, own // GROUP, own // 4 % 2)
    swap = partners(members)
    rows = send_rows(core, gate_pre[0, 0], up_pre[0, 0], hidden_grad[0, 0], w_gate[0], w_up[0])
    arrived = lax.all_to_all(
        rows.reshape(GROUP, 2 * capacity, width),
        BOTH,
        split_axis=0,
        concat_axis=0,
        axis_index_groups=groups(members),
        tiled=True,
    ).reshape(experts * capacity, width)
    theirs = lax.ppermute(routes, BOTH, swap)
    chosen = choice(jnp.stack([theirs, routes]), core, rest, capacity)
    chosen = lax.optimization_barrier(chosen)
    given = jnp.dot(chosen[:tokens], arrived, preferred_element_type=jnp.float32)
    got = lax.ppermute(given.astype(jnp.bfloat16), BOTH, swap)
    kept = jnp.dot(chosen[tokens:], arrived, preferred_element_type=jnp.float32)
    token_grad = (kept + got.astype(jnp.float32)).astype(jnp.bfloat16)
    reduced = reduce_bucket(bucket_terms[0, 0])
    return (token_grad, reduced)


def solution(mesh):
    placed = (
        P(("ep", "edp"), None),
        P("ep", "edp", None, None, None),
        P("ep", "edp", None, None, None),
        P("ep", "edp", None, None, None),
        P("ep", None, None),
        P("ep", None, None),
        P("ep", "edp", None, None),
    )
    return jax.shard_map(
        shards,
        mesh=mesh,
        in_specs=placed,
        out_specs=(P(("ep", "edp"), None), P("ep", "edp", None)),
        check_vma=False,
    )
```

time: 107 us -> 109 us (1.019)
  the two profiles are of different devices: /device:TPU:190 before, /device:TPU:1 now
where the time goes in v3:
time: 109 us; the launch traced here: 108 us
  starting transfers between devices  46.7 us (43%)
  waiting for transfers between devices  46.4 us (43%)
  Pallas kernels  8.09 us (7%)
  local copies, waits for them, and re-layouts  2.15 us (2%)
  matrix products  1.85 us (2%)
  other arithmetic  1.33 us (1%)
  between operations  1.1 us (1%)
    ppermute x1, waiting for transfers between devices, shards(): theirs = lax.ppermute(routes, BOTH, swap)  35.9 us
    all_to_all x1, starting transfers between devices, shards(): lax.all_to_all(rows.reshape(GROUP, 2 * capacity, width), BOTH, split_axis...  19.8 us
    ppermute x5, starting transfers between devices, reduce_bucket(): part = kept + lax.ppermute(given, 'edp', swap)  13.4 us
    ppermute x1, starting transfers between devices, shards(): got = lax.ppermute(given.astype(jnp.bfloat16), BOTH, swap)  8.11 us
    pallas_call x1, Pallas kernels, send_rows(): pl.pallas_call(row_kernel, in_specs=[pl.BlockSpec(memory_space=pltpu.SMEM...  8.09 us
    ppermute x5, waiting for transfers between devices, reduce_bucket(): part = kept + lax.ppermute(given, 'edp', swap)  7.96 us
    ppermute x1, starting transfers between devices, shards(): theirs = lax.ppermute(routes, BOTH, swap)  5.42 us
    ppermute x1, waiting for transfers between devices, shards(): got = lax.ppermute(given.astype(jnp.bfloat16), BOTH, swap)  2.49 us
  transfers between devices with their start and end apart: 8, of which 4 were waited for; matrix products, arithmetic and copies ran while one was open for 4% of the time, Pallas kernels for 0%

profile of v3, /device:TPU:1, one launch (start us, length us, event | category | flops | bytes accessed | tf_op | source)
XLA Modules:
  0.0 107.6 jit_solution(1316872419391477798)
XLA Ops:
  0.6 8.1 %shard_map.86 = bf16[512,2048]{1,0:T(8,128)(2,1)} custom-call(s32[1]{0:T(128)} %bitcast.3.core_ref, bf16[32,16,768]{2,1,0:T(8,128)(2,1)} %bitcast.54, bf16[32,16,768]{2,1,0:T(8,128)(2,1)} %bitcast.55, bf16[32,16,768]{2,1,0:T(8,128)(2,1)} %bitcast.56, bf16[2048,768]{1,0:T(8,128)(2,1)} %bitcast.52, bf16[2048,768]{1,0:T(8,128)(2,1)} %bitcast.53), custom_call_target="tpu_custom_call" | custom-call | flops 3221225472 | bytes 10747904 | tf_op jit(solution)/shard_map/pallas_call | solution.py:111
  8.7 19.8 %all-to-all-start = ((bf16[16,32,2048]{2,1,0:T(8,128)(2,1)}), bf16[16,32,2048]{2,1,0:T(8,128)(2,1)S(1)}, u32[]{:S(2)}, u32[]{:S(2)}) async-start(bf16[16,32,2048]{2,1,0:T(8,128)(2,1)} %bitcast.42), calls=%async_computation | async-start | bytes 4194304 | tf_op jit(solution)/shard_map/all_to_all | solution.py:163
  28.6 0.0 copy-start
  28.6 1.2 %reshape_reshape_squeeze.3 = f32[16,2,48,128]{3,2,1,0:T(8,128)S(1)} reshape(f32[1,1,128,1536]{3,2,1,0:T(8,128)} %param.13) | data formatting | bytes 1572864 | tf_op jit(solution)/shard_map/reshape;reshape;squeeze | solution.py:21
  29.8 1.9 %collective-permute-start.2 = (f32[16,48,128]{2,1,0:T(8,128)S(1)}, f32[16,48,128]{2,1,0:T(8,128)}, u32[]{:S(2)}, u32[]{:S(2)}) collective-permute-start(f32[16,48,128]{2,1,0:T(8,128)S(1)} %dynamic-slice_bitcast_fusion), channel_id=1, source_target_pairs={{0,1},{1,0},{2,3},{3,2},{4,5},{5,4},{6,7},{7,6},{8,9},{9,8},{10,11... | collective-permute-start | bytes 1179656 | tf_op jit(solution)/shard_map/ppermute | solution.py:26
  31.7 0.0 copy-done
  31.7 5.4 %collective-permute-start = (s32[48,8]{0,1:T(8,128)S(1)}, s32[48,8]{0,1:T(8,128)S(1)}, u32[]{:S(2)}, u32[]{:S(2)}) collective-permute-start(s32[48,8]{0,1:T(8,128)S(1)} %copy-done), channel_id=1, source_target_pairs={{0,512},{512,0},{32,544},{544,32},{64,576},{576,64},{96,608},{608,... | collective-permute-start | bytes 4616 | tf_op jit(solution)/shard_map/ppermute | solution.py:171
  37.4 0.0 collective-permute-done.2
  37.4 1.1 bitcast_add_fusion
  38.5 2.9 %collective-permute-start.3 = (f32[8,48,128]{2,1,0:T(8,128)S(1)}, f32[8,48,128]{2,1,0:T(8,128)S(1)}, u32[]{:S(2)}, u32[]{:S(2)}) collective-permute-start(f32[8,48,128]{2,1,0:T(8,128)S(1)} %dynamic-slice_bitcast_fusion.1), channel_id=1, source_target_pairs={{0,2},{1,3},{2,0},{3,1},{4,6},{5,7},{6,4},{7,5},{8,10},{9,11},{10,... | collective-permute-start | bytes 589832 | tf_op jit(solution)/shard_map/ppermute | solution.py:26
  41.5 35.9 %collective-permute-done = s32[48,8]{0,1:T(8,128)S(1)} collective-permute-done((s32[48,8]{0,1:T(8,128)S(1)}, s32[48,8]{0,1:T(8,128)S(1)}, u32[]{:S(2)}, u32[]{:S(2)}) %collective-permute-start) | collective-permute-done | bytes 1568 | tf_op jit(solution)/shard_map/ppermute | solution.py:171
  77.4 0.0 collective-permute-done.3
  77.5 1.9 %collective-permute-start.4 = (f32[4,48,128]{2,1,0:T(8,128)S(1)}, f32[4,48,128]{2,1,0:T(8,128)S(1)}, u32[]{:S(2)}, u32[]{:S(2)}) collective-permute-start(f32[4,48,128]{2,1,0:T(8,128)S(1)} %dynamic-slice_bitcast_fusion.2), channel_id=1, source_target_pairs={{0,4},{1,5},{2,6},{3,7},{4,0},{5,1},{6,2},{7,3},{8,12},{9,13},{10,... | collective-permute-start | bytes 294920 | tf_op jit(solution)/shard_map/ppermute | solution.py:26
  79.4 0.1 compare_reduce_fusion
  79.5 0.1 reduce_or.12
  79.6 0.1 copy.19
  79.7 0.1 reduce_window_sum.13
  79.8 0.1 copy.20
  79.8 3.9 %collective-permute-done.4 = f32[4,48,128]{2,1,0:T(8,128)S(1)} collective-permute-done((f32[4,48,128]{2,1,0:T(8,128)S(1)}, f32[4,48,128]{2,1,0:T(8,128)S(1)}, u32[]{:S(2)}, u32[]{:S(2)}) %collective-permute-start.4) | collective-permute-done | bytes 98336 | tf_op jit(solution)/shard_map/ppermute | solution.py:26
  83.8 4.7 %collective-permute-start.5 = (f32[2,48,128]{2,1,0:T(8,128)S(1)}, f32[2,48,128]{2,1,0:T(8,128)S(1)}, u32[]{:S(2)}, u32[]{:S(2)}) collective-permute-start(f32[2,48,128]{2,1,0:T(8,128)S(1)} %dynamic-slice_bitcast_fusion.3), channel_id=1, source_target_pairs={{0,8},{1,9},{2,10},{3,11},{4,12},{5,13},{6,14},{7,15},{8,0},{9,1},... | collective-permute-start | bytes 147464 | tf_op jit(solution)/shard_map/ppermute | solution.py:26
  88.5 0.2 fusion.1
  88.7 4.0 %collective-permute-done.5 = f32[2,48,128]{2,1,0:T(8,128)S(1)} collective-permute-done((f32[2,48,128]{2,1,0:T(8,128)S(1)}, f32[2,48,128]{2,1,0:T(8,128)S(1)}, u32[]{:S(2)}, u32[]{:S(2)}) %collective-permute-start.5) | collective-permute-done | bytes 49184 | tf_op jit(solution)/shard_map/ppermute | solution.py:26
  92.8 1.9 %collective-permute-start.6 = (f32[1,48,128]{2,1,0:T(8,128)S(1)}, f32[1,48,128]{2,1,0:T(8,128)S(1)}, u32[]{:S(2)}, u32[]{:S(2)}) collective-permute-start(f32[1,48,128]{2,1,0:T(8,128)S(1)} %constant_dynamic-slice_fusion), channel_id=1, source_target_pairs={{0,16},{1,17},{2,18},{3,19},{4,20},{5,21},{6,22},{7,23},{8,24},{9,... | collective-permute-start | bytes 73736 | tf_op jit(solution)/shard_map/ppermute | solution.py:26
  94.7 0.0 all-to-all-done
  94.7 0.5 convolution_convert_fusion
  95.2 8.1 %collective-permute-start.1 = (bf16[48,2048]{1,0:T(8,128)(2,1)S(1)}, bf16[48,2048]{1,0:T(8,128)(2,1)S(1)}, u32[]{:S(2)}, u32[]{:S(2)}) collective-permute-start(bf16[48,2048]{1,0:T(8,128)(2,1)S(1)} %convolution_convert_fusion), channel_id=1, source_target_pairs={{0,512},{512,0},{32,544},{544,32},{64,576},{576,64},{96,608},{608,... | collective-permute-start | bytes 589832 | tf_op jit(solution)/shard_map/ppermute | solution.py:175
  103.3 0.0 collective-permute-done.6
  103.3 0.6 reshape.164
  104.0 2.5 %collective-permute-done.1 = bf16[48,2048]{1,0:T(8,128)(2,1)S(1)} collective-permute-done((bf16[48,2048]{1,0:T(8,128)(2,1)S(1)}, bf16[48,2048]{1,0:T(8,128)(2,1)S(1)}, u32[]{:S(2)}, u32[]{:S(2)}) %collective-permute-start.1) | collective-permute-done | bytes 196640 | tf_op jit(solution)/shard_map/ppermute | solution.py:175
  106.4 1.2 %add_convert_fusion = bf16[48,2048]{1,0:T(8,128)(2,1)} fusion(bf16[48,2048]{1,0:T(8,128)(2,1)S(1)} %collective-permute-done.1, bf16[512,2048]{1,0:T(8,128)(2,1)S(1)} %bitcast.41, bf16[96,512]{1,0:T(8,128)(2,1)S(1)} %fusion.1), kind=kOutput, calls=%fused_computation.6 | convolution fusion | flops 100958208 | bytes 2539520 | tf_op jit(solution)/shard_map/dot_general | solution.py:176
  (16 shorter events, 0.2 us)
Async XLA Ops:
  8.7 85.9 %all-to-all-start = ((bf16[16,32,2048]{2,1,0:T(8,128)(2,1)}), bf16[16,32,2048]{2,1,0:T(8,128)(2,1)S(1)}, u32[]{:S(2)}, u32[]{:S(2)}) async-start(bf16[16,32,2048]{2,1,0:T(8,128)(2,1)} %bitcast.42), calls=%async_computation | async-start | bytes 4194304 | tf_op jit(solution)/shard_map/all_to_all | solution.py:163
  28.6 3.2 %copy-start = (s32[48,8]{0,1:T(8,128)S(1)}, s32[48,8]{0,1:T(8,128)}, u32[]{:S(2)}) copy-start(s32[48,8]{0,1:T(8,128)} %param.7) | copy-start | bytes 4612
  29.8 7.5 %collective-permute-start.2 = (f32[16,48,128]{2,1,0:T(8,128)S(1)}, f32[16,48,128]{2,1,0:T(8,128)}, u32[]{:S(2)}, u32[]{:S(2)}) collective-permute-start(f32[16,48,128]{2,1,0:T(8,128)S(1)} %dynamic-slice_bitcast_fusion), channel_id=1, source_target_pairs={{0,1},{1,0},{2,3},{3,2},{4,5},{5,4},{6,7},{7,6},{8,9},{9,8},{10,11... | collective-permute-start | bytes 1179656 | tf_op jit(solution)/shard_map/ppermute | solution.py:26
  31.7 45.6 %collective-permute-start = (s32[48,8]{0,1:T(8,128)S(1)}, s32[48,8]{0,1:T(8,128)S(1)}, u32[]{:S(2)}, u32[]{:S(2)}) collective-permute-start(s32[48,8]{0,1:T(8,128)S(1)} %copy-done), channel_id=1, source_target_pairs={{0,512},{512,0},{32,544},{544,32},{64,576},{576,64},{96,608},{608,... | collective-permute-start | bytes 4616 | tf_op jit(solution)/shard_map/ppermute | solution.py:171
  38.5 39.0 %collective-permute-start.3 = (f32[8,48,128]{2,1,0:T(8,128)S(1)}, f32[8,48,128]{2,1,0:T(8,128)S(1)}, u32[]{:S(2)}, u32[]{:S(2)}) collective-permute-start(f32[8,48,128]{2,1,0:T(8,128)S(1)} %dynamic-slice_bitcast_fusion.1), channel_id=1, source_target_pairs={{0,2},{1,3},{2,0},{3,1},{4,6},{5,7},{6,4},{7,5},{8,10},{9,11},{10,... | collective-permute-start | bytes 589832 | tf_op jit(solution)/shard_map/ppermute | solution.py:26
  77.5 6.3 %collective-permute-start.4 = (f32[4,48,128]{2,1,0:T(8,128)S(1)}, f32[4,48,128]{2,1,0:T(8,128)S(1)}, u32[]{:S(2)}, u32[]{:S(2)}) collective-permute-start(f32[4,48,128]{2,1,0:T(8,128)S(1)} %dynamic-slice_bitcast_fusion.2), channel_id=1, source_target_pairs={{0,4},{1,5},{2,6},{3,7},{4,0},{5,1},{6,2},{7,3},{8,12},{9,13},{10,... | collective-permute-start | bytes 294920 | tf_op jit(solution)/shard_map/ppermute | solution.py:26
  83.8 9.0 %collective-permute-start.5 = (f32[2,48,128]{2,1,0:T(8,128)S(1)}, f32[2,48,128]{2,1,0:T(8,128)S(1)}, u32[]{:S(2)}, u32[]{:S(2)}) collective-permute-start(f32[2,48,128]{2,1,0:T(8,128)S(1)} %dynamic-slice_bitcast_fusion.3), channel_id=1, source_target_pairs={{0,8},{1,9},{2,10},{3,11},{4,12},{5,13},{6,14},{7,15},{8,0},{9,1},... | collective-permute-start | bytes 147464 | tf_op jit(solution)/shard_map/ppermute | solution.py:26
  92.8 10.5 %collective-permute-start.6 = (f32[1,48,128]{2,1,0:T(8,128)S(1)}, f32[1,48,128]{2,1,0:T(8,128)S(1)}, u32[]{:S(2)}, u32[]{:S(2)}) collective-permute-start(f32[1,48,128]{2,1,0:T(8,128)S(1)} %constant_dynamic-slice_fusion), channel_id=1, source_target_pairs={{0,16},{1,17},{2,18},{3,19},{4,20},{5,21},{6,22},{7,23},{8,24},{9,... | collective-permute-start | bytes 73736 | tf_op jit(solution)/shard_map/ppermute | solution.py:26
  95.2 11.3 %collective-permute-start.1 = (bf16[48,2048]{1,0:T(8,128)(2,1)S(1)}, bf16[48,2048]{1,0:T(8,128)(2,1)S(1)}, u32[]{:S(2)}, u32[]{:S(2)}) collective-permute-start(bf16[48,2048]{1,0:T(8,128)(2,1)S(1)} %convolution_convert_fusion), channel_id=1, source_target_pairs={{0,512},{512,0},{32,544},{544,32},{64,576},{576,64},{96,608},{608,... | collective-permute-start | bytes 589832 | tf_op jit(solution)/shard_map/ppermute | solution.py:175

commit v4 on v3

--- a/solution.py
+++ b/solution.py
@@ -160,6 +160,8 @@
     rest = jnp.where(core == 0, own // GROUP, own // 4 % 2)
     swap = partners(members)
     rows = send_rows(core, gate_pre[0, 0], up_pre[0, 0], hidden_grad[0, 0], w_gate[0], w_up[0])
+    theirs = lax.ppermute(routes, BOTH, swap)
+    rows, theirs = lax.optimization_barrier((rows, theirs))
     arrived = lax.all_to_all(
         rows.reshape(GROUP, 2 * capacity, width),
         BOTH,
@@ -168,7 +170,6 @@
         axis_index_groups=groups(members),
         tiled=True,
     ).reshape(experts * capacity, width)
-    theirs = lax.ppermute(routes, BOTH, swap)
     chosen = choice(jnp.stack([theirs, routes]), core, rest, capacity)
     chosen = lax.optimization_barrier(chosen)
     given = jnp.dot(chosen[:tokens], arrived, preferred_element_type=jnp.float32)

time: 109 us -> 102 us (0.936)
  the two profiles are of different devices: /device:TPU:1 before, /device:TPU:476 now
where the time goes in v4:
time: 102 us; the launch traced here: 101 us
  waiting for transfers between devices  50.2 us (49%)
  starting transfers between devices  37 us (36%)
  Pallas kernels  8.08 us (8%)
  local copies, waits for them, and re-layouts  2.88 us (3%)
  matrix products  1.84 us (2%)
  between operations  1.06 us (1%)
    all_to_all x1, waiting for transfers between devices, shards(): lax.all_to_all(rows.reshape(GROUP, 2 * capacity, width), BOTH, split_axis...  24.3 us
    ppermute x5, waiting for transfers between devices, reduce_bucket(): part = kept + lax.ppermute(given, 'edp', swap)  17 us
    ppermute x5, starting transfers between devices, reduce_bucket(): part = kept + lax.ppermute(given, 'edp', swap)  14.4 us
    ppermute x1, starting transfers between devices, shards(): theirs = lax.ppermute(routes, BOTH, swap)  11.9 us
    ppermute x1, waiting for transfers between devices, shards(): got = lax.ppermute(given.astype(jnp.bfloat16), BOTH, swap)  8.89 us
    all_to_all x1, starting transfers between devices, shards(): lax.all_to_all(rows.reshape(GROUP, 2 * capacity, width), BOTH, split_axis...  8.81 us
    pallas_call x1, Pallas kernels, send_rows(): pl.pallas_call(row_kernel, in_specs=[pl.BlockSpec(memory_space=pltpu.SMEM...  8.08 us
  transfers between devices with their start and end apart: 8, of which 6 were waited for; matrix products, arithmetic and copies ran while one was open for 4% of the time, Pallas kernels for 8%

profile of v4, /device:TPU:476, one launch (start us, length us, event | category | flops | bytes accessed | tf_op | source)
XLA Modules:
  0.0 101.4 jit_solution(1159601484682539371)
XLA Ops:
  0.6 11.9 %collective-permute-start = (s32[48,8]{0,1:T(8,128)}, s32[48,8]{0,1:T(8,128)S(1)}, u32[]{:S(2)}, u32[]{:S(2)}) collective-permute-start(s32[48,8]{0,1:T(8,128)} %param.7), channel_id=1, source_target_pairs={{0,512},{512,0},{32,544},{544,32},{64,576},{576,64},{96,608},{608,... | collective-permute-start | bytes 4616 | tf_op jit(solution)/shard_map/ppermute | solution.py:163
  12.5 8.1 %shard_map.86 = bf16[512,2048]{1,0:T(8,128)(2,1)} custom-call(s32[1]{0:T(128)} %bitcast.core_ref, bf16[32,16,768]{2,1,0:T(8,128)(2,1)} %bitcast.54, bf16[32,16,768]{2,1,0:T(8,128)(2,1)} %bitcast.55, bf16[32,16,768]{2,1,0:T(8,128)(2,1)} %bitcast.56, bf16[2048,768]{1,0:T(8,128)(2,1)} %bitcast.52, bf16[2048,768]{1,0:T(8,128)(2,1)} %bitcast.53), custom_call_target="tpu_custom_call" | custom-call | flops 3221225472 | bytes 10747904 | tf_op jit(solution)/shard_map/pallas_call | solution.py:111
  20.6 0.0 collective-permute-done
  20.6 8.8 %all-to-all-start = ((bf16[16,32,2048]{2,1,0:T(8,128)(2,1)}), bf16[16,32,2048]{2,1,0:T(8,128)(2,1)S(1)}, u32[]{:S(2)}, u32[]{:S(2)}) async-start(bf16[16,32,2048]{2,1,0:T(8,128)(2,1)} %bitcast.42), calls=%async_computation | async-start | bytes 4194304 | tf_op jit(solution)/shard_map/all_to_all | solution.py:165
  29.4 0.0 copy-start
  29.4 1.2 %reshape_reshape_squeeze.3 = f32[16,2,48,128]{3,2,1,0:T(8,128)S(1)} reshape(f32[1,1,128,1536]{3,2,1,0:T(8,128)} %param.13) | data formatting | bytes 1572864 | tf_op jit(solution)/shard_map/reshape;reshape;squeeze | solution.py:21
  30.6 0.8 dynamic-slice_bitcast_fusion
  31.4 1.9 %collective-permute-start.2 = (f32[16,48,128]{2,1,0:T(8,128)}, f32[16,48,128]{2,1,0:T(8,128)S(1)}, u32[]{:S(2)}, u32[]{:S(2)}) collective-permute-start(f32[16,48,128]{2,1,0:T(8,128)} %dynamic-slice_bitcast_fusion), channel_id=1, source_target_pairs={{0,1},{1,0},{2,3},{3,2},{4,5},{5,4},{6,7},{7,6},{8,9},{9,8},{10,11... | collective-permute-start | bytes 1179656 | tf_op jit(solution)/shard_map/ppermute | solution.py:26
  33.5 1.7 %collective-permute-done.2 = f32[16,48,128]{2,1,0:T(8,128)S(1)} collective-permute-done((f32[16,48,128]{2,1,0:T(8,128)}, f32[16,48,128]{2,1,0:T(8,128)S(1)}, u32[]{:S(2)}, u32[]{:S(2)}) %collective-permute-start.2) | collective-permute-done | bytes 393248 | tf_op jit(solution)/shard_map/ppermute | solution.py:26
  35.3 2.5 %collective-permute-start.3 = (f32[8,48,128]{2,1,0:T(8,128)S(1)}, f32[8,48,128]{2,1,0:T(8,128)S(1)}, u32[]{:S(2)}, u32[]{:S(2)}) collective-permute-start(f32[8,48,128]{2,1,0:T(8,128)S(1)} %dynamic-slice_bitcast_fusion.1), channel_id=1, source_target_pairs={{0,2},{1,3},{2,0},{3,1},{4,6},{5,7},{6,4},{7,5},{8,10},{9,11},{10,... | collective-permute-start | bytes 589832 | tf_op jit(solution)/shard_map/ppermute | solution.py:26
  37.8 0.0 copy-done
  37.8 6.3 %collective-permute-done.3 = f32[8,48,128]{2,1,0:T(8,128)S(1)} collective-permute-done((f32[8,48,128]{2,1,0:T(8,128)S(1)}, f32[8,48,128]{2,1,0:T(8,128)S(1)}, u32[]{:S(2)}, u32[]{:S(2)}) %collective-permute-start.3) | collective-permute-done | bytes 196640 | tf_op jit(solution)/shard_map/ppermute | solution.py:26
  44.2 4.2 %collective-permute-start.4 = (f32[4,48,128]{2,1,0:T(8,128)S(1)}, f32[4,48,128]{2,1,0:T(8,128)S(1)}, u32[]{:S(2)}, u32[]{:S(2)}) collective-permute-start(f32[4,48,128]{2,1,0:T(8,128)S(1)} %dynamic-slice_bitcast_fusion.2), channel_id=1, source_target_pairs={{0,4},{1,5},{2,6},{3,7},{4,0},{5,1},{6,2},{7,3},{8,12},{9,13},{10,... | collective-permute-start | bytes 294920 | tf_op jit(solution)/shard_map/ppermute | solution.py:26
  48.4 0.1 compare_reduce_fusion
  48.6 0.1 reduce_or.12
  48.6 0.1 copy.19
  48.7 0.1 reduce_window_sum.13
  48.8 0.1 copy.20
  48.9 3.2 %collective-permute-done.4 = f32[4,48,128]{2,1,0:T(8,128)S(1)} collective-permute-done((f32[4,48,128]{2,1,0:T(8,128)S(1)}, f32[4,48,128]{2,1,0:T(8,128)S(1)}, u32[]{:S(2)}, u32[]{:S(2)}) %collective-permute-start.4) | collective-permute-done | bytes 98336 | tf_op jit(solution)/shard_map/ppermute | solution.py:26
  52.1 3.8 %collective-permute-start.5 = (f32[2,48,128]{2,1,0:T(8,128)S(1)}, f32[2,48,128]{2,1,0:T(8,128)S(1)}, u32[]{:S(2)}, u32[]{:S(2)}) collective-permute-start(f32[2,48,128]{2,1,0:T(8,128)S(1)} %dynamic-slice_bitcast_fusion.3), channel_id=1, source_target_pairs={{0,8},{1,9},{2,10},{3,11},{4,12},{5,13},{6,14},{7,15},{8,0},{9,1},... | collective-permute-start | bytes 147464 | tf_op jit(solution)/shard_map/ppermute | solution.py:26
  55.9 0.2 fusion.1
  56.1 5.8 %collective-permute-done.5 = f32[2,48,128]{2,1,0:T(8,128)S(1)} collective-permute-done((f32[2,48,128]{2,1,0:T(8,128)S(1)}, f32[2,48,128]{2,1,0:T(8,128)S(1)}, u32[]{:S(2)}, u32[]{:S(2)}) %collective-permute-start.5) | collective-permute-done | bytes 49184 | tf_op jit(solution)/shard_map/ppermute | solution.py:26
  62.0 1.9 %collective-permute-start.6 = (f32[1,48,128]{2,1,0:T(8,128)S(1)}, f32[1,48,128]{2,1,0:T(8,128)S(1)}, u32[]{:S(2)}, u32[]{:S(2)}) collective-permute-start(f32[1,48,128]{2,1,0:T(8,128)S(1)} %constant_dynamic-slice_fusion), channel_id=1, source_target_pairs={{0,16},{1,17},{2,18},{3,19},{4,20},{5,21},{6,22},{7,23},{8,24},{9,... | collective-permute-start | bytes 73736 | tf_op jit(solution)/shard_map/ppermute | solution.py:26
  63.9 24.3 %all-to-all-done = bf16[16,32,2048]{2,1,0:T(8,128)(2,1)S(1)} async-done(((bf16[16,32,2048]{2,1,0:T(8,128)(2,1)}), bf16[16,32,2048]{2,1,0:T(8,128)(2,1)S(1)}, u32[]{:S(2)}, u32[]{:S(2)}) %all-to-all-start) | async-done | bytes 2097184 | tf_op jit(solution)/shard_map/all_to_all | solution.py:165
  88.3 0.5 convolution_convert_fusion
  88.8 1.9 %collective-permute-start.1 = (bf16[48,2048]{1,0:T(8,128)(2,1)S(1)}, bf16[48,2048]{1,0:T(8,128)(2,1)S(1)}, u32[]{:S(2)}, u32[]{:S(2)}) collective-permute-start(bf16[48,2048]{1,0:T(8,128)(2,1)S(1)} %convolution_convert_fusion), channel_id=1, source_target_pairs={{0,512},{512,0},{32,544},{544,32},{64,576},{576,64},{96,608},{608,... | collective-permute-start | bytes 589832 | tf_op jit(solution)/shard_map/ppermute | solution.py:176
  90.7 0.0 collective-permute-done.6
  90.7 0.6 reshape.164
  91.3 8.9 %collective-permute-done.1 = bf16[48,2048]{1,0:T(8,128)(2,1)S(1)} collective-permute-done((bf16[48,2048]{1,0:T(8,128)(2,1)S(1)}, bf16[48,2048]{1,0:T(8,128)(2,1)S(1)}, u32[]{:S(2)}, u32[]{:S(2)}) %collective-permute-start.1) | collective-permute-done | bytes 196640 | tf_op jit(solution)/shard_map/ppermute | solution.py:176
  100.2 1.2 %add_convert_fusion = bf16[48,2048]{1,0:T(8,128)(2,1)} fusion(bf16[48,2048]{1,0:T(8,128)(2,1)S(1)} %collective-permute-done.1, bf16[512,2048]{1,0:T(8,128)(2,1)S(1)} %bitcast.41, bf16[96,512]{1,0:T(8,128)(2,1)S(1)} %fusion.1), kind=kOutput, calls=%fused_computation.6 | convolution fusion | flops 100958208 | bytes 2539520 | tf_op jit(solution)/shard_map/dot_general | solution.py:177
  (16 shorter events, 0.2 us)
Async XLA Ops:
  0.6 20.0 %collective-permute-start = (s32[48,8]{0,1:T(8,128)}, s32[48,8]{0,1:T(8,128)S(1)}, u32[]{:S(2)}, u32[]{:S(2)}) collective-permute-start(s32[48,8]{0,1:T(8,128)} %param.7), channel_id=1, source_target_pairs={{0,512},{512,0},{32,544},{544,32},{64,576},{576,64},{96,608},{608,... | collective-permute-start | bytes 4616 | tf_op jit(solution)/shard_map/ppermute | solution.py:163
  20.6 67.7 %all-to-all-start = ((bf16[16,32,2048]{2,1,0:T(8,128)(2,1)}), bf16[16,32,2048]{2,1,0:T(8,128)(2,1)S(1)}, u32[]{:S(2)}, u32[]{:S(2)}) async-start(bf16[16,32,2048]{2,1,0:T(8,128)(2,1)} %bitcast.42), calls=%async_computation | async-start | bytes 4194304 | tf_op jit(solution)/shard_map/all_to_all | solution.py:165
  29.4 8.4 %copy-start = (s32[48,8]{0,1:T(8,128)S(1)}, s32[48,8]{0,1:T(8,128)}, u32[]{:S(2)}) copy-start(s32[48,8]{0,1:T(8,128)} %param.7) | copy-start | bytes 4612
  31.4 3.8 %collective-permute-start.2 = (f32[16,48,128]{2,1,0:T(8,128)}, f32[16,48,128]{2,1,0:T(8,128)S(1)}, u32[]{:S(2)}, u32[]{:S(2)}) collective-permute-start(f32[16,48,128]{2,1,0:T(8,128)} %dynamic-slice_bitcast_fusion), channel_id=1, source_target_pairs={{0,1},{1,0},{2,3},{3,2},{4,5},{5,4},{6,7},{7,6},{8,9},{9,8},{10,11... | collective-permute-start | bytes 1179656 | tf_op jit(solution)/shard_map/ppermute | solution.py:26
  35.3 8.9 %collective-permute-start.3 = (f32[8,48,128]{2,1,0:T(8,128)S(1)}, f32[8,48,128]{2,1,0:T(8,128)S(1)}, u32[]{:S(2)}, u32[]{:S(2)}) collective-permute-start(f32[8,48,128]{2,1,0:T(8,128)S(1)} %dynamic-slice_bitcast_fusion.1), channel_id=1, source_target_pairs={{0,2},{1,3},{2,0},{3,1},{4,6},{5,7},{6,4},{7,5},{8,10},{9,11},{10,... | collective-permute-start | bytes 589832 | tf_op jit(solution)/shard_map/ppermute | solution.py:26
  44.2 7.8 %collective-permute-start.4 = (f32[4,48,128]{2,1,0:T(8,128)S(1)}, f32[4,48,128]{2,1,0:T(8,128)S(1)}, u32[]{:S(2)}, u32[]{:S(2)}) collective-permute-start(f32[4,48,128]{2,1,0:T(8,128)S(1)} %dynamic-slice_bitcast_fusion.2), channel_id=1, source_target_pairs={{0,4},{1,5},{2,6},{3,7},{4,0},{5,1},{6,2},{7,3},{8,12},{9,13},{10,... | collective-permute-start | bytes 294920 | tf_op jit(solution)/shard_map/ppermute | solution.py:26
  52.1 9.9 %collective-permute-start.5 = (f32[2,48,128]{2,1,0:T(8,128)S(1)}, f32[2,48,128]{2,1,0:T(8,128)S(1)}, u32[]{:S(2)}, u32[]{:S(2)}) collective-permute-start(f32[2,48,128]{2,1,0:T(8,128)S(1)} %dynamic-slice_bitcast_fusion.3), channel_id=1, source_target_pairs={{0,8},{1,9},{2,10},{3,11},{4,12},{5,13},{6,14},{7,15},{8,0},{9,1},... | collective-permute-start | bytes 147464 | tf_op jit(solution)/shard_map/ppermute | solution.py:26
  62.0 28.7 %collective-permute-start.6 = (f32[1,48,128]{2,1,0:T(8,128)S(1)}, f32[1,48,128]{2,1,0:T(8,128)S(1)}, u32[]{:S(2)}, u32[]{:S(2)}) collective-permute-start(f32[1,48,128]{2,1,0:T(8,128)S(1)} %constant_dynamic-slice_fusion), channel_id=1, source_target_pairs={{0,16},{1,17},{2,18},{3,19},{4,20},{5,21},{6,22},{7,23},{8,24},{9,... | collective-permute-start | bytes 73736 | tf_op jit(solution)/shard_map/ppermute | solution.py:26
  88.8 11.5 %collective-permute-start.1 = (bf16[48,2048]{1,0:T(8,128)(2,1)S(1)}, bf16[48,2048]{1,0:T(8,128)(2,1)S(1)}, u32[]{:S(2)}, u32[]{:S(2)}) collective-permute-start(bf16[48,2048]{1,0:T(8,128)(2,1)S(1)} %convolution_convert_fusion), channel_id=1, source_target_pairs={{0,512},{512,0},{32,544},{544,32},{64,576},{576,64},{96,608},{608,... | collective-permute-start | bytes 589832 | tf_op jit(solution)/shard_map/ppermute | solution.py:176

commit v5 on v3

v5 whole, which is shorter than its diff:
```python
import jax
import jax.numpy as jnp
from jax import lax
from jax.experimental import pallas as pl
from jax.experimental.pallas import tpu as pltpu
from jax.sharding import PartitionSpec as P

BOTH = ("ep", "edp")
GROUP = 16
CHUNKS = 4
HALVES = 2


def halve(part, stride):
    members = lax.axis_size("edp")
    pairs = part.reshape(part.shape[0] // 2, 2, *part.shape[1:])
    bit = (lax.axis_index("edp") // stride) % 2
    kept = lax.dynamic_index_in_dim(pairs, bit, axis=1, keepdims=False)
    given = lax.dynamic_index_in_dim(pairs, 1 - bit, axis=1, keepdims=False)
    return kept + lax.ppermute(given, "edp", [(i, i ^ stride) for i in range(members)])


def place(core, member, rest):
    across = rest * GROUP + member
    along = (member // 4) * 8 + rest * 4 + member % 4
    return across + core * (along - across)


def groups(members):
    return [
        [place(j % 2, g, r) * members + j for g in range(GROUP)]
        for j in range(members)
        for r in range(2)
    ]


def partners(members):
    return [
        (place(j % 2, g, r) * members + j, place(j % 2, g, 1 - r) * members + j)
        for j in range(members)
        for g in range(GROUP)
        for r in range(2)
    ]


def row_kernel(
    where_ref, gate_hbm, up_hbm, grad_hbm, w_gate_hbm, w_up_hbm, out_hbm,
    gate, up, grad, weight, packed, rows, in_sem, weight_sem, out_sem,
):
    core, rest = where_ref[0], where_ref[1]
    sources, capacity, hidden = gate.shape
    width = weight.shape[0]
    some, tile = sources // CHUNKS, width // HALVES
    arriving, loading, leaving = [], [], []
    for q in range(CHUNKS):
        first = pl.ds(place(core, q * some, rest), some)
        part = pl.ds(q * some, some)
        for i, (here, there) in enumerate(((gate_hbm, gate), (up_hbm, up), (grad_hbm, grad))):
            arriving.append(pltpu.make_async_copy(here.at[first], there.at[part], in_sem.at[q, i]))
            arriving[-1].start()
    for n in range(HALVES):
        part = pl.ds(n * tile, tile)
        for i, here in enumerate((w_gate_hbm, w_up_hbm)):
            there = weight.at[part, pl.ds(i * hidden, hidden)]
            loading.append(pltpu.make_async_copy(here.at[part], there, weight_sem.at[n, i]))
            loading[-1].start()
    for q in range(CHUNKS):
        for i in range(3):
            arriving[3 * q + i].wait()
        for s in range(q * some, (q + 1) * some):
            gate_f = gate[s].astype(jnp.float32)
            up_f = up[s].astype(jnp.float32)
            grad_f = grad[s].astype(jnp.float32)
            sig = 0.5 + 0.5 * jnp.tanh(0.5 * gate_f)
            scaled = grad_f * sig
            to = pl.ds(s * capacity, capacity)
            packed[to, :hidden] = (scaled * up_f * (1.0 + gate_f * (1.0 - sig))).astype(jnp.bfloat16)
            packed[to, hidden:] = (scaled * gate_f).astype(jnp.bfloat16)
    for n in range(HALVES):
        part = pl.ds(n * tile, tile)
        loading[2 * n].wait()
        loading[2 * n + 1].wait()
        total = lax.dot_general(
            packed[...],
            weight[n * tile : (n + 1) * tile, :],
            (((1,), (1,)), ((), ())),
            preferred_element_type=jnp.float32,
        )
        rows[:, n * tile : (n + 1) * tile] = total.astype(jnp.bfloat16)
        leaving.append(pltpu.make_async_copy(rows.at[:, part], out_hbm.at[:, part], out_sem.at[n]))
        leaving[-1].start()
    for copy in leaving:
        copy.wait()


def send_rows(core, rest, gate, up, grad, w_gate, w_up):
    capacity, hidden = gate.shape[1:]
    width = w_gate.shape[0]
    anywhere = pl.BlockSpec(memory_space=pl.ANY)
    held = pltpu.VMEM((GROUP, capacity, hidden), jnp.bfloat16)
    return pl.pallas_call(
        row_kernel,
        in_specs=[pl.BlockSpec(memory_space=pltpu.SMEM)] + [anywhere] * 5,
        out_specs=anywhere,
        scratch_shapes=[
            held,
            held,
            held,
            pltpu.VMEM((width, 2 * hidden), jnp.bfloat16),
            pltpu.VMEM((GROUP * capacity, 2 * hidden), jnp.bfloat16),
            pltpu.VMEM((GROUP * capacity, width), jnp.bfloat16),
            pltpu.SemaphoreType.DMA((CHUNKS, 3)),
            pltpu.SemaphoreType.DMA((HALVES, 2)),
            pltpu.SemaphoreType.DMA((HALVES,)),
        ],
        out_shape=jax.ShapeDtypeStruct((GROUP * capacity, width), jnp.bfloat16),
        compiler_params=pltpu.CompilerParams(vmem_limit_bytes=58 * 1024 * 1024),
        cost_estimate=pl.CostEstimate(
            flops=4 * GROUP * capacity * hidden * width,
            bytes_accessed=6 * GROUP * capacity * hidden + 4 * hidden * width + 2 * GROUP * capacity * width,
            transcendentals=GROUP * capacity * hidden,
        ),
    )(jnp.stack([core, rest]), gate, up, grad, w_gate, w_up)


def choice(routes, core, rest, capacity):
    named = place(core, jnp.arange(GROUP, dtype=jnp.int32), rest)
    matches = (routes[:, :, None] == named).any(axis=1)
    count = matches.astype(jnp.int32)
    earlier = jnp.cumsum(count, axis=0) - count
    slot = jnp.where(matches, earlier, -1).astype(jnp.bfloat16)
    column = jnp.arange(GROUP * capacity, dtype=jnp.int32)
    spread = column[None, :] // capacity == jnp.arange(GROUP, dtype=jnp.int32)[:, None]
    slots = jnp.dot(slot, spread.astype(jnp.bfloat16), preferred_element_type=jnp.float32)
    return (slots == (column % capacity).astype(jnp.float32)[None, :]).astype(jnp.bfloat16)


def shards(routes, gate_pre, up_pre, hidden_grad, w_gate, w_up, bucket_terms):
    members = lax.axis_size("edp")
    capacity = gate_pre.shape[3]
    width = w_gate.shape[1]
    core = lax.axis_index("edp") % 2
    own = lax.axis_index("ep")
    rest = jnp.where(core == 0, own // GROUP, own // 4 % 2)
    swap = partners(members)
    saved = (gate_pre[0, 0], up_pre[0, 0], hidden_grad[0, 0], w_gate[0], w_up[0])

    def exchange(rows):
        return lax.all_to_all(
            rows.reshape(GROUP, capacity, width),
            BOTH,
            split_axis=0,
            concat_axis=0,
            axis_index_groups=groups(members),
            tiled=True,
        ).reshape(GROUP * capacity, width)

    theirs = lax.ppermute(routes, BOTH, swap)
    passed_on = send_rows(core, 1 - rest, *saved)
    passed_on, theirs = lax.optimization_barrier((passed_on, theirs))
    arrived = exchange(passed_on)
    own_rows = send_rows(core, rest, *saved)
    bucket = bucket_terms[0, 0]
    part = bucket.reshape(members, bucket.size // (members * 128), 128)
    part = halve(halve(part, 1), 2)
    chosen, mine, _ = lax.optimization_barrier(
        (choice(theirs, core, rest, capacity), choice(routes, core, rest, capacity), part)
    )
    given = jnp.dot(chosen, arrived, preferred_element_type=jnp.float32).astype(jnp.bfloat16)
    own_rows, given, part = lax.optimization_barrier((own_rows, given, part))
    got = lax.ppermute(given, BOTH, swap)
    kept = jnp.dot(mine, exchange(own_rows), preferred_element_type=jnp.float32)
    token_grad = (kept + got.astype(jnp.float32)).astype(jnp.bfloat16)
    part = halve(halve(halve(part, 4), 8), 16)
    reduced = part.reshape(1, bucket.shape[0] // members, bucket.shape[1])
    return (token_grad, reduced)


def solution(mesh):
    placed = (
        P(("ep", "edp"), None),
        P("ep", "edp", None, None, None),
        P("ep", "edp", None, None, None),
        P("ep", "edp", None, None, None),
        P("ep", None, None),
        P("ep", None, None),
        P("ep", "edp", None, None),
    )
    return jax.shard_map(
        shards,
        mesh=mesh,
        in_specs=placed,
        out_specs=(P(("ep", "edp"), None), P("ep", "edp", None)),
        check_vma=False,
    )
```

time: 109 us -> 104 us (0.954)
  the two profiles are of different devices: /device:TPU:1 before, /device:TPU:6 now
where the time goes in v5:
time: 104 us; the launch traced here: 103 us
  starting transfers between devices  53.8 us (52%)
  waiting for transfers between devices  31.1 us (30%)
  Pallas kernels  13.2 us (13%)
  other arithmetic  1.58 us (2%)
  matrix products  1.53 us (1%)
  between operations  1.09 us (1%)
    ppermute x5, waiting for transfers between devices, halve(): lax.ppermute(given, 'edp', [(i, i ^ stride) for i in range(members)])  19.4 us
    ppermute x5, starting transfers between devices, halve(): lax.ppermute(given, 'edp', [(i, i ^ stride) for i in range(members)])  15.9 us
    all_to_all x2, starting transfers between devices, exchange(): lax.all_to_all(rows.reshape(GROUP, capacity, width), BOTH, split_axis=0,...  15.3 us
    ppermute x1, starting transfers between devices, shards(): theirs = lax.ppermute(routes, BOTH, swap)  14.6 us
    pallas_call x2, Pallas kernels, send_rows(): pl.pallas_call(row_kernel, in_specs=[pl.BlockSpec(memory_space=pltpu.SMEM...  13.2 us
    ppermute x1, starting transfers between devices, shards(): got = lax.ppermute(given, BOTH, swap)  8.05 us
    all_to_all x2, waiting for transfers between devices, exchange(): lax.all_to_all(rows.reshape(GROUP, capacity, width), BOTH, split_axis=0,...  7.25 us
    ppermute x1, waiting for transfers between devices, shards(): got = lax.ppermute(given, BOTH, swap)  4.46 us
  transfers between devices with their start and end apart: 9, of which 5 were waited for; matrix products, arithmetic and copies ran while one was open for 3% of the time, Pallas kernels for 13%

profile of v5, /device:TPU:6, one launch (start us, length us, event | category | flops | bytes accessed | tf_op | source)
XLA Modules:
  0.0 103.4 jit_solution(2667979278690262667)
XLA Ops:
  0.6 14.6 %collective-permute-start = (s32[48,8]{0,1:T(8,128)}, s32[48,8]{0,1:T(8,128)S(1)}, u32[]{:S(2)}, u32[]{:S(2)}) collective-permute-start(s32[48,8]{0,1:T(8,128)} %param.7), channel_id=1, source_target_pairs={{0,512},{512,0},{32,544},{544,32},{64,576},{576,64},{96,608},{608,... | collective-permute-start | bytes 4616 | tf_op jit(solution)/shard_map/ppermute | solution.py:158
  15.2 0.6 pad_add_fusion.where_ref
  15.8 6.6 %shard_map.86 = bf16[256,2048]{1,0:T(8,128)(2,1)} custom-call(s32[2]{0:T(128)} %pad_add_fusion.where_ref, bf16[32,16,768]{2,1,0:T(8,128)(2,1)} %bitcast.48, bf16[32,16,768]{2,1,0:T(8,128)(2,1)} %bitcast.50, bf16[32,16,768]{2,1,0:T(8,128)(2,1)} %bitcast.52, bf16[2048,768]{1,0:T(8,128)(2,1)} %bitcast.41, bf16[2048,768]{1,0:T(8,128)(2,1)} %bitcast.43), custom_call_target="tpu_custom_call" | custom-call | flops 1610612736 | bytes 8519680 | tf_op jit(solution)/shard_map/pallas_call | solution.py:101
  22.4 0.0 collective-permute-done
  22.4 11.3 %all-to-all-start = ((bf16[16,16,2048]{2,1,0:T(8,128)(2,1)}), bf16[16,16,2048]{2,1,0:T(8,128)(2,1)S(1)}, u32[]{:S(2)}, u32[]{:S(2)}) async-start(bf16[16,16,2048]{2,1,0:T(8,128)(2,1)} %bitcast.45), calls=%async_computation | async-start | bytes 2097152 | tf_op jit(solution)/shard_map/all_to_all | solution.py:149
  33.8 0.1 reshape_reshape_squeeze.3
  33.9 1.9 %collective-permute-start.1 = (f32[16,48,128]{2,1,0:T(8,128)S(1)}, f32[16,48,128]{2,1,0:T(8,128)S(1)}, u32[]{:S(2)}, u32[]{:S(2)}) collective-permute-start(f32[16,48,128]{2,1,0:T(8,128)S(1)} %dynamic-slice_bitcast_fusion), channel_id=1, source_target_pairs={{0,1},{1,0},{2,3},{3,2},{4,5},{5,4},{6,7},{7,6},{8,9},{9,8},{10,11... | collective-permute-start | bytes 1179656 | tf_op jit(solution)/shard_map/ppermute | solution.py:20
  35.8 0.6 pad_add_fusion.1.where_ref
  36.5 6.6 %shard_map.87 = bf16[256,2048]{1,0:T(8,128)(2,1)} custom-call(s32[2]{0:T(128)} %pad_add_fusion.1.where_ref, bf16[32,16,768]{2,1,0:T(8,128)(2,1)} %bitcast.49, bf16[32,16,768]{2,1,0:T(8,128)(2,1)} %bitcast.51, bf16[32,16,768]{2,1,0:T(8,128)(2,1)} %bitcast.53, bf16[2048,768]{1,0:T(8,128)(2,1)} %bitcast.42, bf16[2048,768]{1,0:T(8,128)(2,1)} %bitcast.44), custom_call_target="tpu_custom_call" | custom-call | flops 1610612736 | bytes 8519680 | tf_op jit(solution)/shard_map/pallas_call | solution.py:101
  43.1 0.1 compare_reduce_fusion
  43.2 0.1 copy.22
  43.4 0.1 reduce_window_sum.18
  43.4 0.1 copy.20
  43.5 0.1 reduce_window_sum.17
  43.6 0.1 fusion.2
  43.7 0.0 collective-permute-done.1
  43.8 2.4 %collective-permute-start.2 = (f32[8,48,128]{2,1,0:T(8,128)S(1)}, f32[8,48,128]{2,1,0:T(8,128)S(1)}, u32[]{:S(2)}, u32[]{:S(2)}) collective-permute-start(f32[8,48,128]{2,1,0:T(8,128)S(1)} %dynamic-slice_bitcast_fusion.1), channel_id=1, source_target_pairs={{0,2},{1,3},{2,0},{3,1},{4,6},{5,7},{6,4},{7,5},{8,10},{9,11},{10,... | collective-permute-start | bytes 589832 | tf_op jit(solution)/shard_map/ppermute | solution.py:20
  46.3 0.1 fusion.1
  46.4 6.6 %collective-permute-done.2 = f32[8,48,128]{2,1,0:T(8,128)S(1)} collective-permute-done((f32[8,48,128]{2,1,0:T(8,128)S(1)}, f32[8,48,128]{2,1,0:T(8,128)S(1)}, u32[]{:S(2)}, u32[]{:S(2)}) %collective-permute-start.2) | collective-permute-done | bytes 196640 | tf_op jit(solution)/shard_map/ppermute | solution.py:20
  53.1 7.3 %all-to-all-done = bf16[16,16,2048]{2,1,0:T(8,128)(2,1)S(1)} async-done(((bf16[16,16,2048]{2,1,0:T(8,128)(2,1)}), bf16[16,16,2048]{2,1,0:T(8,128)(2,1)S(1)}, u32[]{:S(2)}, u32[]{:S(2)}) %all-to-all-start) | async-done | bytes 1048608 | tf_op jit(solution)/shard_map/all_to_all | solution.py:149
  60.3 0.3 convolution_convert_fusion
  60.6 4.0 %all-to-all-start.1 = ((bf16[16,16,2048]{2,1,0:T(8,128)(2,1)}), bf16[16,16,2048]{2,1,0:T(8,128)(2,1)S(1)}, u32[]{:S(2)}, u32[]{:S(2)}) async-start(bf16[16,16,2048]{2,1,0:T(8,128)(2,1)} %bitcast.15), calls=%async_computation.1 | async-start | bytes 2097152 | tf_op jit(solution)/shard_map/all_to_all | solution.py:149
  64.7 2.4 %collective-permute-start.4 = (f32[4,48,128]{2,1,0:T(8,128)S(1)}, f32[4,48,128]{2,1,0:T(8,128)S(1)}, u32[]{:S(2)}, u32[]{:S(2)}) collective-permute-start(f32[4,48,128]{2,1,0:T(8,128)S(1)} %dynamic-slice_bitcast_fusion.2), channel_id=1, source_target_pairs={{0,4},{1,5},{2,6},{3,7},{4,0},{5,1},{6,2},{7,3},{8,12},{9,13},{10,... | collective-permute-start | bytes 294920 | tf_op jit(solution)/shard_map/ppermute | solution.py:20
  67.2 7.2 %collective-permute-done.4 = f32[4,48,128]{2,1,0:T(8,128)S(1)} collective-permute-done((f32[4,48,128]{2,1,0:T(8,128)S(1)}, f32[4,48,128]{2,1,0:T(8,128)S(1)}, u32[]{:S(2)}, u32[]{:S(2)}) %collective-permute-start.4) | collective-permute-done | bytes 98336 | tf_op jit(solution)/shard_map/ppermute | solution.py:20
  74.4 4.7 %collective-permute-start.5 = (f32[2,48,128]{2,1,0:T(8,128)S(1)}, f32[2,48,128]{2,1,0:T(8,128)S(1)}, u32[]{:S(2)}, u32[]{:S(2)}) collective-permute-start(f32[2,48,128]{2,1,0:T(8,128)S(1)} %dynamic-slice_bitcast_fusion.3), channel_id=1, source_target_pairs={{0,8},{1,9},{2,10},{3,11},{4,12},{5,13},{6,14},{7,15},{8,0},{9,1},... | collective-permute-start | bytes 147464 | tf_op jit(solution)/shard_map/ppermute | solution.py:20
  79.2 5.6 %collective-permute-done.5 = f32[2,48,128]{2,1,0:T(8,128)S(1)} collective-permute-done((f32[2,48,128]{2,1,0:T(8,128)S(1)}, f32[2,48,128]{2,1,0:T(8,128)S(1)}, u32[]{:S(2)}, u32[]{:S(2)}) %collective-permute-start.5) | collective-permute-done | bytes 49184 | tf_op jit(solution)/shard_map/ppermute | solution.py:20
  84.8 4.4 %collective-permute-start.6 = (f32[1,48,128]{2,1,0:T(8,128)S(1)}, f32[1,48,128]{2,1,0:T(8,128)S(1)}, u32[]{:S(2)}, u32[]{:S(2)}) collective-permute-start(f32[1,48,128]{2,1,0:T(8,128)S(1)} %constant_dynamic-slice_fusion), channel_id=1, source_target_pairs={{0,16},{1,17},{2,18},{3,19},{4,20},{5,21},{6,22},{7,23},{8,24},{9,... | collective-permute-start | bytes 73736 | tf_op jit(solution)/shard_map/ppermute | solution.py:20
  89.2 8.1 %collective-permute-start.3 = (bf16[48,2048]{1,0:T(8,128)(2,1)S(1)}, bf16[48,2048]{1,0:T(8,128)(2,1)S(1)}, u32[]{:S(2)}, u32[]{:S(2)}) collective-permute-start(bf16[48,2048]{1,0:T(8,128)(2,1)S(1)} %convolution_convert_fusion), channel_id=1, source_target_pairs={{0,512},{512,0},{32,544},{544,32},{64,576},{576,64},{96,608},{608,... | collective-permute-start | bytes 589832 | tf_op jit(solution)/shard_map/ppermute | solution.py:171
  97.3 0.0 collective-permute-done.6
  97.3 0.6 reshape.117
  97.9 4.5 %collective-permute-done.3 = bf16[48,2048]{1,0:T(8,128)(2,1)S(1)} collective-permute-done((bf16[48,2048]{1,0:T(8,128)(2,1)S(1)}, bf16[48,2048]{1,0:T(8,128)(2,1)S(1)}, u32[]{:S(2)}, u32[]{:S(2)}) %collective-permute-start.3) | collective-permute-done | bytes 196640 | tf_op jit(solution)/shard_map/ppermute | solution.py:171
  102.4 1.0 fusion
  (19 shorter events, 0.2 us)
Async XLA Ops:
  0.6 21.8 %collective-permute-start = (s32[48,8]{0,1:T(8,128)}, s32[48,8]{0,1:T(8,128)S(1)}, u32[]{:S(2)}, u32[]{:S(2)}) collective-permute-start(s32[48,8]{0,1:T(8,128)} %param.7), channel_id=1, source_target_pairs={{0,512},{512,0},{32,544},{544,32},{64,576},{576,64},{96,608},{608,... | collective-permute-start | bytes 4616 | tf_op jit(solution)/shard_map/ppermute | solution.py:158
  15.8 18.0 %copy-start = (f32[1,1,128,1536]{3,2,1,0:T(8,128)S(1)}, f32[1,1,128,1536]{3,2,1,0:T(8,128)}, u32[]{:S(2)}) copy-start(f32[1,1,128,1536]{3,2,1,0:T(8,128)} %param.13) | copy-start | bytes 2359300
  22.4 37.9 %all-to-all-start = ((bf16[16,16,2048]{2,1,0:T(8,128)(2,1)}), bf16[16,16,2048]{2,1,0:T(8,128)(2,1)S(1)}, u32[]{:S(2)}, u32[]{:S(2)}) async-start(bf16[16,16,2048]{2,1,0:T(8,128)(2,1)} %bitcast.45), calls=%async_computation | async-start | bytes 2097152 | tf_op jit(solution)/shard_map/all_to_all | solution.py:149
  33.9 9.9 %collective-permute-start.1 = (f32[16,48,128]{2,1,0:T(8,128)S(1)}, f32[16,48,128]{2,1,0:T(8,128)S(1)}, u32[]{:S(2)}, u32[]{:S(2)}) collective-permute-start(f32[16,48,128]{2,1,0:T(8,128)S(1)} %dynamic-slice_bitcast_fusion), channel_id=1, source_target_pairs={{0,1},{1,0},{2,3},{3,2},{4,5},{5,4},{6,7},{7,6},{8,9},{9,8},{10,11... | collective-permute-start | bytes 1179656 | tf_op jit(solution)/shard_map/ppermute | solution.py:20
  36.5 6.7 %copy-start.1 = (s32[48,8]{0,1:T(8,128)S(1)}, s32[48,8]{0,1:T(8,128)}, u32[]{:S(2)}) copy-start(s32[48,8]{0,1:T(8,128)} %param.7) | copy-start | bytes 4612
  43.8 9.2 %collective-permute-start.2 = (f32[8,48,128]{2,1,0:T(8,128)S(1)}, f32[8,48,128]{2,1,0:T(8,128)S(1)}, u32[]{:S(2)}, u32[]{:S(2)}) collective-permute-start(f32[8,48,128]{2,1,0:T(8,128)S(1)} %dynamic-slice_bitcast_fusion.1), channel_id=1, source_target_pairs={{0,2},{1,3},{2,0},{3,1},{4,6},{5,7},{6,4},{7,5},{8,10},{9,11},{10,... | collective-permute-start | bytes 589832 | tf_op jit(solution)/shard_map/ppermute | solution.py:20
  60.6 41.8 %all-to-all-start.1 = ((bf16[16,16,2048]{2,1,0:T(8,128)(2,1)}), bf16[16,16,2048]{2,1,0:T(8,128)(2,1)S(1)}, u32[]{:S(2)}, u32[]{:S(2)}) async-start(bf16[16,16,2048]{2,1,0:T(8,128)(2,1)} %bitcast.15), calls=%async_computation.1 | async-start | bytes 2097152 | tf_op jit(solution)/shard_map/all_to_all | solution.py:149
  64.7 9.7 %collective-permute-start.4 = (f32[4,48,128]{2,1,0:T(8,128)S(1)}, f32[4,48,128]{2,1,0:T(8,128)S(1)}, u32[]{:S(2)}, u32[]{:S(2)}) collective-permute-start(f32[4,48,128]{2,1,0:T(8,128)S(1)} %dynamic-slice_bitcast_fusion.2), channel_id=1, source_target_pairs={{0,4},{1,5},{2,6},{3,7},{4,0},{5,1},{6,2},{7,3},{8,12},{9,13},{10,... | collective-permute-start | bytes 294920 | tf_op jit(solution)/shard_map/ppermute | solution.py:20
  74.4 10.3 %collective-permute-start.5 = (f32[2,48,128]{2,1,0:T(8,128)S(1)}, f32[2,48,128]{2,1,0:T(8,128)S(1)}, u32[]{:S(2)}, u32[]{:S(2)}) collective-permute-start(f32[2,48,128]{2,1,0:T(8,128)S(1)} %dynamic-slice_bitcast_fusion.3), channel_id=1, source_target_pairs={{0,8},{1,9},{2,10},{3,11},{4,12},{5,13},{6,14},{7,15},{8,0},{9,1},... | collective-permute-start | bytes 147464 | tf_op jit(solution)/shard_map/ppermute | solution.py:20
  84.8 12.5 %collective-permute-start.6 = (f32[1,48,128]{2,1,0:T(8,128)S(1)}, f32[1,48,128]{2,1,0:T(8,128)S(1)}, u32[]{:S(2)}, u32[]{:S(2)}) collective-permute-start(f32[1,48,128]{2,1,0:T(8,128)S(1)} %constant_dynamic-slice_fusion), channel_id=1, source_target_pairs={{0,16},{1,17},{2,18},{3,19},{4,20},{5,21},{6,22},{7,23},{8,24},{9,... | collective-permute-start | bytes 73736 | tf_op jit(solution)/shard_map/ppermute | solution.py:20
  89.2 13.2 %collective-permute-start.3 = (bf16[48,2048]{1,0:T(8,128)(2,1)S(1)}, bf16[48,2048]{1,0:T(8,128)(2,1)S(1)}, u32[]{:S(2)}, u32[]{:S(2)}) collective-permute-start(bf16[48,2048]{1,0:T(8,128)(2,1)S(1)} %convolution_convert_fusion), channel_id=1, source_target_pairs={{0,512},{512,0},{32,544},{544,32},{64,576},{576,64},{96,608},{608,... | collective-permute-start | bytes 589832 | tf_op jit(solution)/shard_map/ppermute | solution.py:171

commit v6 on v5

--- a/solution.py
+++ b/solution.py
@@ -11,10 +11,10 @@
 HALVES = 2
 
 
-def halve(part, stride):
+def halve(part, stride, own):
     members = lax.axis_size("edp")
     pairs = part.reshape(part.shape[0] // 2, 2, *part.shape[1:])
-    bit = (lax.axis_index("edp") // stride) % 2
+    bit = (own // stride) % 2
     kept = lax.dynamic_index_in_dim(pairs, bit, axis=1, keepdims=False)
     given = lax.dynamic_index_in_dim(pairs, 1 - bit, axis=1, keepdims=False)
     return kept + lax.ppermute(given, "edp", [(i, i ^ stride) for i in range(members)])
@@ -157,12 +157,12 @@
 
     theirs = lax.ppermute(routes, BOTH, swap)
     passed_on = send_rows(core, 1 - rest, *saved)
-    passed_on, theirs = lax.optimization_barrier((passed_on, theirs))
+    passed_on, theirs, line = lax.optimization_barrier((passed_on, theirs, lax.axis_index("edp")))
     arrived = exchange(passed_on)
     own_rows = send_rows(core, rest, *saved)
     bucket = bucket_terms[0, 0]
     part = bucket.reshape(members, bucket.size // (members * 128), 128)
-    part = halve(halve(part, 1), 2)
+    part = halve(halve(halve(part, 1, line), 2, line), 4, line)
     chosen, mine, _ = lax.optimization_barrier(
         (choice(theirs, core, rest, capacity), choice(routes, core, rest, capacity), part)
     )
@@ -171,7 +171,7 @@
     got = lax.ppermute(given, BOTH, swap)
     kept = jnp.dot(mine, exchange(own_rows), preferred_element_type=jnp.float32)
     token_grad = (kept + got.astype(jnp.float32)).astype(jnp.bfloat16)
-    part = halve(halve(halve(part, 4), 8), 16)
+    part = halve(halve(part, 8, line), 16, line)
     reduced = part.reshape(1, bucket.shape[0] // members, bucket.shape[1])
     return (token_grad, reduced)
 

time: 104 us -> 104 us (level)
  the two profiles are of different devices: /device:TPU:6 before, /device:TPU:1 now
where the time goes in v6:
time: 104 us; the launch traced here: 103 us
  starting transfers between devices  60.2 us (58%)
  waiting for transfers between devices  24.1 us (23%)
  Pallas kernels  13.2 us (13%)
  other arithmetic  1.59 us (2%)
  matrix products  1.53 us (1%)
  between operations  1.09 us (1%)
    ppermute x5, starting transfers between devices, halve(): lax.ppermute(given, 'edp', [(i, i ^ stride) for i in range(members)])  24.8 us
    all_to_all x2, starting transfers between devices, exchange(): lax.all_to_all(rows.reshape(GROUP, capacity, width), BOTH, split_axis=0,...  22.1 us
    pallas_call x2, Pallas kernels, send_rows(): pl.pallas_call(row_kernel, in_specs=[pl.BlockSpec(memory_space=pltpu.SMEM...  13.2 us
    ppermute x5, waiting for transfers between devices, halve(): lax.ppermute(given, 'edp', [(i, i ^ stride) for i in range(members)])  10 us
    ppermute x1, starting transfers between devices, shards(): theirs = lax.ppermute(routes, BOTH, swap)  8.74 us
    all_to_all x2, waiting for transfers between devices, exchange(): lax.all_to_all(rows.reshape(GROUP, capacity, width), BOTH, split_axis=0,...  7.96 us
    ppermute x1, waiting for transfers between devices, shards(): got = lax.ppermute(given, BOTH, swap)  6.13 us
    ppermute x1, starting transfers between devices, shards(): got = lax.ppermute(given, BOTH, swap)  4.64 us
  transfers between devices with their start and end apart: 9, of which 6 were waited for; matrix products, arithmetic and copies ran while one was open for 3% of the time, Pallas kernels for 13%

profile of v6, /device:TPU:1, one launch (start us, length us, event | category | flops | bytes accessed | tf_op | source)
XLA Modules:
  0.0 102.7 jit_solution(5822417589411219560)
XLA Ops:
  0.6 8.7 %collective-permute-start = (s32[48,8]{0,1:T(8,128)}, s32[48,8]{0,1:T(8,128)S(1)}, u32[]{:S(2)}, u32[]{:S(2)}) collective-permute-start(s32[48,8]{0,1:T(8,128)} %param.7), channel_id=1, source_target_pairs={{0,512},{512,0},{32,544},{544,32},{64,576},{576,64},{96,608},{608,... | collective-permute-start | bytes 4616 | tf_op jit(solution)/shard_map/ppermute | solution.py:158
  9.4 0.6 pad_add_fusion.where_ref
  10.0 6.6 %shard_map.86 = bf16[256,2048]{1,0:T(8,128)(2,1)} custom-call(s32[2]{0:T(128)} %pad_add_fusion.where_ref, bf16[32,16,768]{2,1,0:T(8,128)(2,1)} %bitcast.48, bf16[32,16,768]{2,1,0:T(8,128)(2,1)} %bitcast.50, bf16[32,16,768]{2,1,0:T(8,128)(2,1)} %bitcast.52, bf16[2048,768]{1,0:T(8,128)(2,1)} %bitcast.41, bf16[2048,768]{1,0:T(8,128)(2,1)} %bitcast.43), custom_call_target="tpu_custom_call" | custom-call | flops 1610612736 | bytes 8519680 | tf_op jit(solution)/shard_map/pallas_call | solution.py:101
  16.6 0.6 pad_add_fusion.1.where_ref
  17.2 0.1 reshape_reshape_squeeze.3
  17.3 16.3 %all-to-all-start = ((bf16[16,16,2048]{2,1,0:T(8,128)(2,1)}), bf16[16,16,2048]{2,1,0:T(8,128)(2,1)S(1)}, u32[]{:S(2)}, u32[]{:S(2)}) async-start(bf16[16,16,2048]{2,1,0:T(8,128)(2,1)} %bitcast.45), calls=%async_computation | async-start | bytes 2097152 | tf_op jit(solution)/shard_map/all_to_all | solution.py:149
  33.7 4.3 %collective-permute-start.1 = (f32[16,48,128]{2,1,0:T(8,128)S(1)}, f32[16,48,128]{2,1,0:T(8,128)S(1)}, u32[]{:S(2)}, u32[]{:S(2)}) collective-permute-start(f32[16,48,128]{2,1,0:T(8,128)S(1)} %dynamic-slice_bitcast_fusion), channel_id=1, source_target_pairs={{0,1},{1,0},{2,3},{3,2},{4,5},{5,4},{6,7},{7,6},{8,9},{9,8},{10,11... | collective-permute-start | bytes 1179656 | tf_op jit(solution)/shard_map/ppermute | solution.py:20
  38.0 0.0 copy-start.1
  38.0 6.6 %shard_map.87 = bf16[256,2048]{1,0:T(8,128)(2,1)} custom-call(s32[2]{0:T(128)} %pad_add_fusion.1.where_ref, bf16[32,16,768]{2,1,0:T(8,128)(2,1)} %bitcast.49, bf16[32,16,768]{2,1,0:T(8,128)(2,1)} %bitcast.51, bf16[32,16,768]{2,1,0:T(8,128)(2,1)} %bitcast.53, bf16[2048,768]{1,0:T(8,128)(2,1)} %bitcast.42, bf16[2048,768]{1,0:T(8,128)(2,1)} %bitcast.44), custom_call_target="tpu_custom_call" | custom-call | flops 1610612736 | bytes 8519680 | tf_op jit(solution)/shard_map/pallas_call | solution.py:101
  44.7 0.1 compare_reduce_fusion
  44.8 0.1 copy.22
  44.9 0.1 reduce_window_sum.18
  44.9 0.1 copy.20
  45.1 0.1 reduce_window_sum.17
  45.2 0.1 bitcast_add_fusion
  45.3 3.1 %collective-permute-start.2 = (f32[8,48,128]{2,1,0:T(8,128)S(1)}, f32[8,48,128]{2,1,0:T(8,128)S(1)}, u32[]{:S(2)}, u32[]{:S(2)}) collective-permute-start(f32[8,48,128]{2,1,0:T(8,128)S(1)} %dynamic-slice_bitcast_fusion.1), channel_id=1, source_target_pairs={{0,2},{1,3},{2,0},{3,1},{4,6},{5,7},{6,4},{7,5},{8,10},{9,11},{10,... | collective-permute-start | bytes 589832 | tf_op jit(solution)/shard_map/ppermute | solution.py:20
  48.4 0.1 fusion.2
  48.5 5.2 %collective-permute-done.2 = f32[8,48,128]{2,1,0:T(8,128)S(1)} collective-permute-done((f32[8,48,128]{2,1,0:T(8,128)S(1)}, f32[8,48,128]{2,1,0:T(8,128)S(1)}, u32[]{:S(2)}, u32[]{:S(2)}) %collective-permute-start.2) | collective-permute-done | bytes 196640 | tf_op jit(solution)/shard_map/ppermute | solution.py:20
  53.7 4.0 %collective-permute-start.3 = (f32[4,48,128]{2,1,0:T(8,128)S(1)}, f32[4,48,128]{2,1,0:T(8,128)S(1)}, u32[]{:S(2)}, u32[]{:S(2)}) collective-permute-start(f32[4,48,128]{2,1,0:T(8,128)S(1)} %dynamic-slice_bitcast_fusion.2), channel_id=1, source_target_pairs={{0,4},{1,5},{2,6},{3,7},{4,0},{5,1},{6,2},{7,3},{8,12},{9,13},{10,... | collective-permute-start | bytes 294920 | tf_op jit(solution)/shard_map/ppermute | solution.py:20
  57.8 0.1 fusion.1
  57.9 3.4 %collective-permute-done.3 = f32[4,48,128]{2,1,0:T(8,128)S(1)} collective-permute-done((f32[4,48,128]{2,1,0:T(8,128)S(1)}, f32[4,48,128]{2,1,0:T(8,128)S(1)}, u32[]{:S(2)}, u32[]{:S(2)}) %collective-permute-start.3) | collective-permute-done | bytes 98336 | tf_op jit(solution)/shard_map/ppermute | solution.py:20
  61.4 0.6 all-to-all-done
  61.9 0.3 convolution_convert_fusion
  62.2 5.8 %all-to-all-start.1 = ((bf16[16,16,2048]{2,1,0:T(8,128)(2,1)}), bf16[16,16,2048]{2,1,0:T(8,128)(2,1)S(1)}, u32[]{:S(2)}, u32[]{:S(2)}) async-start(bf16[16,16,2048]{2,1,0:T(8,128)(2,1)} %bitcast.18), calls=%async_computation.1 | async-start | bytes 2097152 | tf_op jit(solution)/shard_map/all_to_all | solution.py:149
  68.1 9.3 %collective-permute-start.5 = (f32[2,48,128]{2,1,0:T(8,128)S(1)}, f32[2,48,128]{2,1,0:T(8,128)S(1)}, u32[]{:S(2)}, u32[]{:S(2)}) collective-permute-start(f32[2,48,128]{2,1,0:T(8,128)S(1)} %dynamic-slice_bitcast_fusion.3), channel_id=1, source_target_pairs={{0,8},{1,9},{2,10},{3,11},{4,12},{5,13},{6,14},{7,15},{8,0},{9,1},... | collective-permute-start | bytes 147464 | tf_op jit(solution)/shard_map/ppermute | solution.py:20
  77.4 1.4 %collective-permute-done.5 = f32[2,48,128]{2,1,0:T(8,128)S(1)} collective-permute-done((f32[2,48,128]{2,1,0:T(8,128)S(1)}, f32[2,48,128]{2,1,0:T(8,128)S(1)}, u32[]{:S(2)}, u32[]{:S(2)}) %collective-permute-start.5) | collective-permute-done | bytes 49184 | tf_op jit(solution)/shard_map/ppermute | solution.py:20
  78.9 4.0 %collective-permute-start.6 = (f32[1,48,128]{2,1,0:T(8,128)S(1)}, f32[1,48,128]{2,1,0:T(8,128)S(1)}, u32[]{:S(2)}, u32[]{:S(2)}) collective-permute-start(f32[1,48,128]{2,1,0:T(8,128)S(1)} %constant_dynamic-slice_fusion), channel_id=1, source_target_pairs={{0,16},{1,17},{2,18},{3,19},{4,20},{5,21},{6,22},{7,23},{8,24},{9,... | collective-permute-start | bytes 73736 | tf_op jit(solution)/shard_map/ppermute | solution.py:20
  82.9 4.6 %collective-permute-start.4 = (bf16[48,2048]{1,0:T(8,128)(2,1)S(1)}, bf16[48,2048]{1,0:T(8,128)(2,1)S(1)}, u32[]{:S(2)}, u32[]{:S(2)}) collective-permute-start(bf16[48,2048]{1,0:T(8,128)(2,1)S(1)} %convolution_convert_fusion), channel_id=1, source_target_pairs={{0,512},{512,0},{32,544},{544,32},{64,576},{576,64},{96,608},{608,... | collective-permute-start | bytes 589832 | tf_op jit(solution)/shard_map/ppermute | solution.py:171
  87.6 0.6 reshape.117
  88.2 6.1 %collective-permute-done.4 = bf16[48,2048]{1,0:T(8,128)(2,1)S(1)} collective-permute-done((bf16[48,2048]{1,0:T(8,128)(2,1)S(1)}, bf16[48,2048]{1,0:T(8,128)(2,1)S(1)}, u32[]{:S(2)}, u32[]{:S(2)}) %collective-permute-start.4) | collective-permute-done | bytes 196640 | tf_op jit(solution)/shard_map/ppermute | solution.py:171
  94.3 7.4 %all-to-all-done.1 = bf16[16,16,2048]{2,1,0:T(8,128)(2,1)S(1)} async-done(((bf16[16,16,2048]{2,1,0:T(8,128)(2,1)}), bf16[16,16,2048]{2,1,0:T(8,128)(2,1)S(1)}, u32[]{:S(2)}, u32[]{:S(2)}) %all-to-all-start.1) | async-done | bytes 1048608 | tf_op jit(solution)/shard_map/all_to_all | solution.py:149
  101.8 1.0 fusion
  (19 shorter events, 0.2 us)
Async XLA Ops:
  0.6 16.7 %collective-permute-start = (s32[48,8]{0,1:T(8,128)}, s32[48,8]{0,1:T(8,128)S(1)}, u32[]{:S(2)}, u32[]{:S(2)}) collective-permute-start(s32[48,8]{0,1:T(8,128)} %param.7), channel_id=1, source_target_pairs={{0,512},{512,0},{32,544},{544,32},{64,576},{576,64},{96,608},{608,... | collective-permute-start | bytes 4616 | tf_op jit(solution)/shard_map/ppermute | solution.py:158
  10.0 7.3 %copy-start = (f32[1,1,128,1536]{3,2,1,0:T(8,128)S(1)}, f32[1,1,128,1536]{3,2,1,0:T(8,128)}, u32[]{:S(2)}) copy-start(f32[1,1,128,1536]{3,2,1,0:T(8,128)} %param.13) | copy-start | bytes 2359300
  17.3 44.6 %all-to-all-start = ((bf16[16,16,2048]{2,1,0:T(8,128)(2,1)}), bf16[16,16,2048]{2,1,0:T(8,128)(2,1)S(1)}, u32[]{:S(2)}, u32[]{:S(2)}) async-start(bf16[16,16,2048]{2,1,0:T(8,128)(2,1)} %bitcast.45), calls=%async_computation | async-start | bytes 2097152 | tf_op jit(solution)/shard_map/all_to_all | solution.py:149
  33.7 11.5 %collective-permute-start.1 = (f32[16,48,128]{2,1,0:T(8,128)S(1)}, f32[16,48,128]{2,1,0:T(8,128)S(1)}, u32[]{:S(2)}, u32[]{:S(2)}) collective-permute-start(f32[16,48,128]{2,1,0:T(8,128)S(1)} %dynamic-slice_bitcast_fusion), channel_id=1, source_target_pairs={{0,1},{1,0},{2,3},{3,2},{4,5},{5,4},{6,7},{7,6},{8,9},{9,8},{10,11... | collective-permute-start | bytes 1179656 | tf_op jit(solution)/shard_map/ppermute | solution.py:20
  38.0 6.7 %copy-start.1 = (s32[48,8]{0,1:T(8,128)S(1)}, s32[48,8]{0,1:T(8,128)}, u32[]{:S(2)}) copy-start(s32[48,8]{0,1:T(8,128)} %param.7) | copy-start | bytes 4612
  45.3 8.4 %collective-permute-start.2 = (f32[8,48,128]{2,1,0:T(8,128)S(1)}, f32[8,48,128]{2,1,0:T(8,128)S(1)}, u32[]{:S(2)}, u32[]{:S(2)}) collective-permute-start(f32[8,48,128]{2,1,0:T(8,128)S(1)} %dynamic-slice_bitcast_fusion.1), channel_id=1, source_target_pairs={{0,2},{1,3},{2,0},{3,1},{4,6},{5,7},{6,4},{7,5},{8,10},{9,11},{10,... | collective-permute-start | bytes 589832 | tf_op jit(solution)/shard_map/ppermute | solution.py:20
  53.7 7.6 %collective-permute-start.3 = (f32[4,48,128]{2,1,0:T(8,128)S(1)}, f32[4,48,128]{2,1,0:T(8,128)S(1)}, u32[]{:S(2)}, u32[]{:S(2)}) collective-permute-start(f32[4,48,128]{2,1,0:T(8,128)S(1)} %dynamic-slice_bitcast_fusion.2), channel_id=1, source_target_pairs={{0,4},{1,5},{2,6},{3,7},{4,0},{5,1},{6,2},{7,3},{8,12},{9,13},{10,... | collective-permute-start | bytes 294920 | tf_op jit(solution)/shard_map/ppermute | solution.py:20
  62.2 39.5 %all-to-all-start.1 = ((bf16[16,16,2048]{2,1,0:T(8,128)(2,1)}), bf16[16,16,2048]{2,1,0:T(8,128)(2,1)S(1)}, u32[]{:S(2)}, u32[]{:S(2)}) async-start(bf16[16,16,2048]{2,1,0:T(8,128)(2,1)} %bitcast.18), calls=%async_computation.1 | async-start | bytes 2097152 | tf_op jit(solution)/shard_map/all_to_all | solution.py:149
  68.1 10.8 %collective-permute-start.5 = (f32[2,48,128]{2,1,0:T(8,128)S(1)}, f32[2,48,128]{2,1,0:T(8,128)S(1)}, u32[]{:S(2)}, u32[]{:S(2)}) collective-permute-start(f32[2,48,128]{2,1,0:T(8,128)S(1)} %dynamic-slice_bitcast_fusion.3), channel_id=1, source_target_pairs={{0,8},{1,9},{2,10},{3,11},{4,12},{5,13},{6,14},{7,15},{8,0},{9,1},... | collective-permute-start | bytes 147464 | tf_op jit(solution)/shard_map/ppermute | solution.py:20
  78.9 8.7 %collective-permute-start.6 = (f32[1,48,128]{2,1,0:T(8,128)S(1)}, f32[1,48,128]{2,1,0:T(8,128)S(1)}, u32[]{:S(2)}, u32[]{:S(2)}) collective-permute-start(f32[1,48,128]{2,1,0:T(8,128)S(1)} %constant_dynamic-slice_fusion), channel_id=1, source_target_pairs={{0,16},{1,17},{2,18},{3,19},{4,20},{5,21},{6,22},{7,23},{8,24},{9,... | collective-permute-start | bytes 73736 | tf_op jit(solution)/shard_map/ppermute | solution.py:20
  82.9 11.4 %collective-permute-start.4 = (bf16[48,2048]{1,0:T(8,128)(2,1)S(1)}, bf16[48,2048]{1,0:T(8,128)(2,1)S(1)}, u32[]{:S(2)}, u32[]{:S(2)}) collective-permute-start(bf16[48,2048]{1,0:T(8,128)(2,1)S(1)} %convolution_convert_fusion), channel_id=1, source_target_pairs={{0,512},{512,0},{32,544},{544,32},{64,576},{576,64},{96,608},{608,... | collective-permute-start | bytes 589832 | tf_op jit(solution)/shard_map/ppermute | solution.py:171

commit v7 on v4

--- a/solution.py
+++ b/solution.py
@@ -9,23 +9,6 @@
 GROUP = 16
 CHUNKS = 4
 HALVES = 2
-
-
-def reduce_bucket(bucket):
-    rows, width = bucket.shape
-    members = lax.axis_size("edp")
-    own = lax.axis_index("edp")
-    part = bucket.reshape(members, rows * width // (members * 128), 128)
-    stride = 1
-    while stride < members:
-        pairs = part.reshape(part.shape[0] // 2, 2, *part.shape[1:])
-        bit = (own // stride) % 2
-        kept = lax.dynamic_index_in_dim(pairs, bit, axis=1, keepdims=False)
-        given = lax.dynamic_index_in_dim(pairs, 1 - bit, axis=1, keepdims=False)
-        swap = [(i, i ^ stride) for i in range(members)]
-        part = kept + lax.ppermute(given, "edp", swap)
-        stride *= 2
-    return part.reshape(1, rows // members, width)
 
 
 def place(core, member, rest):
@@ -159,6 +142,9 @@
     own = lax.axis_index("ep")
     rest = jnp.where(core == 0, own // GROUP, own // 4 % 2)
     swap = partners(members)
+    bucket = bucket_terms[0, 0]
+    parts = bucket.reshape(members, bucket.size // (members * 128), 128)
+    summed = lax.psum_scatter(parts, "edp", scatter_dimension=0, tiled=True)
     rows = send_rows(core, gate_pre[0, 0], up_pre[0, 0], hidden_grad[0, 0], w_gate[0], w_up[0])
     theirs = lax.ppermute(routes, BOTH, swap)
     rows, theirs = lax.optimization_barrier((rows, theirs))
@@ -175,8 +161,9 @@
     given = jnp.dot(chosen[:tokens], arrived, preferred_element_type=jnp.float32)
     got = lax.ppermute(given.astype(jnp.bfloat16), BOTH, swap)
     kept = jnp.dot(chosen[tokens:], arrived, preferred_element_type=jnp.float32)
+    got, kept, summed = lax.optimization_barrier((got, kept, summed))
     token_grad = (kept + got.astype(jnp.float32)).astype(jnp.bfloat16)
-    reduced = reduce_bucket(bucket_terms[0, 0])
+    reduced = summed.reshape(1, bucket.shape[0] // members, bucket.shape[1])
     return (token_grad, reduced)
 
 

time: 102 us -> 179 us (1.75)
  the two profiles are of different devices: /device:TPU:476 before, /device:TPU:1 now
where the time goes in v7:
time: 179 us; the launch traced here: 176 us
  waiting for transfers between devices  121 us (68%)
  starting transfers between devices  27.7 us (15%)
  between operations  14.2 us (8%)
  Pallas kernels  8.07 us (5%)
  local copies, waits for them, and re-layouts  2.56 us (1%)
    reduce_scatter x1, waiting for transfers between devices, shards(): summed = lax.psum_scatter(parts, 'edp', scatter_dimension=0, tiled=True)  71.5 us
    all_to_all x1, waiting for transfers between devices, shards(): lax.all_to_all(rows.reshape(GROUP, 2 * capacity, width), BOTH, split_axis...  49.7 us
    all_to_all x1, starting transfers between devices, shards(): lax.all_to_all(rows.reshape(GROUP, 2 * capacity, width), BOTH, split_axis...  16.4 us
    ppermute x1, starting transfers between devices, shards(): theirs = lax.ppermute(routes, BOTH, swap)  8.74 us
    pallas_call x1, Pallas kernels, send_rows(): pl.pallas_call(row_kernel, in_specs=[pl.BlockSpec(memory_space=pltpu.SMEM...  8.07 us
  transfers between devices with their start and end apart: 4, of which 2 were waited for; matrix products, arithmetic and copies ran while one was open for 1% of the time, Pallas kernels for 5%

profile of v7, /device:TPU:1, one launch (start us, length us, event | category | flops | bytes accessed | tf_op | source)
XLA Modules:
  0.0 176.0 jit_solution(6668798656443231906)
XLA Ops:
  7.2 8.7 %collective-permute-start = (s32[48,8]{0,1:T(8,128)}, s32[48,8]{0,1:T(8,128)S(1)}, u32[]{:S(2)}, u32[]{:S(2)}) collective-permute-start(s32[48,8]{0,1:T(8,128)} %param.7), channel_id=1, source_target_pairs={{0,512},{512,0},{32,544},{544,32},{64,576},{576,64},{96,608},{608,... | collective-permute-start | bytes 4616 | tf_op jit(solution)/shard_map/ppermute | solution.py:149
  15.9 8.1 %shard_map.86 = bf16[512,2048]{1,0:T(8,128)(2,1)} custom-call(s32[1]{0:T(128)} %bitcast.core_ref, bf16[32,16,768]{2,1,0:T(8,128)(2,1)} %bitcast.25, bf16[32,16,768]{2,1,0:T(8,128)(2,1)} %bitcast.26, bf16[32,16,768]{2,1,0:T(8,128)(2,1)} %bitcast.27, bf16[2048,768]{1,0:T(8,128)(2,1)} %bitcast.23, bf16[2048,768]{1,0:T(8,128)(2,1)} %bitcast.24), custom_call_target="tpu_custom_call" | custom-call | flops 3221225472 | bytes 10747904 | tf_op jit(solution)/shard_map/pallas_call | solution.py:94
  24.0 0.0 collective-permute-done
  24.0 0.0 copy-start
  24.0 16.4 %all-to-all-start = ((bf16[16,32,2048]{2,1,0:T(8,128)(2,1)}), bf16[16,32,2048]{2,1,0:T(8,128)(2,1)S(1)}, u32[]{:S(2)}, u32[]{:S(2)}) async-start(bf16[16,32,2048]{2,1,0:T(8,128)(2,1)} %bitcast.19), calls=%async_computation | async-start | bytes 4194304 | tf_op jit(solution)/shard_map/all_to_all | solution.py:151
  40.5 0.0 copy-start.1
  40.5 0.0 reduce-scatter.2.cloned.1.call-start
  40.5 0.0 copy-done
  40.5 1.0 reshape_squeeze.3
  41.5 0.0 reduce-scatter.2.cloned.1.call-update
  41.6 0.0 copy-done.1
  41.6 0.1 compare_reduce_fusion
  41.8 0.1 reduce_or.12
  41.8 0.1 copy.12
  41.9 0.1 reduce_window_sum.13
  42.0 0.1 copy.13
  42.1 0.2 fusion.1
  42.3 49.7 %all-to-all-done = bf16[16,32,2048]{2,1,0:T(8,128)(2,1)S(1)} async-done(((bf16[16,32,2048]{2,1,0:T(8,128)(2,1)}), bf16[16,32,2048]{2,1,0:T(8,128)(2,1)S(1)}, u32[]{:S(2)}, u32[]{:S(2)}) %all-to-all-start) | async-done | bytes 2097184 | tf_op jit(solution)/shard_map/all_to_all | solution.py:151
  92.0 0.5 convolution_convert_fusion
  92.5 2.6 %collective-permute-start.1 = (bf16[48,2048]{1,0:T(8,128)(2,1)S(1)}, bf16[48,2048]{1,0:T(8,128)(2,1)S(1)}, u32[]{:S(2)}, u32[]{:S(2)}) collective-permute-start(bf16[48,2048]{1,0:T(8,128)(2,1)S(1)} %convolution_convert_fusion), channel_id=1, source_target_pairs={{0,512},{512,0},{32,544},{544,32},{64,576},{576,64},{96,608},{608,... | collective-permute-start | bytes 589832 | tf_op jit(solution)/shard_map/ppermute | solution.py:162
  95.1 0.5 fusion.2
  95.5 71.5 %reduce-scatter.2.cloned.1.call-done = f32[1,48,128]{2,1,0:T(8,128)} async-done(((f32[32,48,128]{2,1,0:T(8,128)}), f32[1,48,128]{2,1,0:T(8,128)}) %reduce-scatter.2.cloned.1.call-update) | async-done | bytes 24592 | tf_op jit(solution)/shard_map/reduce_scatter | solution.py:147
  167.0 0.0 collective-permute-done.1
  167.0 1.4 reshape.147
  168.4 0.7 add_convert_fusion
  (7 shorter events, 0.1 us)
Async XLA Ops:
  7.2 16.8 %collective-permute-start = (s32[48,8]{0,1:T(8,128)}, s32[48,8]{0,1:T(8,128)S(1)}, u32[]{:S(2)}, u32[]{:S(2)}) collective-permute-start(s32[48,8]{0,1:T(8,128)} %param.7), channel_id=1, source_target_pairs={{0,512},{512,0},{32,544},{544,32},{64,576},{576,64},{96,608},{608,... | collective-permute-start | bytes 4616 | tf_op jit(solution)/shard_map/ppermute | solution.py:149
  24.0 16.5 %copy-start = (f32[1,1,128,1536]{3,2,1,0:T(8,128)S(1)}, f32[1,1,128,1536]{3,2,1,0:T(8,128)}, u32[]{:S(2)}) copy-start(f32[1,1,128,1536]{3,2,1,0:T(8,128)} %param.13) | copy-start | bytes 2359300
  24.0 68.0 %all-to-all-start = ((bf16[16,32,2048]{2,1,0:T(8,128)(2,1)}), bf16[16,32,2048]{2,1,0:T(8,128)(2,1)S(1)}, u32[]{:S(2)}, u32[]{:S(2)}) async-start(bf16[16,32,2048]{2,1,0:T(8,128)(2,1)} %bitcast.19), calls=%async_computation | async-start | bytes 4194304 | tf_op jit(solution)/shard_map/all_to_all | solution.py:151
  40.5 1.2 copy-start.1
  40.5 126.6 %reduce-scatter.2.cloned.1.call-start = ((), (), s32[]{:S(2)}) async-start(), calls=%async_computation.2 | async-start | bytes 811008 | tf_op jit(solution)/shard_map/reduce_scatter | solution.py:147
  92.5 74.6 %collective-permute-start.1 = (bf16[48,2048]{1,0:T(8,128)(2,1)S(1)}, bf16[48,2048]{1,0:T(8,128)(2,1)S(1)}, u32[]{:S(2)}, u32[]{:S(2)}) collective-permute-start(bf16[48,2048]{1,0:T(8,128)(2,1)S(1)} %convolution_convert_fusion), channel_id=1, source_target_pairs={{0,512},{512,0},{32,544},{544,32},{64,576},{576,64},{96,608},{608,... | collective-permute-start | bytes 589832 | tf_op jit(solution)/shard_map/ppermute | solution.py:162
Sparse Core Ops, SparseCore 0:
  44.7 122.3 reduce-scatter.1

commit v8 on v1

--- a/solution.py
+++ b/solution.py
@@ -21,37 +21,59 @@
     return part.reshape(1, rows // members, width)
 
 
-def choice(routes, experts, capacity):
-    matches = (routes[:, :, None] == jnp.arange(experts, dtype=jnp.int32)).any(axis=1)
+def choice(routes, parity, experts, capacity):
+    tokens = routes.shape[1]
+    group = experts // 2
+    named = 2 * jnp.arange(group, dtype=jnp.int32) + parity
+    matches = (routes[:, :, :, None] == named).any(axis=2)
     count = matches.astype(jnp.int32)
-    earlier = jnp.cumsum(count, axis=0) - count
-    slot = jnp.where(matches, earlier, -1)
-    chosen = slot[:, :, None] == jnp.arange(capacity, dtype=jnp.int32)
-    return chosen.astype(jnp.bfloat16).reshape(routes.shape[0], experts * capacity)
+    earlier = jnp.cumsum(count, axis=1) - count
+    slot = jnp.where(matches, earlier, -1).reshape(2 * tokens, group).astype(jnp.bfloat16)
+    column = jnp.arange(experts * capacity, dtype=jnp.int32)
+    spread = column[None, :] // (2 * capacity) == jnp.arange(group, dtype=jnp.int32)[:, None]
+    slots = jnp.dot(slot, spread.astype(jnp.bfloat16), preferred_element_type=jnp.float32)
+    second = jnp.arange(2 * tokens, dtype=jnp.int32)[:, None] // tokens
+    owner = jnp.where(second == 0, 1 - parity, parity)
+    same = owner == (column // capacity % 2)[None, :]
+    chosen = same & (slots == (column % capacity).astype(jnp.float32)[None, :])
+    return chosen.astype(jnp.bfloat16)
 
 
 def shards(routes, gate_pre, up_pre, hidden_grad, w_gate, w_up, bucket_terms):
     experts = lax.axis_size("ep")
     capacity = gate_pre.shape[3]
+    tokens = routes.shape[0]
     width, hidden = w_gate.shape[1:]
+    parity = lax.axis_index("ep") % 2
+    swap = [(e, e ^ 1) for e in range(experts)]
     gate_f = gate_pre.reshape(experts * capacity, hidden).astype(jnp.float32)
     up_f = up_pre.reshape(experts * capacity, hidden).astype(jnp.float32)
     grad_f = hidden_grad.reshape(experts * capacity, hidden).astype(jnp.float32)
-    sigmoid_gate = 1.0 / (1.0 + jnp.exp(-gate_f))
-    grad_gate = (grad_f * up_f * sigmoid_gate * (1.0 + gate_f * (1.0 - sigmoid_gate))).astype(
-        jnp.bfloat16
-    )
-    grad_up = (grad_f * gate_f * sigmoid_gate).astype(jnp.bfloat16)
+    sigmoid_gate = 0.5 + 0.5 * jnp.tanh(0.5 * gate_f)
+    scaled = grad_f * sigmoid_gate
+    grad_gate = (scaled * up_f * (1.0 + gate_f * (1.0 - sigmoid_gate))).astype(jnp.bfloat16)
+    grad_up = (scaled * gate_f).astype(jnp.bfloat16)
     dims = (((1,), (1,)), ((), ()))
     first = lax.dot_general(grad_gate, w_gate[0], dims, preferred_element_type=jnp.float32)
     second = lax.dot_general(grad_up, w_up[0], dims, preferred_element_type=jnp.float32)
-    slot_grad = (first + second).astype(jnp.bfloat16)
-    returned = lax.all_to_all(
-        slot_grad.reshape(experts, capacity, width), "ep", split_axis=0, concat_axis=0, tiled=True
-    )
-    flat_rows = returned.reshape(experts * capacity, width)
-    chosen = choice(routes, experts, capacity)
-    token_grad = jnp.dot(chosen, flat_rows, preferred_element_type=jnp.float32).astype(jnp.bfloat16)
+    rows = (first + second).astype(jnp.bfloat16)
+    theirs = lax.ppermute(routes, "ep", swap)
+    rows, theirs = lax.optimization_barrier((rows, theirs))
+    arrived = lax.all_to_all(
+        rows.reshape(experts // 2, 2 * capacity, width),
+        "ep",
+        split_axis=0,
+        concat_axis=0,
+        axis_index_groups=[list(range(p, experts, 2)) for p in range(2)],
+        tiled=True,
+    ).reshape(experts * capacity, width)
+    chosen = choice(jnp.stack([theirs, routes]), parity, experts, capacity)
+    chosen = lax.optimization_barrier(chosen)
+    given = jnp.dot(chosen[:tokens], arrived, preferred_element_type=jnp.float32)
+    got = lax.ppermute(given.astype(jnp.bfloat16), "ep", swap)
+    kept = jnp.dot(chosen[tokens:], arrived, preferred_element_type=jnp.float32)
+    kept = lax.optimization_barrier(kept)
+    token_grad = (kept + got.astype(jnp.float32)).astype(jnp.bfloat16)
     reduced = reduce_bucket(bucket_terms[0, 0])
     return (token_grad, reduced)
 

time: 107 us -> 119 us (1.11)
  the two profiles are of different devices: /device:TPU:190 before, /device:TPU:102 now
where the time goes in v8:
time: 119 us
  waiting for transfers between devices  58 us (49%)
  starting transfers between devices  41.4 us (35%)
  matrix products  9.3 us (8%)
  local copies, waits for them, and re-layouts  4.86 us (4%)
  other arithmetic  4.4 us (4%)
    ppermute x5, waiting for transfers between devices, reduce_bucket(): part = kept + lax.ppermute(given, 'edp', swap)  32 us
    all_to_all x1, waiting for transfers between devices, shards(): lax.all_to_all(rows.reshape(experts // 2, 2 * capacity, width), 'ep', spl...  22.4 us
    all_to_all x1, starting transfers between devices, shards(): lax.all_to_all(rows.reshape(experts // 2, 2 * capacity, width), 'ep', spl...  20.7 us
    ppermute x5, starting transfers between devices, reduce_bucket(): part = kept + lax.ppermute(given, 'edp', swap)  15.8 us
    ppermute x1, waiting for transfers between devices, shards(): got = lax.ppermute(given.astype(jnp.bfloat16), 'ep', swap)  3.56 us
    dot_general x1, matrix products, shards(): lax.dot_general(grad_gate, w_gate[0], dims, preferred_element_type=jnp.fl...  3.13 us
    ppermute x1, starting transfers between devices, shards(): theirs = lax.ppermute(routes, 'ep', swap)  2.96 us
    convert_element_type x1, other arithmetic, shards(): (scaled * up_f * (1.0 + gate_f * (1.0 - sigmoid_gate))).astype(jnp.bfloat16)  2.39 us
  transfers between devices with their start and end apart: 8, of which 7 were waited for; matrix products, arithmetic and copies ran while one was open for 13% of the time, Pallas kernels for 0%

profile of v8, /device:TPU:102, one launch (start us, length us, event | category | flops | bytes accessed | tf_op | source)
XLA Modules:
  0.0 118.9 jit_solution(11440417253138026252)
XLA Ops:
  0.6 3.0 %collective-permute-start = (s32[48,8]{0,1:T(8,128)}, s32[48,8]{0,1:T(8,128)S(1)}, u32[]{:S(2)}, u32[]{:S(2)}) collective-permute-start(s32[48,8]{0,1:T(8,128)} %param.7), channel_id=1, source_target_pairs={{0,32},{32,0},{64,96},{96,64},{128,160},{160,128},{192,224},{224,1... | collective-permute-start | bytes 4616 | tf_op jit(solution)/shard_map/ppermute | solution.py:60
  3.6 2.4 %fusion.13 = (bf16[1,1,32,16,768]{4,3,2,1,0:T(8,128)(2,1)S(1)}, bf16[1,1,32,16,768]{4,3,2,1,0:T(8,128)(2,1)S(1)}) fusion(bf16[1,1,32,16,768]{4,3,2,1,0:T(8,128)(2,1)} %param.8, bf16[1,1,32,16,768]{4,3,2,1,0:T(8,128)(2,1)} %param.9, bf16[1,1,32,16,768]{4,3,2,1,0:T(8,128)(2,1)} %param.10), kind=kLoop, calls=%fused_computation.16 | loop fusion | flops 5898240 | bytes 3932160 | tf_op jit(solution)/shard_map/convert_element_type | solution.py:54
  6.0 1.8 %fusion = f32[512,2048]{1,0:T(8,128)S(1)} fusion(bf16[512,768]{1,0:T(8,128)(2,1)S(1)} %bitcast.52, bf16[1,2048,768]{2,1,0:T(8,128)(2,1)S(1)} %copy-done), kind=kOutput, calls=%fused_computation.1 | convolution fusion | flops 1610612736 | bytes 8126464 | tf_op jit(solution)/shard_map/dot_general | solution.py:58
  7.9 0.1 copy-done.2
  7.9 3.1 %add_convert_fusion = bf16[512,2048]{1,0:T(8,128)(2,1)} fusion(f32[512,2048]{1,0:T(8,128)S(1)} %fusion, bf16[512,768]{1,0:T(8,128)(2,1)S(1)} %bitcast.51, bf16[1,2048,768]{2,1,0:T(8,128)(2,1)S(1)} %copy-done.2), kind=kOutput, calls=%fused_computation | convolution fusion | flops 1612709888 | bytes 10223616 | tf_op jit(solution)/shard_map/dot_general | solution.py:57
  11.0 20.7 %all-to-all-start = ((bf16[16,32,2048]{2,1,0:T(8,128)(2,1)}), bf16[16,32,2048]{2,1,0:T(8,128)(2,1)}, u32[]{:S(2)}, u32[]{:S(2)}) async-start(bf16[16,32,2048]{2,1,0:T(8,128)(2,1)} %bitcast.46), calls=%async_computation | async-start | bytes 4194304 | tf_op jit(solution)/shard_map/all_to_all | solution.py:62
  31.7 2.1 %reshape_reshape_squeeze.3 = f32[16,2,48,128]{3,2,1,0:T(8,128)} reshape(f32[1,1,128,1536]{3,2,1,0:T(8,128)} %param.13) | data formatting | bytes 1572864 | tf_op jit(solution)/shard_map/reshape;reshape;squeeze | solution.py:14
  33.8 1.8 %dynamic-slice_bitcast_fusion = f32[16,48,128]{2,1,0:T(8,128)} fusion(f32[16,2,48,128]{3,2,1,0:T(8,128)} %reshape_reshape_squeeze.3, s32[]{:T(128)S(6)} %select_n.147), kind=kLoop, calls=%fused_computation.22 | loop fusion | bytes 786436 | tf_op jit(solution)/shard_map/jit(dynamic_index_in_dim)/squeeze | solution.py:17
  35.6 1.9 %collective-permute-start.2 = (f32[16,48,128]{2,1,0:T(8,128)}, f32[16,48,128]{2,1,0:T(8,128)S(1)}, u32[]{:S(2)}, u32[]{:S(2)}) collective-permute-start(f32[16,48,128]{2,1,0:T(8,128)} %dynamic-slice_bitcast_fusion), channel_id=1, source_target_pairs={{0,1},{1,0},{2,3},{3,2},{4,5},{5,4},{6,7},{7,6},{8,9},{9,8},{10,11... | collective-permute-start | bytes 1179656 | tf_op jit(solution)/shard_map/ppermute | solution.py:19
  37.7 1.7 %collective-permute-done.2 = f32[16,48,128]{2,1,0:T(8,128)S(1)} collective-permute-done((f32[16,48,128]{2,1,0:T(8,128)}, f32[16,48,128]{2,1,0:T(8,128)S(1)}, u32[]{:S(2)}, u32[]{:S(2)}) %collective-permute-start.2) | collective-permute-done | bytes 393248 | tf_op jit(solution)/shard_map/ppermute | solution.py:19
  39.4 1.0 bitcast_add_fusion
  40.5 2.4 %collective-permute-start.3 = (f32[8,48,128]{2,1,0:T(8,128)S(1)}, f32[8,48,128]{2,1,0:T(8,128)S(1)}, u32[]{:S(2)}, u32[]{:S(2)}) collective-permute-start(f32[8,48,128]{2,1,0:T(8,128)S(1)} %dynamic-slice_bitcast_fusion.1), channel_id=1, source_target_pairs={{0,2},{1,3},{2,0},{3,1},{4,6},{5,7},{6,4},{7,5},{8,10},{9,11},{10,... | collective-permute-start | bytes 589832 | tf_op jit(solution)/shard_map/ppermute | solution.py:19
  43.0 6.4 %collective-permute-done.3 = f32[8,48,128]{2,1,0:T(8,128)S(1)} collective-permute-done((f32[8,48,128]{2,1,0:T(8,128)S(1)}, f32[8,48,128]{2,1,0:T(8,128)S(1)}, u32[]{:S(2)}, u32[]{:S(2)}) %collective-permute-start.3) | collective-permute-done | bytes 196640 | tf_op jit(solution)/shard_map/ppermute | solution.py:19
  49.4 2.4 %collective-permute-start.4 = (f32[4,48,128]{2,1,0:T(8,128)S(1)}, f32[4,48,128]{2,1,0:T(8,128)S(1)}, u32[]{:S(2)}, u32[]{:S(2)}) collective-permute-start(f32[4,48,128]{2,1,0:T(8,128)S(1)} %dynamic-slice_bitcast_fusion.2), channel_id=1, source_target_pairs={{0,4},{1,5},{2,6},{3,7},{4,0},{5,1},{6,2},{7,3},{8,12},{9,13},{10,... | collective-permute-start | bytes 294920 | tf_op jit(solution)/shard_map/ppermute | solution.py:19
  51.8 6.5 %collective-permute-done.4 = f32[4,48,128]{2,1,0:T(8,128)S(1)} collective-permute-done((f32[4,48,128]{2,1,0:T(8,128)S(1)}, f32[4,48,128]{2,1,0:T(8,128)S(1)}, u32[]{:S(2)}, u32[]{:S(2)}) %collective-permute-start.4) | collective-permute-done | bytes 98336 | tf_op jit(solution)/shard_map/ppermute | solution.py:19
  58.4 4.7 %collective-permute-start.5 = (f32[2,48,128]{2,1,0:T(8,128)S(1)}, f32[2,48,128]{2,1,0:T(8,128)S(1)}, u32[]{:S(2)}, u32[]{:S(2)}) collective-permute-start(f32[2,48,128]{2,1,0:T(8,128)S(1)} %dynamic-slice_bitcast_fusion.3), channel_id=1, source_target_pairs={{0,8},{1,9},{2,10},{3,11},{4,12},{5,13},{6,14},{7,15},{8,0},{9,1},... | collective-permute-start | bytes 147464 | tf_op jit(solution)/shard_map/ppermute | solution.py:19
  63.1 0.1 compare_reduce_fusion
  63.3 0.1 reduce_or.12
  63.4 0.1 copy.19
  63.4 0.1 reduce_window_sum.13
  63.5 0.1 copy.20
  63.6 4.7 %collective-permute-done.5 = f32[2,48,128]{2,1,0:T(8,128)S(1)} collective-permute-done((f32[2,48,128]{2,1,0:T(8,128)S(1)}, f32[2,48,128]{2,1,0:T(8,128)S(1)}, u32[]{:S(2)}, u32[]{:S(2)}) %collective-permute-start.5) | collective-permute-done | bytes 49184 | tf_op jit(solution)/shard_map/ppermute | solution.py:19
  68.3 4.3 %collective-permute-start.6 = (f32[1,48,128]{2,1,0:T(8,128)S(1)}, f32[1,48,128]{2,1,0:T(8,128)S(1)}, u32[]{:S(2)}, u32[]{:S(2)}) collective-permute-start(f32[1,48,128]{2,1,0:T(8,128)S(1)} %constant_dynamic-slice_fusion), channel_id=1, source_target_pairs={{0,16},{1,17},{2,18},{3,19},{4,20},{5,21},{6,22},{7,23},{8,24},{9,... | collective-permute-start | bytes 73736 | tf_op jit(solution)/shard_map/ppermute | solution.py:19
  72.6 0.2 fusion.16
  72.9 12.7 %collective-permute-done.6 = f32[1,48,128]{2,1,0:T(8,128)S(1)} collective-permute-done((f32[1,48,128]{2,1,0:T(8,128)S(1)}, f32[1,48,128]{2,1,0:T(8,128)S(1)}, u32[]{:S(2)}, u32[]{:S(2)}) %collective-permute-start.6) | collective-permute-done | bytes 24608 | tf_op jit(solution)/shard_map/ppermute | solution.py:19
  85.5 0.6 reshape.142
  86.1 22.4 %all-to-all-done = bf16[16,32,2048]{2,1,0:T(8,128)(2,1)} async-done(((bf16[16,32,2048]{2,1,0:T(8,128)(2,1)}), bf16[16,32,2048]{2,1,0:T(8,128)(2,1)}, u32[]{:S(2)}, u32[]{:S(2)}) %all-to-all-start) | async-done | bytes 2097184 | tf_op jit(solution)/shard_map/all_to_all | solution.py:62
  108.6 2.1 %convolution_convert_fusion = bf16[48,2048]{1,0:T(8,128)(2,1)S(1)} fusion(bf16[512,2048]{1,0:T(8,128)(2,1)} %bitcast.8, bf16[96,512]{1,0:T(8,128)(2,1)S(1)} %fusion.16), kind=kOutput, calls=%fused_computation.8 | convolution fusion | flops 100761600 | bytes 2342912 | tf_op jit(solution)/shard_map/dot_general | solution.py:72
  110.6 1.9 %collective-permute-start.1 = (bf16[48,2048]{1,0:T(8,128)(2,1)S(1)}, bf16[48,2048]{1,0:T(8,128)(2,1)S(1)}, u32[]{:S(2)}, u32[]{:S(2)}) collective-permute-start(bf16[48,2048]{1,0:T(8,128)(2,1)S(1)} %convolution_convert_fusion), channel_id=1, source_target_pairs={{0,32},{32,0},{64,96},{96,64},{128,160},{160,128},{192,224},{224,1... | collective-permute-start | bytes 589832 | tf_op jit(solution)/shard_map/ppermute | solution.py:73
  112.6 2.1 %fusion.18 = f32[48,2048]{1,0:T(8,128)S(1)} fusion(bf16[512,2048]{1,0:T(8,128)(2,1)} %bitcast.8, bf16[96,512]{1,0:T(8,128)(2,1)S(1)} %fusion.16), kind=kOutput, calls=%fused_computation.30 | convolution fusion | flops 100663296 | bytes 2539520 | tf_op jit(solution)/shard_map/dot_general | solution.py:74
  114.6 3.6 %collective-permute-done.1 = bf16[48,2048]{1,0:T(8,128)(2,1)S(1)} collective-permute-done((bf16[48,2048]{1,0:T(8,128)(2,1)S(1)}, bf16[48,2048]{1,0:T(8,128)(2,1)S(1)}, u32[]{:S(2)}, u32[]{:S(2)}) %collective-permute-start.1) | collective-permute-done | bytes 196640 | tf_op jit(solution)/shard_map/ppermute | solution.py:73
  118.2 0.7 add_convert_fusion.1
  (21 shorter events, 0.2 us)
Async XLA Ops:
  0.6 5.4 %copy-start = (bf16[1,2048,768]{2,1,0:T(8,128)(2,1)S(1)}, bf16[1,2048,768]{2,1,0:T(8,128)(2,1)}, u32[]{:S(2)}) copy-start(bf16[1,2048,768]{2,1,0:T(8,128)(2,1)} %param.12) | copy-start | bytes 9437188
  0.6 10.4 %collective-permute-start = (s32[48,8]{0,1:T(8,128)}, s32[48,8]{0,1:T(8,128)S(1)}, u32[]{:S(2)}, u32[]{:S(2)}) collective-permute-start(s32[48,8]{0,1:T(8,128)} %param.7), channel_id=1, source_target_pairs={{0,32},{32,0},{64,96},{96,64},{128,160},{160,128},{192,224},{224,1... | collective-permute-start | bytes 4616 | tf_op jit(solution)/shard_map/ppermute | solution.py:60
  6.0 1.9 %copy-start.2 = (bf16[1,2048,768]{2,1,0:T(8,128)(2,1)S(1)}, bf16[1,2048,768]{2,1,0:T(8,128)(2,1)}, u32[]{:S(2)}) copy-start(bf16[1,2048,768]{2,1,0:T(8,128)(2,1)} %param.11) | copy-start | bytes 9437188
  11.0 97.5 %all-to-all-start = ((bf16[16,32,2048]{2,1,0:T(8,128)(2,1)}), bf16[16,32,2048]{2,1,0:T(8,128)(2,1)}, u32[]{:S(2)}, u32[]{:S(2)}) async-start(bf16[16,32,2048]{2,1,0:T(8,128)(2,1)} %bitcast.46), calls=%async_computation | async-start | bytes 4194304 | tf_op jit(solution)/shard_map/all_to_all | solution.py:62
  33.8 18.0 %copy-start.1 = (s32[48,8]{0,1:T(8,128)S(1)}, s32[48,8]{0,1:T(8,128)}, u32[]{:S(2)}) copy-start(s32[48,8]{0,1:T(8,128)} %param.7) | copy-start | bytes 4612
  35.6 3.8 %collective-permute-start.2 = (f32[16,48,128]{2,1,0:T(8,128)}, f32[16,48,128]{2,1,0:T(8,128)S(1)}, u32[]{:S(2)}, u32[]{:S(2)}) collective-permute-start(f32[16,48,128]{2,1,0:T(8,128)} %dynamic-slice_bitcast_fusion), channel_id=1, source_target_pairs={{0,1},{1,0},{2,3},{3,2},{4,5},{5,4},{6,7},{7,6},{8,9},{9,8},{10,11... | collective-permute-start | bytes 1179656 | tf_op jit(solution)/shard_map/ppermute | solution.py:19
  40.5 8.8 %collective-permute-start.3 = (f32[8,48,128]{2,1,0:T(8,128)S(1)}, f32[8,48,128]{2,1,0:T(8,128)S(1)}, u32[]{:S(2)}, u32[]{:S(2)}) collective-permute-start(f32[8,48,128]{2,1,0:T(8,128)S(1)} %dynamic-slice_bitcast_fusion.1), channel_id=1, source_target_pairs={{0,2},{1,3},{2,0},{3,1},{4,6},{5,7},{6,4},{7,5},{8,10},{9,11},{10,... | collective-permute-start | bytes 589832 | tf_op jit(solution)/shard_map/ppermute | solution.py:19
  49.4 9.0 %collective-permute-start.4 = (f32[4,48,128]{2,1,0:T(8,128)S(1)}, f32[4,48,128]{2,1,0:T(8,128)S(1)}, u32[]{:S(2)}, u32[]{:S(2)}) collective-permute-start(f32[4,48,128]{2,1,0:T(8,128)S(1)} %dynamic-slice_bitcast_fusion.2), channel_id=1, source_target_pairs={{0,4},{1,5},{2,6},{3,7},{4,0},{5,1},{6,2},{7,3},{8,12},{9,13},{10,... | collective-permute-start | bytes 294920 | tf_op jit(solution)/shard_map/ppermute | solution.py:19
  58.4 9.9 %collective-permute-start.5 = (f32[2,48,128]{2,1,0:T(8,128)S(1)}, f32[2,48,128]{2,1,0:T(8,128)S(1)}, u32[]{:S(2)}, u32[]{:S(2)}) collective-permute-start(f32[2,48,128]{2,1,0:T(8,128)S(1)} %dynamic-slice_bitcast_fusion.3), channel_id=1, source_target_pairs={{0,8},{1,9},{2,10},{3,11},{4,12},{5,13},{6,14},{7,15},{8,0},{9,1},... | collective-permute-start | bytes 147464 | tf_op jit(solution)/shard_map/ppermute | solution.py:19
  68.3 17.2 %collective-permute-start.6 = (f32[1,48,128]{2,1,0:T(8,128)S(1)}, f32[1,48,128]{2,1,0:T(8,128)S(1)}, u32[]{:S(2)}, u32[]{:S(2)}) collective-permute-start(f32[1,48,128]{2,1,0:T(8,128)S(1)} %constant_dynamic-slice_fusion), channel_id=1, source_target_pairs={{0,16},{1,17},{2,18},{3,19},{4,20},{5,21},{6,22},{7,23},{8,24},{9,... | collective-permute-start | bytes 73736 | tf_op jit(solution)/shard_map/ppermute | solution.py:19
  110.6 7.6 %collective-permute-start.1 = (bf16[48,2048]{1,0:T(8,128)(2,1)S(1)}, bf16[48,2048]{1,0:T(8,128)(2,1)S(1)}, u32[]{:S(2)}, u32[]{:S(2)}) collective-permute-start(bf16[48,2048]{1,0:T(8,128)(2,1)S(1)} %convolution_convert_fusion), channel_id=1, source_target_pairs={{0,32},{32,0},{64,96},{96,64},{128,160},{160,128},{192,224},{224,1... | collective-permute-start | bytes 589832 | tf_op jit(solution)/shard_map/ppermute | solution.py:73

commit v9 on v3

--- a/solution.py
+++ b/solution.py
@@ -5,8 +5,6 @@
 from jax.experimental.pallas import tpu as pltpu
 from jax.sharding import PartitionSpec as P
 
-BOTH = ("ep", "edp")
-GROUP = 16
 CHUNKS = 4
 HALVES = 2
 
@@ -28,34 +26,10 @@
     return part.reshape(1, rows // members, width)
 
 
-def place(core, member, rest):
-    across = rest * GROUP + member
-    along = (member // 4) * 8 + rest * 4 + member % 4
-    return across + core * (along - across)
-
-
-def groups(members):
-    return [
-        [place(j % 2, g, r) * members + j for g in range(GROUP)]
-        for j in range(members)
-        for r in range(2)
-    ]
-
-
-def partners(members):
-    return [
-        (place(j % 2, g, r) * members + j, place(j % 2, g, 1 - r) * members + j)
-        for j in range(members)
-        for g in range(GROUP)
-        for r in range(2)
-    ]
-
-
 def row_kernel(
-    core_ref, gate_hbm, up_hbm, grad_hbm, w_gate_hbm, w_up_hbm, out_hbm,
+    gate_hbm, up_hbm, grad_hbm, w_gate_hbm, w_up_hbm, out_hbm,
     gate, up, grad, weight, packed, rows, in_sem, weight_sem, out_sem,
 ):
-    core = core_ref[0]
     sources, capacity, hidden = gate.shape
     width = weight.shape[0]
     some, tile = sources // CHUNKS, width // HALVES
@@ -80,10 +54,7 @@
             grad_f = grad[s].astype(jnp.float32)
             sig = 0.5 + 0.5 * jnp.tanh(0.5 * gate_f)
             scaled = grad_f * sig
-            across = s % GROUP * 2 + s // GROUP
-            along = (s // 8 * 4 + s % 4) * 2 + s // 4 % 2
-            position = jnp.where(core == 0, across, along)
-            to = pl.ds(pl.multiple_of(position * capacity, capacity), capacity)
+            to = pl.ds(s * capacity, capacity)
             packed[to, :hidden] = (scaled * up_f * (1.0 + gate_f * (1.0 - sig))).astype(jnp.bfloat16)
             packed[to, hidden:] = (scaled * gate_f).astype(jnp.bfloat16)
     for n in range(HALVES):
@@ -103,14 +74,14 @@
         copy.wait()
 
 
-def send_rows(core, gate, up, grad, w_gate, w_up):
+def send_rows(gate, up, grad, w_gate, w_up):
     sources, capacity, hidden = gate.shape
     width = w_gate.shape[0]
     anywhere = pl.BlockSpec(memory_space=pl.ANY)
     held = pltpu.VMEM((sources, capacity, hidden), jnp.bfloat16)
     return pl.pallas_call(
         row_kernel,
-        in_specs=[pl.BlockSpec(memory_space=pltpu.SMEM)] + [anywhere] * 5,
+        in_specs=[anywhere] * 5,
         out_specs=anywhere,
         scratch_shapes=[
             held,
@@ -130,51 +101,30 @@
             bytes_accessed=6 * sources * capacity * hidden + 4 * hidden * width + 2 * sources * capacity * width,
             transcendentals=sources * capacity * hidden,
         ),
-    )(core.reshape(1), gate, up, grad, w_gate, w_up)
+    )(gate, up, grad, w_gate, w_up)
 
 
-def choice(routes, core, rest, capacity):
-    tokens = routes.shape[1]
-    named = place(core, jnp.arange(GROUP, dtype=jnp.int32), rest)
-    matches = (routes[:, :, :, None] == named).any(axis=2)
+def choice(routes, experts, capacity):
+    named = jnp.arange(experts, dtype=jnp.int32)
+    matches = (routes[:, :, None] == named).any(axis=1)
     count = matches.astype(jnp.int32)
-    earlier = jnp.cumsum(count, axis=1) - count
-    slot = jnp.where(matches, earlier, -1).reshape(2 * tokens, GROUP).astype(jnp.bfloat16)
-    column = jnp.arange(GROUP * 2 * capacity, dtype=jnp.int32)
-    spread = column[None, :] // (2 * capacity) == jnp.arange(GROUP, dtype=jnp.int32)[:, None]
+    earlier = jnp.cumsum(count, axis=0) - count
+    slot = jnp.where(matches, earlier, -1).astype(jnp.bfloat16)
+    column = jnp.arange(experts * capacity, dtype=jnp.int32)
+    spread = column[None, :] // capacity == named[:, None]
     slots = jnp.dot(slot, spread.astype(jnp.bfloat16), preferred_element_type=jnp.float32)
-    second = jnp.arange(2 * tokens, dtype=jnp.int32)[:, None] // tokens
-    owner = jnp.where(second == 0, 1 - rest, rest)
-    same = owner == (column // capacity % 2)[None, :]
-    chosen = same & (slots == (column % capacity).astype(jnp.float32)[None, :])
-    return chosen.astype(jnp.bfloat16)
+    return (slots == (column % capacity).astype(jnp.float32)[None, :]).astype(jnp.bfloat16)
 
 
 def shards(routes, gate_pre, up_pre, hidden_grad, w_gate, w_up, bucket_terms):
-    members = lax.axis_size("edp")
     experts, capacity = gate_pre.shape[2:4]
-    tokens = routes.shape[0]
     width = w_gate.shape[1]
-    core = lax.axis_index("edp") % 2
-    own = lax.axis_index("ep")
-    rest = jnp.where(core == 0, own // GROUP, own // 4 % 2)
-    swap = partners(members)
-    rows = send_rows(core, gate_pre[0, 0], up_pre[0, 0], hidden_grad[0, 0], w_gate[0], w_up[0])
+    rows = send_rows(gate_pre[0, 0], up_pre[0, 0], hidden_grad[0, 0], w_gate[0], w_up[0])
     arrived = lax.all_to_all(
-        rows.reshape(GROUP, 2 * capacity, width),
-        BOTH,
-        split_axis=0,
-        concat_axis=0,
-        axis_index_groups=groups(members),
-        tiled=True,
+        rows.reshape(experts, capacity, width), "ep", split_axis=0, concat_axis=0, tiled=True
     ).reshape(experts * capacity, width)
-    theirs = lax.ppermute(routes, BOTH, swap)
-    chosen = choice(jnp.stack([theirs, routes]), core, rest, capacity)
-    chosen = lax.optimization_barrier(chosen)
-    given = jnp.dot(chosen[:tokens], arrived, preferred_element_type=jnp.float32)
-    got = lax.ppermute(given.astype(jnp.bfloat16), BOTH, swap)
-    kept = jnp.dot(chosen[tokens:], arrived, preferred_element_type=jnp.float32)
-    token_grad = (kept + got.astype(jnp.float32)).astype(jnp.bfloat16)
+    chosen = lax.optimization_barrier(choice(routes, experts, capacity))
+    token_grad = jnp.dot(chosen, arrived, preferred_element_type=jnp.float32).astype(jnp.bfloat16)
     reduced = reduce_bucket(bucket_terms[0, 0])
     return (token_grad, reduced)
 

time: 109 us -> 106 us (0.972)
  starting transfers between devices: 46.7 us -> 45 us
    ppermute x2 -> x0, waiting for transfers between devices: 38.4 us -> none  [the longest x1 35.9 us: shards(): theirs = lax.ppermute(routes, BOTH, swap)]
    all_to_all x1, waiting for transfers between devices: 0.01 us -> 33.6 us  [shards(): lax.all_to_all(rows.reshape(experts, capacity, width), 'ep', split_axis=0...]
    ppermute x2 -> x0, starting transfers between devices: 13.5 us -> none  [the longest x1 8.11 us: shards(): got = lax.ppermute(given.astype(jnp.bfloat16), BOTH, swap)]
    ppermute x5, starting transfers between devices: 13.4 us -> 22.6 us  [reduce_bucket(): part = kept + lax.ppermute(given, 'edp', swap)]
    ppermute x5, waiting for transfers between devices: 7.96 us -> 12.7 us  [reduce_bucket(): part = kept + lax.ppermute(given, 'edp', swap)]
    all_to_all x1, starting transfers between devices: 19.8 us -> 22.4 us  [shards(): lax.all_to_all(rows.reshape(experts, capacity, width), 'ep', split_axis=0...]
  transfers between devices with their start and end apart: 8 -> 6, of which waited for: 4 -> 6; matrix products, arithmetic and copies ran while one was open for 4% -> 3% of each run, Pallas kernels for 0% -> 0%
where the time goes in v9:
time: 106 us; the launch traced here: 105 us
  waiting for transfers between devices  46.3 us (44%)
  starting transfers between devices  45 us (42%)
  Pallas kernels  8.07 us (8%)
  local copies, waits for them, and re-layouts  2.01 us (2%)
  matrix products  1.3 us (1%)
  other arithmetic  1.22 us (1%)
    all_to_all x1, waiting for transfers between devices, shards(): lax.all_to_all(rows.reshape(experts, capacity, width), 'ep', split_axis=0...  33.6 us
    ppermute x5, starting transfers between devices, reduce_bucket(): part = kept + lax.ppermute(given, 'edp', swap)  22.6 us
    all_to_all x1, starting transfers between devices, shards(): lax.all_to_all(rows.reshape(experts, capacity, width), 'ep', split_axis=0...  22.4 us
    ppermute x5, waiting for transfers between devices, reduce_bucket(): part = kept + lax.ppermute(given, 'edp', swap)  12.7 us
    pallas_call x1, Pallas kernels, send_rows(): pl.pallas_call(row_kernel, in_specs=[anywhere] * 5, out_specs=anywhere, s...  8.07 us
  transfers between devices with their start and end apart: 6, of which 6 were waited for; matrix products, arithmetic and copies ran while one was open for 3% of the time, Pallas kernels for 0%

profile of v9, /device:TPU:1, one launch (start us, length us, event | category | flops | bytes accessed | tf_op | source)
XLA Modules:
  0.0 104.9 jit_solution(8297206297102251963)
XLA Ops:
  0.6 8.1 %shard_map.86 = bf16[512,2048]{1,0:T(8,128)(2,1)} custom-call(bf16[32,16,768]{2,1,0:T(8,128)(2,1)} %bitcast.44, bf16[32,16,768]{2,1,0:T(8,128)(2,1)} %bitcast.45, bf16[32,16,768]{2,1,0:T(8,128)(2,1)} %bitcast.46, bf16[2048,768]{1,0:T(8,128)(2,1)} %bitcast.42, bf16[2048,768]{1,0:T(8,128)(2,1)} %bitcast.43), custom_call_target="tpu_custom_call" | custom-call | flops 3221225472 | bytes 10747904 | tf_op jit(solution)/shard_map/pallas_call | solution.py:82
  8.7 22.4 %all-to-all-start = ((bf16[32,16,2048]{2,1,0:T(8,128)(2,1)}), bf16[32,16,2048]{2,1,0:T(8,128)(2,1)S(1)}, u32[]{:S(2)}, u32[]{:S(2)}) async-start(bf16[32,16,2048]{2,1,0:T(8,128)(2,1)} %bitcast.35), calls=%async_computation | async-start | bytes 4194304 | tf_op jit(solution)/shard_map/all_to_all | solution.py:123
  31.2 0.0 copy-start
  31.2 1.2 %reshape_reshape_squeeze.3 = f32[16,2,48,128]{3,2,1,0:T(8,128)S(1)} reshape(f32[1,1,128,1536]{3,2,1,0:T(8,128)} %param.13) | data formatting | bytes 1572864 | tf_op jit(solution)/shard_map/reshape;reshape;squeeze | solution.py:19
  32.4 2.9 %collective-permute-start = (f32[16,48,128]{2,1,0:T(8,128)S(1)}, f32[16,48,128]{2,1,0:T(8,128)}, u32[]{:S(2)}, u32[]{:S(2)}) collective-permute-start(f32[16,48,128]{2,1,0:T(8,128)S(1)} %dynamic-slice_bitcast_fusion), channel_id=1, source_target_pairs={{0,1},{1,0},{2,3},{3,2},{4,5},{5,4},{6,7},{7,6},{8,9},{9,8},{10,11... | collective-permute-start | bytes 1179656 | tf_op jit(solution)/shard_map/ppermute | solution.py:24
  35.3 1.4 %collective-permute-done = f32[16,48,128]{2,1,0:T(8,128)} collective-permute-done((f32[16,48,128]{2,1,0:T(8,128)S(1)}, f32[16,48,128]{2,1,0:T(8,128)}, u32[]{:S(2)}, u32[]{:S(2)}) %collective-permute-start) | collective-permute-done | bytes 393248 | tf_op jit(solution)/shard_map/ppermute | solution.py:24
  36.8 1.1 %bitcast_add_fusion = f32[16,48,128]{2,1,0:T(8,128)S(1)} fusion(f32[16,48,128]{2,1,0:T(8,128)} %collective-permute-done, f32[16,2,48,128]{3,2,1,0:T(8,128)S(1)} %reshape_reshape_squeeze.3, s32[]{:T(128)S(6)} %select_n.100), kind=kLoop, calls=%fused_computation.3 | loop fusion | flops 98304 | bytes 1179652 | tf_op jit(solution)/shard_map/add | solution.py:24
  37.8 3.1 %collective-permute-start.1 = (f32[8,48,128]{2,1,0:T(8,128)S(1)}, f32[8,48,128]{2,1,0:T(8,128)S(1)}, u32[]{:S(2)}, u32[]{:S(2)}) collective-permute-start(f32[8,48,128]{2,1,0:T(8,128)S(1)} %dynamic-slice_bitcast_fusion.1), channel_id=1, source_target_pairs={{0,2},{1,3},{2,0},{3,1},{4,6},{5,7},{6,4},{7,5},{8,10},{9,11},{10,... | collective-permute-start | bytes 589832 | tf_op jit(solution)/shard_map/ppermute | solution.py:24
  41.0 4.8 %collective-permute-done.1 = f32[8,48,128]{2,1,0:T(8,128)S(1)} collective-permute-done((f32[8,48,128]{2,1,0:T(8,128)S(1)}, f32[8,48,128]{2,1,0:T(8,128)S(1)}, u32[]{:S(2)}, u32[]{:S(2)}) %collective-permute-start.1) | collective-permute-done | bytes 196640 | tf_op jit(solution)/shard_map/ppermute | solution.py:24
  45.9 4.0 %collective-permute-start.2 = (f32[4,48,128]{2,1,0:T(8,128)S(1)}, f32[4,48,128]{2,1,0:T(8,128)S(1)}, u32[]{:S(2)}, u32[]{:S(2)}) collective-permute-start(f32[4,48,128]{2,1,0:T(8,128)S(1)} %dynamic-slice_bitcast_fusion.2), channel_id=1, source_target_pairs={{0,4},{1,5},{2,6},{3,7},{4,0},{5,1},{6,2},{7,3},{8,12},{9,13},{10,... | collective-permute-start | bytes 294920 | tf_op jit(solution)/shard_map/ppermute | solution.py:24
  50.0 0.0 copy-done
  50.0 3.5 %collective-permute-done.2 = f32[4,48,128]{2,1,0:T(8,128)S(1)} collective-permute-done((f32[4,48,128]{2,1,0:T(8,128)S(1)}, f32[4,48,128]{2,1,0:T(8,128)S(1)}, u32[]{:S(2)}, u32[]{:S(2)}) %collective-permute-start.2) | collective-permute-done | bytes 98336 | tf_op jit(solution)/shard_map/ppermute | solution.py:24
  53.6 8.6 %collective-permute-start.3 = (f32[2,48,128]{2,1,0:T(8,128)S(1)}, f32[2,48,128]{2,1,0:T(8,128)S(1)}, u32[]{:S(2)}, u32[]{:S(2)}) collective-permute-start(f32[2,48,128]{2,1,0:T(8,128)S(1)} %dynamic-slice_bitcast_fusion.3), channel_id=1, source_target_pairs={{0,8},{1,9},{2,10},{3,11},{4,12},{5,13},{6,14},{7,15},{8,0},{9,1},... | collective-permute-start | bytes 147464 | tf_op jit(solution)/shard_map/ppermute | solution.py:24
  62.2 0.1 copy.16
  62.3 0.1 reduce_window_sum.11
  62.4 1.3 %collective-permute-done.3 = f32[2,48,128]{2,1,0:T(8,128)S(1)} collective-permute-done((f32[2,48,128]{2,1,0:T(8,128)S(1)}, f32[2,48,128]{2,1,0:T(8,128)S(1)}, u32[]{:S(2)}, u32[]{:S(2)}) %collective-permute-start.3) | collective-permute-done | bytes 49184 | tf_op jit(solution)/shard_map/ppermute | solution.py:24
  63.6 4.0 %collective-permute-start.4 = (f32[1,48,128]{2,1,0:T(8,128)S(1)}, f32[1,48,128]{2,1,0:T(8,128)S(1)}, u32[]{:S(2)}, u32[]{:S(2)}) collective-permute-start(f32[1,48,128]{2,1,0:T(8,128)S(1)} %constant_dynamic-slice_fusion), channel_id=1, source_target_pairs={{0,16},{1,17},{2,18},{3,19},{4,20},{5,21},{6,22},{7,23},{8,24},{9,... | collective-permute-start | bytes 73736 | tf_op jit(solution)/shard_map/ppermute | solution.py:24
  67.6 0.1 fusion
  67.8 1.7 %collective-permute-done.4 = f32[1,48,128]{2,1,0:T(8,128)S(1)} collective-permute-done((f32[1,48,128]{2,1,0:T(8,128)S(1)}, f32[1,48,128]{2,1,0:T(8,128)S(1)}, u32[]{:S(2)}, u32[]{:S(2)}) %collective-permute-start.4) | collective-permute-done | bytes 24608 | tf_op jit(solution)/shard_map/ppermute | solution.py:24
  69.5 0.6 reshape.80
  70.1 33.6 %all-to-all-done = bf16[32,16,2048]{2,1,0:T(8,128)(2,1)S(1)} async-done(((bf16[32,16,2048]{2,1,0:T(8,128)(2,1)}), bf16[32,16,2048]{2,1,0:T(8,128)(2,1)S(1)}, u32[]{:S(2)}, u32[]{:S(2)}) %all-to-all-start) | async-done | bytes 2097184 | tf_op jit(solution)/shard_map/all_to_all | solution.py:123
  103.8 1.2 %convolution_convert_fusion = bf16[48,2048]{1,0:T(8,128)(2,1)} fusion(bf16[48,512]{1,0:T(8,128)(2,1)S(1)} %fusion, bf16[512,2048]{1,0:T(8,128)(2,1)S(1)} %bitcast.34), kind=kOutput, calls=%fused_computation | convolution fusion | flops 100761600 | bytes 2342912 | tf_op jit(solution)/shard_map/dot_general | solution.py:127
  (12 shorter events, 0.2 us)
Async XLA Ops:
  8.7 95.0 %all-to-all-start = ((bf16[32,16,2048]{2,1,0:T(8,128)(2,1)}), bf16[32,16,2048]{2,1,0:T(8,128)(2,1)S(1)}, u32[]{:S(2)}, u32[]{:S(2)}) async-start(bf16[32,16,2048]{2,1,0:T(8,128)(2,1)} %bitcast.35), calls=%async_computation | async-start | bytes 4194304 | tf_op jit(solution)/shard_map/all_to_all | solution.py:123
  31.2 18.8 %copy-start = (s32[48,8]{0,1:T(8,128)S(1)}, s32[48,8]{0,1:T(8,128)}, u32[]{:S(2)}) copy-start(s32[48,8]{0,1:T(8,128)} %param.7) | copy-start | bytes 4612
  32.4 4.3 %collective-permute-start = (f32[16,48,128]{2,1,0:T(8,128)S(1)}, f32[16,48,128]{2,1,0:T(8,128)}, u32[]{:S(2)}, u32[]{:S(2)}) collective-permute-start(f32[16,48,128]{2,1,0:T(8,128)S(1)} %dynamic-slice_bitcast_fusion), channel_id=1, source_target_pairs={{0,1},{1,0},{2,3},{3,2},{4,5},{5,4},{6,7},{7,6},{8,9},{9,8},{10,11... | collective-permute-start | bytes 1179656 | tf_op jit(solution)/shard_map/ppermute | solution.py:24
  37.8 8.0 %collective-permute-start.1 = (f32[8,48,128]{2,1,0:T(8,128)S(1)}, f32[8,48,128]{2,1,0:T(8,128)S(1)}, u32[]{:S(2)}, u32[]{:S(2)}) collective-permute-start(f32[8,48,128]{2,1,0:T(8,128)S(1)} %dynamic-slice_bitcast_fusion.1), channel_id=1, source_target_pairs={{0,2},{1,3},{2,0},{3,1},{4,6},{5,7},{6,4},{7,5},{8,10},{9,11},{10,... | collective-permute-start | bytes 589832 | tf_op jit(solution)/shard_map/ppermute | solution.py:24
  45.9 7.6 %collective-permute-start.2 = (f32[4,48,128]{2,1,0:T(8,128)S(1)}, f32[4,48,128]{2,1,0:T(8,128)S(1)}, u32[]{:S(2)}, u32[]{:S(2)}) collective-permute-start(f32[4,48,128]{2,1,0:T(8,128)S(1)} %dynamic-slice_bitcast_fusion.2), channel_id=1, source_target_pairs={{0,4},{1,5},{2,6},{3,7},{4,0},{5,1},{6,2},{7,3},{8,12},{9,13},{10,... | collective-permute-start | bytes 294920 | tf_op jit(solution)/shard_map/ppermute | solution.py:24
  53.6 10.0 %collective-permute-start.3 = (f32[2,48,128]{2,1,0:T(8,128)S(1)}, f32[2,48,128]{2,1,0:T(8,128)S(1)}, u32[]{:S(2)}, u32[]{:S(2)}) collective-permute-start(f32[2,48,128]{2,1,0:T(8,128)S(1)} %dynamic-slice_bitcast_fusion.3), channel_id=1, source_target_pairs={{0,8},{1,9},{2,10},{3,11},{4,12},{5,13},{6,14},{7,15},{8,0},{9,1},... | collective-permute-start | bytes 147464 | tf_op jit(solution)/shard_map/ppermute | solution.py:24
  63.6 5.9 %collective-permute-start.4 = (f32[1,48,128]{2,1,0:T(8,128)S(1)}, f32[1,48,128]{2,1,0:T(8,128)S(1)}, u32[]{:S(2)}, u32[]{:S(2)}) collective-permute-start(f32[1,48,128]{2,1,0:T(8,128)S(1)} %constant_dynamic-slice_fusion), channel_id=1, source_target_pairs={{0,16},{1,17},{2,18},{3,19},{4,20},{5,21},{6,22},{7,23},{8,24},{9,... | collective-permute-start | bytes 73736 | tf_op jit(solution)/shard_map/ppermute | solution.py:24

commit v10 on v4

--- a/solution.py
+++ b/solution.py
@@ -175,6 +175,7 @@
     given = jnp.dot(chosen[:tokens], arrived, preferred_element_type=jnp.float32)
     got = lax.ppermute(given.astype(jnp.bfloat16), BOTH, swap)
     kept = jnp.dot(chosen[tokens:], arrived, preferred_element_type=jnp.float32)
+    kept = lax.optimization_barrier(kept)
     token_grad = (kept + got.astype(jnp.float32)).astype(jnp.bfloat16)
     reduced = reduce_bucket(bucket_terms[0, 0])
     return (token_grad, reduced)

time: 102 us -> 101 us (level)
  the two profiles are of different devices: /device:TPU:476 before, /device:TPU:472 now
where the time goes in v10:
time: 101 us
  waiting for transfers between devices  52.9 us (52%)
  starting transfers between devices  33.8 us (33%)
  Pallas kernels  8.08 us (8%)
  local copies, waits for them, and re-layouts  2.88 us (3%)
  matrix products  1.16 us (1%)
  between operations  1.05 us (1%)
  other arithmetic  1.02 us (1%)
    ppermute x5, waiting for transfers between devices, reduce_bucket(): part = kept + lax.ppermute(given, 'edp', swap)  26.8 us
    all_to_all x1, waiting for transfers between devices, shards(): lax.all_to_all(rows.reshape(GROUP, 2 * capacity, width), BOTH, split_axis...  17.1 us
    ppermute x1, starting transfers between devices, shards(): theirs = lax.ppermute(routes, BOTH, swap)  11.9 us
    ppermute x5, starting transfers between devices, reduce_bucket(): part = kept + lax.ppermute(given, 'edp', swap)  11.2 us
    ppermute x1, waiting for transfers between devices, shards(): got = lax.ppermute(given.astype(jnp.bfloat16), BOTH, swap)  9.07 us
    all_to_all x1, starting transfers between devices, shards(): lax.all_to_all(rows.reshape(GROUP, 2 * capacity, width), BOTH, split_axis...  8.81 us
    pallas_call x1, Pallas kernels, send_rows(): pl.pallas_call(row_kernel, in_specs=[pl.BlockSpec(memory_space=pltpu.SMEM...  8.08 us
  transfers between devices with their start and end apart: 8, of which 7 were waited for; matrix products, arithmetic and copies ran while one was open for 4% of the time, Pallas kernels for 8%

profile of v10, /device:TPU:472, one launch (start us, length us, event | category | flops | bytes accessed | tf_op | source)
XLA Modules:
  0.0 100.9 jit_solution(16462422384635016545)
XLA Ops:
  0.6 11.9 %collective-permute-start = (s32[48,8]{0,1:T(8,128)}, s32[48,8]{0,1:T(8,128)S(1)}, u32[]{:S(2)}, u32[]{:S(2)}) collective-permute-start(s32[48,8]{0,1:T(8,128)} %param.7), channel_id=1, source_target_pairs={{0,512},{512,0},{32,544},{544,32},{64,576},{576,64},{96,608},{608,... | collective-permute-start | bytes 4616 | tf_op jit(solution)/shard_map/ppermute | solution.py:163
  12.5 8.1 %shard_map.86 = bf16[512,2048]{1,0:T(8,128)(2,1)} custom-call(s32[1]{0:T(128)} %bitcast.core_ref, bf16[32,16,768]{2,1,0:T(8,128)(2,1)} %bitcast.54, bf16[32,16,768]{2,1,0:T(8,128)(2,1)} %bitcast.55, bf16[32,16,768]{2,1,0:T(8,128)(2,1)} %bitcast.56, bf16[2048,768]{1,0:T(8,128)(2,1)} %bitcast.52, bf16[2048,768]{1,0:T(8,128)(2,1)} %bitcast.53), custom_call_target="tpu_custom_call" | custom-call | flops 3221225472 | bytes 10747904 | tf_op jit(solution)/shard_map/pallas_call | solution.py:111
  20.6 0.0 collective-permute-done
  20.6 8.8 %all-to-all-start = ((bf16[16,32,2048]{2,1,0:T(8,128)(2,1)}), bf16[16,32,2048]{2,1,0:T(8,128)(2,1)S(1)}, u32[]{:S(2)}, u32[]{:S(2)}) async-start(bf16[16,32,2048]{2,1,0:T(8,128)(2,1)} %bitcast.42), calls=%async_computation | async-start | bytes 4194304 | tf_op jit(solution)/shard_map/all_to_all | solution.py:165
  29.4 1.2 %reshape_reshape_squeeze.3 = f32[16,2,48,128]{3,2,1,0:T(8,128)S(1)} reshape(f32[1,1,128,1536]{3,2,1,0:T(8,128)} %param.13) | data formatting | bytes 1572864 | tf_op jit(solution)/shard_map/reshape;reshape;squeeze | solution.py:21
  30.6 0.0 copy-start
  30.6 0.8 dynamic-slice_bitcast_fusion
  31.4 1.9 %collective-permute-start.2 = (f32[16,48,128]{2,1,0:T(8,128)}, f32[16,48,128]{2,1,0:T(8,128)S(1)}, u32[]{:S(2)}, u32[]{:S(2)}) collective-permute-start(f32[16,48,128]{2,1,0:T(8,128)} %dynamic-slice_bitcast_fusion), channel_id=1, source_target_pairs={{0,1},{1,0},{2,3},{3,2},{4,5},{5,4},{6,7},{7,6},{8,9},{9,8},{10,11... | collective-permute-start | bytes 1179656 | tf_op jit(solution)/shard_map/ppermute | solution.py:26
  33.5 1.7 %collective-permute-done.2 = f32[16,48,128]{2,1,0:T(8,128)S(1)} collective-permute-done((f32[16,48,128]{2,1,0:T(8,128)}, f32[16,48,128]{2,1,0:T(8,128)S(1)}, u32[]{:S(2)}, u32[]{:S(2)}) %collective-permute-start.2) | collective-permute-done | bytes 393248 | tf_op jit(solution)/shard_map/ppermute | solution.py:26
  35.3 2.5 %collective-permute-start.3 = (f32[8,48,128]{2,1,0:T(8,128)S(1)}, f32[8,48,128]{2,1,0:T(8,128)S(1)}, u32[]{:S(2)}, u32[]{:S(2)}) collective-permute-start(f32[8,48,128]{2,1,0:T(8,128)S(1)} %dynamic-slice_bitcast_fusion.1), channel_id=1, source_target_pairs={{0,2},{1,3},{2,0},{3,1},{4,6},{5,7},{6,4},{7,5},{8,10},{9,11},{10,... | collective-permute-start | bytes 589832 | tf_op jit(solution)/shard_map/ppermute | solution.py:26
  37.8 6.3 %collective-permute-done.3 = f32[8,48,128]{2,1,0:T(8,128)S(1)} collective-permute-done((f32[8,48,128]{2,1,0:T(8,128)S(1)}, f32[8,48,128]{2,1,0:T(8,128)S(1)}, u32[]{:S(2)}, u32[]{:S(2)}) %collective-permute-start.3) | collective-permute-done | bytes 196640 | tf_op jit(solution)/shard_map/ppermute | solution.py:26
  44.2 2.5 %collective-permute-start.4 = (f32[4,48,128]{2,1,0:T(8,128)S(1)}, f32[4,48,128]{2,1,0:T(8,128)S(1)}, u32[]{:S(2)}, u32[]{:S(2)}) collective-permute-start(f32[4,48,128]{2,1,0:T(8,128)S(1)} %dynamic-slice_bitcast_fusion.2), channel_id=1, source_target_pairs={{0,4},{1,5},{2,6},{3,7},{4,0},{5,1},{6,2},{7,3},{8,12},{9,13},{10,... | collective-permute-start | bytes 294920 | tf_op jit(solution)/shard_map/ppermute | solution.py:26
  46.7 0.0 copy-done
  46.8 6.4 %collective-permute-done.4 = f32[4,48,128]{2,1,0:T(8,128)S(1)} collective-permute-done((f32[4,48,128]{2,1,0:T(8,128)S(1)}, f32[4,48,128]{2,1,0:T(8,128)S(1)}, u32[]{:S(2)}, u32[]{:S(2)}) %collective-permute-start.4) | collective-permute-done | bytes 98336 | tf_op jit(solution)/shard_map/ppermute | solution.py:26
  53.2 2.4 %collective-permute-start.5 = (f32[2,48,128]{2,1,0:T(8,128)S(1)}, f32[2,48,128]{2,1,0:T(8,128)S(1)}, u32[]{:S(2)}, u32[]{:S(2)}) collective-permute-start(f32[2,48,128]{2,1,0:T(8,128)S(1)} %dynamic-slice_bitcast_fusion.3), channel_id=1, source_target_pairs={{0,8},{1,9},{2,10},{3,11},{4,12},{5,13},{6,14},{7,15},{8,0},{9,1},... | collective-permute-start | bytes 147464 | tf_op jit(solution)/shard_map/ppermute | solution.py:26
  55.5 0.1 compare_reduce_fusion
  55.6 0.1 reduce_or.12
  55.7 0.1 copy.19
  55.8 0.1 reduce_window_sum.13
  55.9 0.1 copy.20
  55.9 7.1 %collective-permute-done.5 = f32[2,48,128]{2,1,0:T(8,128)S(1)} collective-permute-done((f32[2,48,128]{2,1,0:T(8,128)S(1)}, f32[2,48,128]{2,1,0:T(8,128)S(1)}, u32[]{:S(2)}, u32[]{:S(2)}) %collective-permute-start.5) | collective-permute-done | bytes 49184 | tf_op jit(solution)/shard_map/ppermute | solution.py:26
  63.1 1.9 %collective-permute-start.6 = (f32[1,48,128]{2,1,0:T(8,128)S(1)}, f32[1,48,128]{2,1,0:T(8,128)S(1)}, u32[]{:S(2)}, u32[]{:S(2)}) collective-permute-start(f32[1,48,128]{2,1,0:T(8,128)S(1)} %constant_dynamic-slice_fusion), channel_id=1, source_target_pairs={{0,16},{1,17},{2,18},{3,19},{4,20},{5,21},{6,22},{7,23},{8,24},{9,... | collective-permute-start | bytes 73736 | tf_op jit(solution)/shard_map/ppermute | solution.py:26
  65.0 0.2 fusion.1
  65.2 5.4 %collective-permute-done.6 = f32[1,48,128]{2,1,0:T(8,128)S(1)} collective-permute-done((f32[1,48,128]{2,1,0:T(8,128)S(1)}, f32[1,48,128]{2,1,0:T(8,128)S(1)}, u32[]{:S(2)}, u32[]{:S(2)}) %collective-permute-start.6) | collective-permute-done | bytes 24608 | tf_op jit(solution)/shard_map/ppermute | solution.py:26
  70.6 0.6 reshape.164
  71.2 17.1 %all-to-all-done = bf16[16,32,2048]{2,1,0:T(8,128)(2,1)S(1)} async-done(((bf16[16,32,2048]{2,1,0:T(8,128)(2,1)}), bf16[16,32,2048]{2,1,0:T(8,128)(2,1)S(1)}, u32[]{:S(2)}, u32[]{:S(2)}) %all-to-all-start) | async-done | bytes 2097184 | tf_op jit(solution)/shard_map/all_to_all | solution.py:165
  88.3 0.5 convolution_convert_fusion
  88.8 1.9 %collective-permute-start.1 = (bf16[48,2048]{1,0:T(8,128)(2,1)S(1)}, bf16[48,2048]{1,0:T(8,128)(2,1)S(1)}, u32[]{:S(2)}, u32[]{:S(2)}) collective-permute-start(bf16[48,2048]{1,0:T(8,128)(2,1)S(1)} %convolution_convert_fusion), channel_id=1, source_target_pairs={{0,512},{512,0},{32,544},{544,32},{64,576},{576,64},{96,608},{608,... | collective-permute-start | bytes 589832 | tf_op jit(solution)/shard_map/ppermute | solution.py:176
  90.7 0.5 fusion.3
  91.2 9.1 %collective-permute-done.1 = bf16[48,2048]{1,0:T(8,128)(2,1)S(1)} collective-permute-done((bf16[48,2048]{1,0:T(8,128)(2,1)S(1)}, bf16[48,2048]{1,0:T(8,128)(2,1)S(1)}, u32[]{:S(2)}, u32[]{:S(2)}) %collective-permute-start.1) | collective-permute-done | bytes 196640 | tf_op jit(solution)/shard_map/ppermute | solution.py:176
  100.2 0.7 add_convert_fusion
  (16 shorter events, 0.2 us)
Async XLA Ops:
  0.6 20.0 %collective-permute-start = (s32[48,8]{0,1:T(8,128)}, s32[48,8]{0,1:T(8,128)S(1)}, u32[]{:S(2)}, u32[]{:S(2)}) collective-permute-start(s32[48,8]{0,1:T(8,128)} %param.7), channel_id=1, source_target_pairs={{0,512},{512,0},{32,544},{544,32},{64,576},{576,64},{96,608},{608,... | collective-permute-start | bytes 4616 | tf_op jit(solution)/shard_map/ppermute | solution.py:163
  20.6 67.7 %all-to-all-start = ((bf16[16,32,2048]{2,1,0:T(8,128)(2,1)}), bf16[16,32,2048]{2,1,0:T(8,128)(2,1)S(1)}, u32[]{:S(2)}, u32[]{:S(2)}) async-start(bf16[16,32,2048]{2,1,0:T(8,128)(2,1)} %bitcast.42), calls=%async_computation | async-start | bytes 4194304 | tf_op jit(solution)/shard_map/all_to_all | solution.py:165
  30.6 16.1 %copy-start = (s32[48,8]{0,1:T(8,128)S(1)}, s32[48,8]{0,1:T(8,128)}, u32[]{:S(2)}) copy-start(s32[48,8]{0,1:T(8,128)} %param.7) | copy-start | bytes 4612
  31.4 3.8 %collective-permute-start.2 = (f32[16,48,128]{2,1,0:T(8,128)}, f32[16,48,128]{2,1,0:T(8,128)S(1)}, u32[]{:S(2)}, u32[]{:S(2)}) collective-permute-start(f32[16,48,128]{2,1,0:T(8,128)} %dynamic-slice_bitcast_fusion), channel_id=1, source_target_pairs={{0,1},{1,0},{2,3},{3,2},{4,5},{5,4},{6,7},{7,6},{8,9},{9,8},{10,11... | collective-permute-start | bytes 1179656 | tf_op jit(solution)/shard_map/ppermute | solution.py:26
  35.3 8.9 %collective-permute-start.3 = (f32[8,48,128]{2,1,0:T(8,128)S(1)}, f32[8,48,128]{2,1,0:T(8,128)S(1)}, u32[]{:S(2)}, u32[]{:S(2)}) collective-permute-start(f32[8,48,128]{2,1,0:T(8,128)S(1)} %dynamic-slice_bitcast_fusion.1), channel_id=1, source_target_pairs={{0,2},{1,3},{2,0},{3,1},{4,6},{5,7},{6,4},{7,5},{8,10},{9,11},{10,... | collective-permute-start | bytes 589832 | tf_op jit(solution)/shard_map/ppermute | solution.py:26
  44.2 8.9 %collective-permute-start.4 = (f32[4,48,128]{2,1,0:T(8,128)S(1)}, f32[4,48,128]{2,1,0:T(8,128)S(1)}, u32[]{:S(2)}, u32[]{:S(2)}) collective-permute-start(f32[4,48,128]{2,1,0:T(8,128)S(1)} %dynamic-slice_bitcast_fusion.2), channel_id=1, source_target_pairs={{0,4},{1,5},{2,6},{3,7},{4,0},{5,1},{6,2},{7,3},{8,12},{9,13},{10,... | collective-permute-start | bytes 294920 | tf_op jit(solution)/shard_map/ppermute | solution.py:26
  53.2 9.9 %collective-permute-start.5 = (f32[2,48,128]{2,1,0:T(8,128)S(1)}, f32[2,48,128]{2,1,0:T(8,128)S(1)}, u32[]{:S(2)}, u32[]{:S(2)}) collective-permute-start(f32[2,48,128]{2,1,0:T(8,128)S(1)} %dynamic-slice_bitcast_fusion.3), channel_id=1, source_target_pairs={{0,8},{1,9},{2,10},{3,11},{4,12},{5,13},{6,14},{7,15},{8,0},{9,1},... | collective-permute-start | bytes 147464 | tf_op jit(solution)/shard_map/ppermute | solution.py:26
  63.1 7.5 %collective-permute-start.6 = (f32[1,48,128]{2,1,0:T(8,128)S(1)}, f32[1,48,128]{2,1,0:T(8,128)S(1)}, u32[]{:S(2)}, u32[]{:S(2)}) collective-permute-start(f32[1,48,128]{2,1,0:T(8,128)S(1)} %constant_dynamic-slice_fusion), channel_id=1, source_target_pairs={{0,16},{1,17},{2,18},{3,19},{4,20},{5,21},{6,22},{7,23},{8,24},{9,... | collective-permute-start | bytes 73736 | tf_op jit(solution)/shard_map/ppermute | solution.py:26
  88.8 11.5 %collective-permute-start.1 = (bf16[48,2048]{1,0:T(8,128)(2,1)S(1)}, bf16[48,2048]{1,0:T(8,128)(2,1)S(1)}, u32[]{:S(2)}, u32[]{:S(2)}) collective-permute-start(bf16[48,2048]{1,0:T(8,128)(2,1)S(1)} %convolution_convert_fusion), channel_id=1, source_target_pairs={{0,512},{512,0},{32,544},{544,32},{64,576},{576,64},{96,608},{608,... | collective-permute-start | bytes 589832 | tf_op jit(solution)/shard_map/ppermute | solution.py:176
